TPU v7x, 32 devices: a whole 2x2x4 slice. The times are simulated.
32 devices in a mesh: dp: 8 (over y, x, core), mp: 4 (over z).
Axes of the slice: x: 2, y: 2, z: 4, core: 2. Of those that a mesh axis runs over, the one named last changes fastest.
Arguments:
- latents: bfloat16 [24, 1024, 1152], P('dp'), may hold values from -6 to 6
- condition: float32 [24, 1152], P('dp'), may hold values from -6 to 6
- cotangent: bfloat16 [24, 1024, 1152], P('dp'), may hold values from -6 to 6
- qkv_weight: bfloat16 [1152, 3, 1152], P(None, None, 'mp'), may hold values from -1 to 1
- qv_bias: bfloat16 [2, 1152], P(None, 'mp'), may hold values from -3 to 3
- proj_weight: bfloat16 [1152, 1152], P('mp'), may hold values from -6 to 6
- proj_bias: bfloat16 [1152], replicated, may hold values from -3 to 3
- fc1_weight: bfloat16 [1152, 4608], P(None, 'mp'), may hold values from -0.1875 to 0.1875
- fc1_bias: bfloat16 [4608], P('mp'), may hold values from -3 to 3
- fc2_weight: bfloat16 [4608, 1152], P('mp'), may hold values from -0.09375 to 0.09375
- fc2_bias: bfloat16 [1152], replicated, may hold values from -3 to 3
- ada_weight: bfloat16 [1152, 6912], P(None, 'mp'), may hold values from -0.1875 to 0.1875
- ada_bias: bfloat16 [6912], P('mp'), may hold values from -3 to 3
Outputs:
- block_out: bfloat16 [24, 1024, 1152], P('dp')
- latents_grad: bfloat16 [24, 1024, 1152], P('dp')
- condition_grad: float32 [24, 1152], P('dp')
- qkv_weight_grad: float32 [1152, 3, 1152], P(None, None, 'mp')
- qv_bias_grad: float32 [2, 1152], P(None, 'mp')
- proj_weight_grad: float32 [1152, 1152], P('mp')
- proj_bias_grad: float32 [1152], replicated
- fc1_weight_grad: float32 [1152, 4608], P(None, 'mp')
- fc1_bias_grad: float32 [4608], P('mp')
- fc2_weight_grad: float32 [4608, 1152], P('mp')
- fc2_bias_grad: float32 [1152], replicated
- ada_weight_grad: float32 [1152, 6912], P(None, 'mp')
- ada_bias_grad: float32 [6912], P('mp')
All inputs are finite; a program needn't handle non-finite values.
Results may differ from a plain program's by a relative error of at most 0.025.
Values may be sent and summed in bfloat16 or wider, within the bound.
A program may use at most 448 MiB of HBM per device.

v0:
```python
from functools import partial

import jax
import jax.numpy as jnp
from jax import lax
from jax.sharding import PartitionSpec as P

HEAD_DIM = 72


norm_eps = 1e-06


def norm_stats(values):
    centered = values - jnp.mean(values, -1, keepdims=True)
    inv_std = lax.rsqrt(jnp.mean(centered * centered, -1, keepdims=True) + norm_eps)
    return (centered * inv_std, inv_std)


def norm_back(normed, inv_std, grad_normed):
    first = jnp.mean(grad_normed, -1, keepdims=True)
    second = jnp.mean(grad_normed * normed, -1, keepdims=True)
    return inv_std * (grad_normed - first - normed * second)


def attend_forward(queries, key_rows, values, block_rows, scaling):
    outputs = []
    totals = []
    for row_start in range(0, queries.shape[1], block_rows):
        query_block = queries[:, row_start : row_start + block_rows]
        scores = (
            jnp.einsum("lqhd,lkhd->lhqk", query_block, key_rows, preferred_element_type=jnp.float32)
            * scaling
        )
        row_max = jnp.max(scores, -1, keepdims=True)
        expo_vals = jnp.exp(scores - row_max)
        row_sum = jnp.sum(expo_vals, -1, keepdims=True)
        weights_low = (expo_vals / row_sum).astype(jnp.bfloat16)
        outputs.append(
            jnp.einsum("lhqk,lkhd->lqhd", weights_low, values, preferred_element_type=jnp.float32)
        )
        totals.append(row_max + jnp.log(row_sum))
    return (jnp.concatenate(outputs, 1), jnp.concatenate(totals, 2))


def attend_backward(queries, key_rows, values, log_totals, grad_heads, block_rows, scaling):
    grad_queries = []
    grad_keys = jnp.zeros(key_rows.shape, jnp.float32)
    grad_values = jnp.zeros(values.shape, jnp.float32)
    for row_start in range(0, queries.shape[1], block_rows):
        query_block = queries[:, row_start : row_start + block_rows]
        grad_block = grad_heads[:, row_start : row_start + block_rows]
        scores = (
            jnp.einsum("lqhd,lkhd->lhqk", query_block, key_rows, preferred_element_type=jnp.float32)
            * scaling
        )
        weights = jnp.exp(scores - log_totals[:, :, row_start : row_start + block_rows])
        weights_low = weights.astype(jnp.bfloat16)
        grad_weights = jnp.einsum(
            "lqhd,lkhd->lhqk", grad_block, values, preferred_element_type=jnp.float32
        )
        inner_sum = jnp.sum(weights * grad_weights, -1, keepdims=True)
        grad_scores = (weights * (grad_weights - inner_sum)).astype(jnp.bfloat16)
        grad_queries.append(
            jnp.einsum("lhqk,lkhd->lqhd", grad_scores, key_rows, preferred_element_type=jnp.float32)
            * scaling
        )
        grad_keys = (
            grad_keys
            + jnp.einsum(
                "lhqk,lqhd->lkhd", grad_scores, query_block, preferred_element_type=jnp.float32
            )
            * scaling
        )
        grad_values = grad_values + jnp.einsum(
            "lhqk,lqhd->lkhd", weights_low, grad_block, preferred_element_type=jnp.float32
        )
    return (jnp.concatenate(grad_queries, 1), grad_keys, grad_values)


def sum_mlp_grads(gradients):
    return lax.psum((gradients[0], gradients[1], gradients[2], gradients[3]), "dp")


def sum_other_grads(gradients):
    return lax.psum(
        (gradients[0], gradients[1], gradients[2], gradients[3], gradients[4], gradients[5]), "dp"
    )


def per_device(
    latents,
    condition,
    cotangent,
    qkv_weight,
    qv_bias,
    proj_weight,
    proj_bias,
    fc1_weight,
    fc1_bias,
    fc2_weight,
    fc2_bias,
    ada_weight,
    ada_bias,
):
    lat_count, seq_len, model_width = latents.shape
    local_width = qkv_weight.shape[2]
    local_heads = local_width // HEAD_DIM
    col_share = ada_weight.shape[1]
    block_rows = min(512, seq_len)
    scaling = 1.0 / HEAD_DIM**0.5
    tok_rows = lat_count * seq_len
    cond_low = jax.nn.silu(condition).astype(jnp.bfloat16)
    mod_part = jnp.dot(cond_low, ada_weight, preferred_element_type=jnp.float32) + ada_bias.astype(
        jnp.float32
    )
    modulation = lax.all_gather(mod_part, "mp", axis=1, tiled=True).reshape(
        lat_count, 6, 1, model_width
    )
    shift_one, scale_one, gate_one = (modulation[:, 0], modulation[:, 1], modulation[:, 2])
    shift_two, scale_two, gate_two = (modulation[:, 3], modulation[:, 4], modulation[:, 5])
    residual = latents.astype(jnp.float32)
    normed_one, inv_one = norm_stats(residual)
    mixed_one = (
        (normed_one * (1.0 + scale_one) + shift_one)
        .astype(jnp.bfloat16)
        .reshape(tok_rows, model_width)
    )
    qkv_flat = jnp.dot(
        mixed_one,
        qkv_weight.reshape(model_width, 3 * local_width),
        preferred_element_type=jnp.float32,
    )
    bias_rows = jnp.stack(
        [
            qv_bias[0].astype(jnp.float32),
            jnp.zeros((local_width,), jnp.float32),
            qv_bias[1].astype(jnp.float32),
        ]
    )
    qkv_low = (qkv_flat.reshape(tok_rows, 3, local_width) + bias_rows).astype(jnp.bfloat16)
    head_shape = (lat_count, seq_len, local_heads, HEAD_DIM)
    queries = qkv_low[:, 0].reshape(head_shape)
    key_rows = qkv_low[:, 1].reshape(head_shape)
    values = qkv_low[:, 2].reshape(head_shape)
    heads_out, log_totals = attend_forward(queries, key_rows, values, block_rows, scaling)
    heads_low = heads_out.astype(jnp.bfloat16).reshape(tok_rows, local_width)
    attn_part = jnp.dot(heads_low, proj_weight, preferred_element_type=jnp.float32).reshape(
        lat_count, seq_len, model_width
    )
    attn_out = lax.psum(attn_part.astype(jnp.bfloat16), "mp").astype(
        jnp.float32
    ) + proj_bias.astype(jnp.float32)
    resid_two = residual + gate_one * attn_out
    normed_two, inv_two = norm_stats(resid_two)
    mixed_local = (normed_two * (1.0 + scale_two) + shift_two).astype(jnp.bfloat16)
    mixed_two = mixed_local.reshape(tok_rows, model_width)
    hidden_pre = jnp.dot(
        mixed_two, fc1_weight, preferred_element_type=jnp.float32
    ) + fc1_bias.astype(jnp.float32)
    gelu_tanh = partial(jax.nn.gelu, approximate=True)
    activ_low = gelu_tanh(hidden_pre).astype(jnp.bfloat16)
    mlp_part = jnp.dot(activ_low, fc2_weight, preferred_element_type=jnp.float32).reshape(
        lat_count, seq_len, model_width
    )
    mlp_out = lax.psum(mlp_part.astype(jnp.bfloat16), "mp").astype(jnp.float32) + fc2_bias.astype(
        jnp.float32
    )
    out_local = (resid_two + gate_two * mlp_out).astype(jnp.bfloat16)
    grad_out = cotangent.astype(jnp.float32)
    grad_mlp = (gate_two * grad_out).reshape(tok_rows, model_width)
    grad_fc2_bias = jnp.sum(grad_mlp, 0)
    grad_mlp_low = grad_mlp.astype(jnp.bfloat16)
    grad_fc2 = jnp.einsum("tf,td->fd", activ_low, grad_mlp_low, preferred_element_type=jnp.float32)
    grad_activ = jnp.einsum(
        "td,fd->tf", grad_mlp_low, fc2_weight, preferred_element_type=jnp.float32
    )
    gelu_unused, gelu_pull = jax.vjp(gelu_tanh, hidden_pre)
    grad_hidden_low = gelu_pull(grad_activ)[0].astype(jnp.bfloat16)
    grad_fc1_bias = jnp.sum(grad_hidden_low.astype(jnp.float32), 0)
    grad_fc1 = jnp.einsum(
        "td,tf->df", mixed_two, grad_hidden_low, preferred_element_type=jnp.float32
    )
    mlp_gradients = (grad_fc1, grad_fc1_bias, grad_fc2, grad_fc2_bias)
    grad_mixed_part = jnp.einsum(
        "tf,df->td", grad_hidden_low, fc1_weight, preferred_element_type=jnp.float32
    ).reshape(lat_count, seq_len, model_width)
    grad_mixed_two = lax.psum(grad_mixed_part.astype(jnp.bfloat16), "mp").astype(jnp.float32)
    resid_grad_local = grad_out + norm_back(normed_two, inv_two, grad_mixed_two * (1.0 + scale_two))
    stats_two = jnp.stack(
        [
            jnp.sum(grad_out * mlp_out, 1),
            jnp.sum(grad_mixed_two, 1),
            jnp.sum(grad_mixed_two * normed_two, 1),
            jnp.sum(resid_grad_local * attn_out, 1),
        ],
        1,
    )
    grad_gate_two, grad_shift_two = (stats_two[:, 0], stats_two[:, 1])
    grad_scale_two, grad_gate_one = (stats_two[:, 2], stats_two[:, 3])
    grad_attn = (gate_one * resid_grad_local).reshape(tok_rows, model_width)
    grad_proj_bias = jnp.sum(grad_attn, 0)
    grad_attn_low = grad_attn.astype(jnp.bfloat16)
    grad_proj = jnp.einsum(
        "te,td->ed", heads_low, grad_attn_low, preferred_element_type=jnp.float32
    )
    grad_heads = jnp.einsum(
        "td,ed->te", grad_attn_low, proj_weight, preferred_element_type=jnp.float32
    )
    grad_heads = grad_heads.astype(jnp.bfloat16).reshape(head_shape)
    grad_queries, grad_keys, grad_values = attend_backward(
        queries, key_rows, values, log_totals, grad_heads, block_rows, scaling
    )
    grad_qkv_low = jnp.stack(
        [
            grad_queries.reshape(tok_rows, local_width),
            grad_keys.reshape(tok_rows, local_width),
            grad_values.reshape(tok_rows, local_width),
        ],
        1,
    ).astype(jnp.bfloat16)
    grad_qkv = jnp.einsum(
        "td,tce->dce", mixed_one, grad_qkv_low, preferred_element_type=jnp.float32
    )
    bias_sums = jnp.sum(grad_qkv_low.astype(jnp.float32), 0)
    grad_qv_bias = jnp.stack([bias_sums[0], bias_sums[2]])
    grad_one_part = jnp.einsum(
        "tce,dce->td", grad_qkv_low, qkv_weight, preferred_element_type=jnp.float32
    )
    grad_mixed_one = (
        lax.psum(grad_one_part.astype(jnp.bfloat16), "mp")
        .astype(jnp.float32)
        .reshape(lat_count, seq_len, model_width)
    )
    grad_shift_one = jnp.sum(grad_mixed_one, 1)
    grad_scale_one = jnp.sum(grad_mixed_one * normed_one, 1)
    latents_grad = (
        resid_grad_local + norm_back(normed_one, inv_one, grad_mixed_one * (1.0 + scale_one))
    ).astype(jnp.bfloat16)
    grad_mod = jnp.stack(
        [
            grad_shift_one,
            grad_scale_one,
            grad_gate_one,
            grad_shift_two,
            grad_scale_two,
            grad_gate_two,
        ],
        1,
    )
    grad_mod_low = grad_mod.reshape(lat_count, 6 * model_width).astype(jnp.bfloat16)
    mod_slice = lax.dynamic_slice_in_dim(
        grad_mod_low, lax.axis_index("mp") * col_share, col_share, 1
    )
    grad_ada = jnp.einsum("ld,lm->dm", cond_low, mod_slice, preferred_element_type=jnp.float32)
    grad_ada_bias = jnp.sum(mod_slice.astype(jnp.float32), 0)
    grad_cond_part = jnp.einsum(
        "lm,dm->ld", mod_slice, ada_weight, preferred_element_type=jnp.float32
    )
    grad_cond_act = lax.psum(grad_cond_part, "mp")
    silu_unused, silu_pull = jax.vjp(jax.nn.silu, condition)
    condition_grad = silu_pull(grad_cond_act)[0]
    mlp_gradients = sum_mlp_grads(mlp_gradients)
    grad_fc1, grad_fc1_bias, grad_fc2, grad_fc2_bias = mlp_gradients
    other_gradients = sum_other_grads(
        (grad_qkv, grad_qv_bias, grad_proj, grad_proj_bias, grad_ada, grad_ada_bias)
    )
    grad_qkv, grad_qv_bias, grad_proj, grad_proj_bias, grad_ada, grad_ada_bias = other_gradients
    return (
        out_local,
        latents_grad,
        condition_grad,
        grad_qkv,
        grad_qv_bias,
        grad_proj,
        grad_proj_bias,
        grad_fc1,
        grad_fc1_bias,
        grad_fc2,
        grad_fc2_bias,
        grad_ada,
        grad_ada_bias,
    )


def solution(mesh):
    in_specs = (
        P("dp", None, None),
        P("dp", None),
        P("dp", None, None),
        P(None, None, "mp"),
        P(None, "mp"),
        P("mp", None),
        P(),
        P(None, "mp"),
        P("mp"),
        P("mp", None),
        P(),
        P(None, "mp"),
        P("mp"),
    )
    out_specs = (
        P("dp", None, None),
        P("dp", None, None),
        P("dp", None),
        P(None, None, "mp"),
        P(None, "mp"),
        P("mp", None),
        P(),
        P(None, "mp"),
        P("mp"),
        P("mp", None),
        P(),
        P(None, "mp"),
        P("mp"),
    )
    return jax.shard_map(
        per_device, mesh=mesh, in_specs=in_specs, out_specs=out_specs, check_vma=False
    )
```

profile of v0, /device:TPU:0, one launch (start us, length us, event | category | flops | bytes accessed | tf_op | source)
XLA Modules:
  0.0 1786.9 jit_solution(3253555170883167061)
XLA Ops:
  19.5 15.3 all-gather
  75.1 13.3 multiply_reduce_fusion.3
  88.4 10.3 multiply_reduce_fusion.2
  98.7 11.1 fusion
  109.8 11.3 fusion.56
  121.1 11.0 fusion.1
  132.1 12.0 fusion.55
  163.0 13.2 fusion.101
  176.2 227.6 %all-reduce.8.cloned.1.call-done = bf16[3,1024,1152]{2,1,0:T(8,128)(2,1)} async-done(((bf16[3,1024,1152]{2,1,0:T(8,128)(2,1)}), bf16[3,1024,1152]{2,1,0:T(8,128)(2,1)}) %all-reduce.8.cloned.1.call-update) | async-done | bytes 7077904 | tf_op jit(solution)/shard_map/psum | solution.py:151
  425.7 23.6 %convert_reduce_fusion.1 = (f32[1152]{0:T(1024)}, bf16[3072,1152]{1,0:T(8,128)(2,1)S(1)}, f32[3072,1152]{1,0:T(8,128)}) fusion(f32[3072,1152]{1,0:T(8,128)} %fusion.101, f32[1152]{0:T(1024)S(1)} %convert_element_type.160, bf16[3072,1152]{1,0:T(8,128)(2,1)S(1)} %bitcast.129, bf16[1152,1152]{1,0:T(8,128)(2,1)S(1)} %copy-done), kind=kOutput, calls=%fused_computation.61 | convolution fusion | flops 8235121664 | bytes 45130752 | tf_op jit(solution)/shard_map/dot_general | solution.py:158
  449.4 12.2 convolution_convert_fusion
  461.8 18.1 %convolution_convert_fusion.1 = bf16[3072,1152]{1,0:T(8,128)(2,1)} fusion(bf16[1152,1152]{1,0:T(8,128)(2,1)} %param.22, f32[3072,1152]{1,0:T(8,128)} %get-tuple-element.62), kind=kOutput, calls=%fused_computation.82 | convolution fusion | flops 8189116416 | bytes 23887872 | tf_op jit(solution)/shard_map/dot_general | solution.py:163
  479.9 229.1 %all-reduce.10.cloned.1.call-done = bf16[3,1024,1152]{2,1,0:T(8,128)(2,1)} async-done(((bf16[3,1024,1152]{2,1,0:T(8,128)(2,1)}), bf16[3,1024,1152]{2,1,0:T(8,128)(2,1)}) %all-reduce.10.cloned.1.call-update) | async-done | bytes 7077904 | tf_op jit(solution)/shard_map/psum | solution.py:188
  709.0 12.4 fusion.27
  721.5 17.7 multiply_reduce_fusion.6
  739.2 9.2 multiply_convert_fusion.3
  765.0 16.7 multiply_reduce_fusion.1
  781.7 22.1 %multiply_convert_fusion.1 = bf16[3,4,512,1024]{3,2,1,0:T(8,128)(2,1)} fusion(f32[3,4,512,1024]{3,2,1,0:T(8,128)} %get-tuple-element.66, f32[3,4,512,1024]{3,2,1,0:T(8,128)} %get-tuple-element.61, f32[3,4,512]{2,1,0:T(4,128)S(1)} %get-tuple-element.65, f32[3,4,512]{2,1,0:T(4,128)S(1)} %log_add_fusion.1), kind=kLoop, calls=%fused_computation.3 | loop fusion | flops 31457280 | bytes 62963712 | tf_op jit(solution)/shard_map/convert_element_type | solution.py:63
  821.2 12.4 fusion.37
  833.6 18.5 %multiply_reduce_fusion = (f32[3,4,512]{2,1,0:T(4,128)S(1)}, f32[3,4,512,1024]{3,2,1,0:T(8,128)}) fusion(f32[3,4,512,1024]{3,2,1,0:T(8,128)} %get-tuple-element.59, f32[3,4,512]{2,1,0:T(4,128)S(1)} %log_add_fusion, bf16[3,1024,4,72]{1,0,3,2:T(4,128)(2,1)} %reshape_squeeze.9, bf16[3,512,4,72]{1,0,3,2:T(4,128)(2,1)} %get-tuple-element.45), kind=kOutput, calls=%fused_computation.1 | convolution fusion | flops 931129344 | bytes 53035008 | tf_op jit(solution)/shard_map/lqhd,lkhd->lhqk/dot_general | solution.py:59
  852.1 12.5 fusion.51
  873.3 21.5 %multiply_convert_fusion = bf16[3,4,512,1024]{3,2,1,0:T(8,128)(2,1)} fusion(f32[3,4,512,1024]{3,2,1,0:T(8,128)} %get-tuple-element.64, f32[3,4,512,1024]{3,2,1,0:T(8,128)} %get-tuple-element.59, f32[3,4,512]{2,1,0:T(4,128)S(1)} %get-tuple-element.63, f32[3,4,512]{2,1,0:T(4,128)S(1)} %log_add_fusion), kind=kLoop, calls=%fused_computation | loop fusion | flops 31457280 | bytes 62963712 | tf_op jit(solution)/shard_map/convert_element_type | solution.py:63
  929.0 13.6 bitcast_convert_fusion
  947.8 15.2 fusion.104
  963.0 16.2 fusion.94
  990.3 8.9 fusion.102
  999.2 420.1 %all-reduce.14.cloned.1.call-done = (bf16[3,1024,1152]{2,1,0:T(8,128)(2,1)}, bf16[3072,1152]{1,0:T(8,128)(2,1)}) async-done(((bf16[3,1024,1152]{2,1,0:T(8,128)(2,1)}, bf16[3072,1152]{1,0:T(8,128)(2,1)}), (bf16[3,1024,1152]{2,1,0:T(8,128)(2,1)}, bf16[3072,1152]{1,0:T(8,128)(2,1)})) %all-reduce.14.cloned.1.call-update) | async-done | bytes 14155792 | tf_op jit(solution)/shard_map/psum | solution.py:166
  1423.8 13.2 fusion.22
  1437.3 23.9 %fusion.11 = (f32[1152]{0:T(1024)S(1)}, bf16[3,1152]{1,0:T(4,128)(2,1)S(1)}, bf16[3,1024,1152]{2,1,0:T(8,128)(2,1)}, bf16[3,1024,1152]{2,1,0:T(8,128)(2,1)}) fusion(bf16[3,1024,1152]{2,1,0:T(8,128)(2,1)} %param.15, f32[3,1152]{1,0:T(4,128)S(1)} %copy-done.35, f32[1152]{0:T(1024)S(1)} %convert_element_type.165, bf16[3,1024,1152]{2,1,0:T(8,128)(2,1)S(1)} %copy-done.15, ...), kind=kLoop, calls=%fused_computation.33 | loop fusion | flops 84930048 | bytes 70890240 | tf_op jit(solution)/shard_map/reduce_sum | solution.py:172
  1469.4 27.4 %all-reduce = (f32[2,288]{1,0:T(2,128)}, f32[1152]{0:T(1024)}, f32[1152]{0:T(1024)}, f32[1152]{0:T(1024)}, f32[1728]{0:T(1024)}) all-reduce(f32[2,288]{1,0:T(2,128)S(1)} %pad_maximum_fusion.2, f32[1152]{0:T(1024)S(1)} %copy-done.38, f32[1152]{0:T(1024)S(1)} %copy-done.39, ...), channel_id=1, replica_groups=mesh['dp'=8,'mp'=4] {'dp'}, use_global_device_ids=true, to_apply=%region_27.28 | all-reduce | flops 5760 | bytes 46080 | tf_op jit(solution)/shard_map/psum | solution.py:86
  1500.0 16.6 psum.109
  1517.2 246.5 %all-reduce.12.cloned.1.call-done = (f32[1152,3,288]{0,2,1:T(8,128)}, f32[288,1152]{1,0:T(8,128)}, f32[1152,1152]{1,0:T(8,128)}, f32[1152,1152]{1,0:T(8,128)}, f32[1152,1728]{0,1:T(8,128)}) async-done(((f32[1152,3,288]{0,2,1:T(8,128)}, f32[288,1152]{1,0:T(8,128)}, f32[1152,1152]{1,0:T(8,128)}, f32[1152,1152]{1,0:T(8,128)}, f32[1152,1728]{0,1:T(8,128)}), (f32[1152,3,288]{0,2,1:T(8,128)}, ...) | async-done | bytes 23887888 | tf_op jit(solution)/shard_map/psum | solution.py:86
  (213 shorter events, 219.1 us)
Async XLA Ops:
  7.2 418.6 %copy-start = (bf16[1152,1152]{1,0:T(8,128)(2,1)S(1)}, bf16[1152,1152]{1,0:T(8,128)(2,1)}, u32[]{:S(2)}) copy-start(bf16[1152,1152]{1,0:T(8,128)(2,1)} %param.20) | copy-start | bytes 7962628
  7.2 11.2 copy-start.32
  7.2 396.6 %all-reduce.8.cloned.1.call-start = ((), (), s32[]{:S(2)}) async-start(), calls=%async_computation | async-start | bytes 14155776 | tf_op jit(solution)/shard_map/psum | solution.py:151
  7.3 11.1 copy-start.5
  13.3 29.1 %copy-start.26 = (f32[3,1024]{1,0:T(4,128)}, f32[3,1024]{1,0:T(4,128)S(1)}, u32[]{:S(2)}) copy-start(f32[3,1024]{1,0:T(4,128)S(1)} %broadcast_multiply_fusion.4) | copy-start | bytes 36868
  18.4 34.1 %copy-start.30 = (f32[3,1024]{1,0:T(4,128)}, f32[3,1024]{1,0:T(4,128)S(1)}, u32[]{:S(2)}) copy-start(f32[3,1024]{1,0:T(4,128)S(1)} %add_rsqrt_fusion.1) | copy-start | bytes 36868
  75.1 13.3 copy-start.13
  75.1 13.3 copy-start.11
  75.1 13.3 copy-start.3
  154.2 554.9 %all-reduce.10.cloned.1.call-start = ((), (), s32[]{:S(2)}) async-start(), calls=%async_computation.1 | async-start | bytes 14155776 | tf_op jit(solution)/shard_map/psum | solution.py:188
  154.2 567.2 %copy-start.28 = (f32[1152]{0:T(1024)}, f32[1152]{0:T(1024)S(1)}, u32[]{:S(2)}) copy-start(f32[1152]{0:T(1024)S(1)} %convert_element_type.158) | copy-start | bytes 13828
  154.3 584.9 %copy-start.22 = (f32[3,1152]{1,0:T(4,128)}, f32[3,1152]{1,0:T(4,128)S(1)}, u32[]{:S(2)}) copy-start(f32[3,1152]{1,0:T(4,128)S(1)} %get-tuple-element.70) | copy-start | bytes 41476
  425.7 23.7 %copy-start.17 = (bf16[3,1024,1152]{2,1,0:T(8,128)(2,1)}, bf16[3,1024,1152]{2,1,0:T(8,128)(2,1)S(1)}, u32[]{:S(2)}) copy-start(bf16[3,1024,1152]{2,1,0:T(8,128)(2,1)S(1)} %add_convert_fusion.1) | copy-start | bytes 21233668
  449.4 12.2 copy-start.46
  461.7 957.6 %all-reduce.14.cloned.1.call-start = ((), (), s32[]{:S(2)}) async-start(), calls=%async_computation.3 | async-start | bytes 28311552 | tf_op jit(solution)/shard_map/psum | solution.py:166
  709.0 12.4 copy-start.2
  748.4 16.6 copy-start.7
  781.7 22.1 %copy-start.4 = (bf16[3,1024,4,72]{1,0,3,2:T(4,128)(2,1)S(1)}, bf16[3,1024,4,72]{1,0,3,2:T(4,128)(2,1)}, u32[]{:S(2)}) copy-start(bf16[3,1024,4,72]{1,0,3,2:T(4,128)(2,1)} %reshape_squeeze.11) | copy-start | bytes 5308420
  803.8 17.5 copy-start.10
  929.0 13.6 copy-start.9
  942.6 821.0 %all-reduce.12.cloned.1.call-start = ((), (), s32[]{:S(2)}) async-start(), calls=%async_computation.2 | async-start | bytes 47775744 | tf_op jit(solution)/shard_map/psum | solution.py:86
  963.0 20.5 %copy-start.21 = (bf16[36,8,3,1024]{3,1,2,0:T(8,128)(2,1)S(1)}, bf16[36,8,3,1024]{3,1,2,0:T(8,128)(2,1)}, u32[]{:S(2)}) copy-start(bf16[36,8,3,1024]{3,1,2,0:T(8,128)(2,1)} %copy.116) | copy-start | bytes 5308420
  990.2 429.0 %copy-start.25 = (f32[3,1152]{1,0:T(4,128)S(1)}, f32[3,1152]{1,0:T(4,128)}, u32[]{:S(2)}) copy-start(f32[3,1152]{1,0:T(4,128)} %copy-done.24) | copy-start | bytes 41476
  990.2 433.5 %copy-start.27 = (f32[3,1024]{1,0:T(4,128)S(1)}, f32[3,1024]{1,0:T(4,128)}, u32[]{:S(2)}) copy-start(f32[3,1024]{1,0:T(4,128)} %copy-done.26) | copy-start | bytes 36868
  990.3 433.5 %copy-start.31 = (f32[3,1024]{1,0:T(4,128)S(1)}, f32[3,1024]{1,0:T(4,128)}, u32[]{:S(2)}) copy-start(f32[3,1024]{1,0:T(4,128)} %copy-done.30) | copy-start | bytes 36868
  1423.8 13.4 copy-start.37
  1423.8 13.4 copy-start.36
  1423.8 13.4 copy-start.15
  1423.8 13.4 copy-start.23
  1423.8 13.4 copy-start.29
  1423.8 13.4 copy-start.35
  1437.3 24.0 %copy-start.33 = (f32[3,1152]{1,0:T(4,128)S(1)}, f32[3,1152]{1,0:T(4,128)}, u32[]{:S(2)}) copy-start(f32[3,1152]{1,0:T(4,128)} %param.14) | copy-start | bytes 41476
  (31 other events, 211.8 us)
Sparse Core Ops, SparseCore 0:
  154.3 249.4 all-reduce.7
  461.8 247.1 all-reduce.9
  942.8 476.4 all-reduce.13
  1466.1 297.5 all-reduce.11
where the time goes:
time: 1790 us
  waiting for transfers between devices  1120 us (63%)
  matrix products  300 us (17%)
  other arithmetic  201 us (11%)
  local copies, waits for them, and re-layouts  88.3 us (5%)
  blocking collectives  59.3 us (3%)
    psum x1, waiting for transfers between devices, per_device(): lax.psum(mlp_part.astype(jnp.bfloat16), 'mp').astype(jnp.float32)  420 us
    psum x1, waiting for transfers between devices, sum_other_grads(): lax.psum((gradients[0], gradients[1], gradients[2], gradients[3], gradien...  246 us
    psum x1, waiting for transfers between devices, per_device(): lax.psum(grad_mixed_part.astype(jnp.bfloat16), 'mp').astype(jnp.float32)  229 us
    psum x1, waiting for transfers between devices, per_device(): lax.psum(attn_part.astype(jnp.bfloat16), 'mp').astype(jnp.float32)  228 us
    convert_element_type x2, other arithmetic, attend_backward(): grad_scores = (weights * (grad_weights - inner_sum)).astype(jnp.bfloat16)  43.6 us
  transfers between devices with their start and end apart: 4, of which 4 were waited for; matrix products, arithmetic and copies ran while one was open for 6% of the time, Pallas kernels for 0%

commit v1 on v0

v1 whole, which is shorter than its diff:
```python
import functools

import jax
import jax.numpy as jnp
from jax import lax
from jax.experimental import pallas as pl
from jax.experimental.pallas import tpu as pltpu
from jax.sharding import PartitionSpec as P

HEAD_DIM = 72
EPS = 1e-06
LOG2E = 1.4426950408889634
GELU_A = 0.7978845608028654
GELU_B = 0.044715
BF = jnp.bfloat16
F32 = jnp.float32
MIB = 2**20


def mm(a, b):
    return jnp.dot(a, b, preferred_element_type=F32)


def nt(a, b):
    return lax.dot_general(a, b, (((1,), (1,)), ((), ())), preferred_element_type=F32)


def tn(a, b):
    return lax.dot_general(a, b, (((0,), (0,)), ((), ())), preferred_element_type=F32)


def norm_stats(values):
    centered = values - jnp.mean(values, -1, keepdims=True)
    inv_std = lax.rsqrt(jnp.mean(centered * centered, -1, keepdims=True) + EPS)
    return centered * inv_std, inv_std


def norm_back(normed, inv_std, grad_normed):
    first = jnp.mean(grad_normed, -1, keepdims=True)
    second = jnp.mean(grad_normed * normed, -1, keepdims=True)
    return inv_std * (grad_normed - first - normed * second)


def attn_fwd_kernel(
    me_ref, lat_ref, mod_ref, w_ref, bias_ref, heads_ref, qkv_ref, lse_ref, h1_ref, h1_all
):
    slot, lat = pl.program_id(0), pl.program_id(1)
    n_heads = qkv_ref.shape[1] // 3
    seq = lat_ref.shape[1]

    @pl.when(slot == 0)
    def _():
        normed, _ = norm_stats(lat_ref[0].astype(F32))
        h1 = (normed * (1.0 + mod_ref[0, 1:2]) + mod_ref[0, 0:1]).astype(BF)
        h1_all[lat] = h1
        h1_ref[0] = h1

    flat = nt(w_ref[0], h1_all[lat]) + bias_ref[0]
    parts = flat.reshape(3 * n_heads, HEAD_DIM, seq)
    scaling = LOG2E / HEAD_DIM**0.5
    outs = []
    lses = []
    for h in range(n_heads):
        q_t = (parts[h] * scaling).astype(BF)
        k_t = parts[n_heads + h]
        v_t = parts[2 * n_heads + h]
        v_ext = jnp.concatenate([v_t, jnp.ones((8, seq), F32)], 0).astype(BF)
        scores = mm(k_t.T.astype(BF), q_t)
        top = jnp.max(scores, 0, keepdims=True)
        probs = jnp.exp2(scores - top).astype(BF)
        out = mm(v_ext, probs)
        total = out[HEAD_DIM : HEAD_DIM + 1]
        outs.append(out[:HEAD_DIM] * (1.0 / total))
        lses.append(top + jnp.log2(total))

        @pl.when(slot == 0)
        def _():
            qkv_ref[0, h] = q_t
            qkv_ref[0, n_heads + h] = k_t.astype(BF)
            qkv_ref[0, 2 * n_heads + h] = v_t.astype(BF)
            lse_ref[0, h : h + 1] = lses[h]

    heads_ref[0, 0] = jnp.concatenate(outs, 0).astype(BF)


def attn_fwd(me, latents, mod, gathered, bias, n_mp):
    lat, seq, dim = latents.shape
    local = dim // n_mp
    n_heads = local // HEAD_DIM
    last = lat - 1
    first = lambda s, l: jnp.where(s == 0, l, last)
    return pl.pallas_call(
        attn_fwd_kernel,
        grid_spec=pltpu.PrefetchScalarGridSpec(
            num_scalar_prefetch=1,
            grid=(n_mp, lat),
            in_specs=[
                pl.BlockSpec((1, seq, dim), lambda s, l, me: (first(s, l), 0, 0)),
                pl.BlockSpec((1, 6, dim), lambda s, l, me: (l, 0, 0)),
                pl.BlockSpec(
                    (1, 3 * local, dim), lambda s, l, me: (lax.rem(me[0] + s, n_mp), 0, 0)
                ),
                pl.BlockSpec((1, 3 * local, 1), lambda s, l, me: (lax.rem(me[0] + s, n_mp), 0, 0)),
            ],
            out_specs=[
                pl.BlockSpec(
                    (1, 1, local, seq), lambda s, l, me: (lax.rem(me[0] + s, n_mp), l, 0, 0)
                ),
                pl.BlockSpec(
                    (1, 3 * n_heads, HEAD_DIM, seq), lambda s, l, me: (first(s, l), 0, 0, 0)
                ),
                pl.BlockSpec((1, n_heads, seq), lambda s, l, me: (first(s, l), 0, 0)),
                pl.BlockSpec((1, seq, dim), lambda s, l, me: (first(s, l), 0, 0)),
            ],
            scratch_shapes=[pltpu.VMEM((lat, seq, dim), BF)],
        ),
        out_shape=[
            jax.ShapeDtypeStruct((n_mp, lat, local, seq), BF),
            jax.ShapeDtypeStruct((lat, 3 * n_heads, HEAD_DIM, seq), BF),
            jax.ShapeDtypeStruct((lat, n_heads, seq), F32),
            jax.ShapeDtypeStruct((lat, seq, dim), BF),
        ],
        compiler_params=pltpu.CompilerParams(vmem_limit_bytes=60 * MIB),
        name="attn_fwd",
    )(me, latents, mod, gathered, bias)


def mlp_kernel(
    me_ref,
    heads_ref,
    lat_ref,
    cot_ref,
    mod_ref,
    wp_ref,
    w1_ref,
    w2_ref,
    bp_ref,
    b1_ref,
    b2_ref,
    out_ref,
    dx1_ref,
    da_ref,
    h2_ref,
    dm_ref,
    z_ref,
    du_ref,
    stats_ref,
    macc,
    dacc,
):
    n_mp, hid, dim = w1_ref.shape
    rows = lat_ref.shape[1]
    gate_one, shift_two = mod_ref[0, 2:3], mod_ref[0, 3:4]
    scale_two, gate_two = mod_ref[0, 4:5], mod_ref[0, 5:6]
    heads = heads_ref[:, 0].reshape(dim, rows)
    attn = tn(heads, wp_ref[...].reshape(dim, dim)) + bp_ref[...]
    x1 = lat_ref[0].astype(F32) + gate_one * attn
    n2, inv2 = norm_stats(x1)
    h2 = (n2 * (1.0 + scale_two) + shift_two).astype(BF)
    h2_ref[0] = h2
    cot = cot_ref[0].astype(F32)
    dm = (gate_two * cot).astype(BF)
    dm_ref[0] = dm

    macc[...] = jnp.zeros_like(macc)
    dacc[...] = jnp.zeros_like(dacc)

    def part(slot, own):
        w1 = w1_ref[slot]
        w2 = w2_ref[slot]
        u = nt(h2_ref[0], w1) + b1_ref[slot]
        dz = nt(dm_ref[0], w2)
        u2 = u * u
        t = jnp.tanh(u * (GELU_A + (GELU_A * GELU_B) * u2))
        half = 0.5 + 0.5 * t
        z = (u * half).astype(BF)
        slope = half + u * (1.0 - t * t) * (0.5 * GELU_A + (1.5 * GELU_A * GELU_B) * u2)
        du = (dz * slope).astype(BF)
        if own:
            z_ref[0] = z
            du_ref[0] = du
        macc[...] += mm(z, w2)
        dacc[...] += mm(du, w1)

    part(me_ref[0], True)

    def body(s, carry):
        part(lax.rem(me_ref[0] + s, n_mp), False)
        return carry

    lax.fori_loop(1, n_mp, body, 0)
    mlp = macc[...] + b2_ref[...]
    out_ref[0] = (x1 + gate_two * mlp).astype(BF)
    dh2 = dacc[...]
    dx1 = cot + norm_back(n2, inv2, dh2 * (1.0 + scale_two))
    dx1_ref[0] = dx1.astype(BF)
    da_ref[0] = (gate_one * dx1).astype(BF)
    total = lambda v: jnp.sum(v, 0, keepdims=True)
    stats = jnp.concatenate(
        [
            total(dx1 * attn),
            total(dh2),
            total(dh2 * n2),
            total(cot * mlp),
            total(cot),
            total(dx1),
            jnp.zeros((2, dim), F32),
        ],
        0,
    )

    @pl.when(pl.program_id(1) == 0)
    def _():
        stats_ref[0] = stats

    @pl.when(pl.program_id(1) > 0)
    def _():
        stats_ref[0] += stats


def mlp_both(me, heads, latents, cotangent, mod, gathered, bp, b1, b2, n_mp, rows):
    lat, seq, dim = latents.shape
    local = dim // n_mp
    hid = b1.shape[2]
    tok = pl.BlockSpec((1, rows, dim), lambda l, t, me: (l, t, 0))
    hidden = pl.BlockSpec((1, rows, hid), lambda l, t, me: (l, t, 0))
    once = lambda shape, at: pl.BlockSpec(
        shape, lambda l, t, me: at, pipeline_mode=pl.Buffered(1)
    )
    return pl.pallas_call(
        mlp_kernel,
        grid_spec=pltpu.PrefetchScalarGridSpec(
            num_scalar_prefetch=1,
            grid=(lat, seq // rows),
            in_specs=[
                pl.BlockSpec((n_mp, 1, local, rows), lambda l, t, me: (0, l, 0, t)),
                tok,
                tok,
                pl.BlockSpec((1, 6, dim), lambda l, t, me: (l, 0, 0)),
                once((n_mp, local, dim), (0, 3, 0)),
                once((n_mp, hid, dim), (0, 1, 0)),
                once((n_mp, hid, dim), (0, 2, 0)),
                once((1, dim), (0, 0)),
                once((n_mp, 1, hid), (0, 0, 0)),
                once((1, dim), (0, 0)),
            ],
            out_specs=[
                tok,
                tok,
                tok,
                tok,
                tok,
                hidden,
                hidden,
                pl.BlockSpec((1, 8, dim), lambda l, t, me: (l, 0, 0)),
            ],
            scratch_shapes=[pltpu.VMEM((rows, dim), F32)] * 2,
        ),
        out_shape=[jax.ShapeDtypeStruct((lat, seq, dim), BF)] * 5
        + [jax.ShapeDtypeStruct((lat, seq, hid), BF)] * 2
        + [jax.ShapeDtypeStruct((lat, 8, dim), F32)],
        compiler_params=pltpu.CompilerParams(vmem_limit_bytes=60 * MIB),
        name="mlp_both",
    )(me, heads, latents, cotangent, mod, gathered, gathered, gathered, bp, b1, b2)


def attn_bwd_kernel(da_ref, heads_ref, qkv_ref, lse_ref, wp_ref, wq_ref, dqkv_ref, dh1_ref, *, rows):
    n_heads = lse_ref.shape[1]
    seq = da_ref.shape[1]
    dheads = nt(wp_ref[...], da_ref[0]).reshape(n_heads, HEAD_DIM, seq)
    heads = heads_ref[0].astype(F32).reshape(n_heads, HEAD_DIM, seq)
    scaling = 1.0 / HEAD_DIM**0.5
    dq_list, dk_list, dv_list = [], [], []
    for h in range(n_heads):
        q_t = qkv_ref[0, h]
        k_t = qkv_ref[0, n_heads + h]
        v_t = qkv_ref[0, 2 * n_heads + h]
        q = q_t.astype(F32).T.astype(BF)
        k = k_t.astype(F32).T.astype(BF)
        v = v_t.astype(F32).T.astype(BF)
        do_t = dheads[h].astype(BF)
        do = dheads[h].T.astype(BF)
        inner = jnp.sum(do_t.astype(F32) * heads[h], 0, keepdims=True)
        dq_parts = []
        for i in range(seq // rows):
            cols = slice(i * rows, (i + 1) * rows)
            probs = jnp.exp2(mm(k, q_t[:, cols]) - lse_ref[0, h : h + 1, cols])
            dprobs = mm(v, do_t[:, cols])
            dscores = (probs * (dprobs - inner[:, cols])).astype(BF)
            dq_parts.append(mm(k_t, dscores))
            dv_new = mm(probs.astype(BF), do[cols])
            dk_new = mm(dscores, q[cols])
            dv = dv_new if i == 0 else dv + dv_new
            dk = dk_new if i == 0 else dk + dk_new
        dq_list.append(jnp.concatenate(dq_parts, 1) * scaling)
        dk_list.append(dk.T * (1.0 / LOG2E))
        dv_list.append(dv.T)
    dqkv = jnp.concatenate(dq_list + dk_list + dv_list, 0).astype(BF)
    dqkv_ref[0] = dqkv
    dh1_ref[0] = tn(dqkv, wq_ref[...]).astype(BF)


def attn_bwd(da, heads_own, qkv, lse, wp, wq, index, rows):
    lat, seq, dim = da.shape
    n_heads = lse.shape[1]
    local = n_heads * HEAD_DIM
    one = lambda shape: pl.BlockSpec((1,) + shape, lambda i: (index,) + (0,) * len(shape))
    whole = lambda shape: pl.BlockSpec(shape, lambda i: (0,) * len(shape))
    out = lambda shape: pl.BlockSpec((1,) + shape, lambda i: (0,) * (len(shape) + 1))
    return pl.pallas_call(
        functools.partial(attn_bwd_kernel, rows=rows),
        grid=(1,),
        in_specs=[
            one((seq, dim)),
            one((local, seq)),
            one((3 * n_heads, HEAD_DIM, seq)),
            one((n_heads, seq)),
            whole((local, dim)),
            whole((3 * local, dim)),
        ],
        out_specs=[out((3 * local, seq)), out((seq, dim))],
        out_shape=[
            jax.ShapeDtypeStruct((1, 3 * local, seq), BF),
            jax.ShapeDtypeStruct((1, seq, dim), BF),
        ],
        compiler_params=pltpu.CompilerParams(vmem_limit_bytes=60 * MIB),
        name="attn_bwd",
    )(da, heads_own, qkv, lse, wp, wq)


def latents_kernel(dh1_ref, dx1_ref, lat_ref, mod_ref, grad_ref, stats_ref):
    n1, inv1 = norm_stats(lat_ref[0].astype(F32))
    dh1 = dh1_ref[0].astype(F32)
    grad = dx1_ref[0].astype(F32) + norm_back(n1, inv1, dh1 * (1.0 + mod_ref[0, 1:2]))
    grad_ref[0] = grad.astype(BF)
    stats = jnp.concatenate(
        [
            jnp.sum(dh1, 0, keepdims=True),
            jnp.sum(dh1 * n1, 0, keepdims=True),
            jnp.zeros((6, dh1.shape[1]), F32),
        ],
        0,
    )

    @pl.when(pl.program_id(1) == 0)
    def _():
        stats_ref[0] = stats

    @pl.when(pl.program_id(1) > 0)
    def _():
        stats_ref[0] += stats


def latents_back(dh1, dx1, latents, mod, rows):
    lat, seq, dim = latents.shape
    tok = pl.BlockSpec((1, rows, dim), lambda l, t: (l, t, 0))
    return pl.pallas_call(
        latents_kernel,
        grid=(lat, seq // rows),
        in_specs=[tok, tok, tok, pl.BlockSpec((1, 6, dim), lambda l, t: (l, 0, 0))],
        out_specs=[tok, pl.BlockSpec((1, 8, dim), lambda l, t: (l, 0, 0))],
        out_shape=[
            jax.ShapeDtypeStruct((lat, seq, dim), BF),
            jax.ShapeDtypeStruct((lat, 8, dim), F32),
        ],
        compiler_params=pltpu.CompilerParams(vmem_limit_bytes=40 * MIB),
        name="latents_back",
    )(dh1, dx1, latents, mod)


def per_device(
    n_dp,
    n_mp,
    latents,
    condition,
    cotangent,
    qkv_weight,
    qv_bias,
    proj_weight,
    proj_bias,
    fc1_weight,
    fc1_bias,
    fc2_weight,
    fc2_bias,
    ada_weight,
    ada_bias,
):
    lat, seq, dim = latents.shape
    local = qkv_weight.shape[2]
    n_heads = local // HEAD_DIM
    hid = fc1_weight.shape[1]
    cols = ada_weight.shape[1]
    mp_at = lax.axis_index("mp")
    dp_at = lax.axis_index("dp")
    me = jnp.full((1,), mp_at, jnp.int32)

    cond_low = jax.nn.silu(condition).astype(BF)
    mod_part = mm(cond_low, ada_weight) + ada_bias.astype(F32)
    bias_row = jnp.concatenate([qv_bias.reshape(-1), fc1_bias]).astype(F32)[None]
    small = lax.all_gather(jnp.concatenate([mod_part, bias_row], 0), "mp", axis=0)
    mod = small[:, :lat].transpose(1, 0, 2).reshape(lat, 6, dim)
    qv_all = small[:, lat, : 2 * local].reshape(n_mp, 2, local)
    b_qkv = jnp.stack([qv_all[:, 0], jnp.zeros((n_mp, local), F32), qv_all[:, 1]], 1).reshape(
        n_mp, 3 * local, 1
    )
    b_fc1 = small[:, lat, 2 * local :].reshape(n_mp, 1, hid)

    wq_own = (
        qkv_weight.reshape(dim, 3, n_heads, HEAD_DIM).transpose(1, 2, 3, 0).reshape(3 * local, dim)
    )
    own = jnp.concatenate([wq_own, proj_weight, fc1_weight.T, fc2_weight], 0)
    share = own.shape[0] // n_dp
    mine = lax.dynamic_slice_in_dim(own, dp_at * share, share, 0)
    gathered = lax.all_gather(mine, ("dp", "mp"), axis=0).reshape(n_dp, n_mp, share, dim)
    gathered = gathered.transpose(1, 0, 2, 3).reshape(n_mp, n_dp * share, dim)

    heads, qkv, lse, h1 = attn_fwd(me, latents, mod, gathered, b_qkv, n_mp)
    block_out, dx1, da, h2, dm, z, du, stats_two = mlp_both(
        me,
        heads,
        latents,
        cotangent,
        mod,
        gathered,
        proj_bias.astype(F32)[None],
        b_fc1,
        fc2_bias.astype(F32)[None],
        n_mp,
        256,
    )
    flat = lambda v: v.reshape(lat * seq, v.shape[-1])
    grad_fc2 = tn(flat(z), flat(dm)).astype(BF)
    grad_fc1 = tn(flat(h2), flat(du)).astype(BF)
    grad_fc1_bias = jnp.sum(flat(du).astype(F32), 0)
    gate_one, gate_two = mod[:, 2], mod[:, 5]
    grad_fc2_bias = jnp.sum(gate_two * stats_two[:, 4], 0)
    grad_proj_bias = jnp.sum(gate_one * stats_two[:, 5], 0)
    grad_fc1, grad_fc2 = lax.psum((grad_fc1, grad_fc2), "dp")

    heads_own = lax.dynamic_index_in_dim(heads, mp_at, 0, keepdims=False)
    dqkv, dh1 = [], []
    for i in range(lat):
        dqkv_i, dh1_i = attn_bwd(da, heads_own, qkv, lse, proj_weight, wq_own, i, min(512, seq))
        dqkv.append(dqkv_i)
        dh1.append(lax.psum(dh1_i, "mp"))
    dqkv = jnp.concatenate(dqkv, 0)
    dh1 = jnp.concatenate(dh1, 0)
    grad_qkv = jnp.einsum("les,lsd->ed", dqkv, h1, preferred_element_type=F32).astype(BF)
    grad_proj = jnp.einsum("les,lsd->ed", heads_own, da, preferred_element_type=F32).astype(BF)
    bias_sums = jnp.sum(dqkv.astype(F32), (0, 2)).reshape(3, local)
    grad_qv_bias = jnp.stack([bias_sums[0], bias_sums[2]])
    grad_qkv, grad_proj = lax.psum((grad_qkv, grad_proj), "dp")
    biases = lax.psum(
        (grad_fc1_bias, grad_fc2_bias, grad_proj_bias, grad_qv_bias), "dp"
    )
    grad_fc1_bias, grad_fc2_bias, grad_proj_bias, grad_qv_bias = biases

    latents_grad, stats_one = latents_back(dh1, dx1, latents, mod, 256)

    dmod = jnp.stack(
        [
            stats_one[:, 0],
            stats_one[:, 1],
            stats_two[:, 0],
            stats_two[:, 1],
            stats_two[:, 2],
            stats_two[:, 3],
        ],
        1,
    )
    dmod = dmod.reshape(lat, 6 * dim).astype(BF)
    dmod_own = lax.dynamic_slice_in_dim(dmod, mp_at * cols, cols, 1)
    every = lax.all_gather(jnp.concatenate([cond_low, dmod_own], 1), "dp", axis=0, tiled=True)
    grad_ada = tn(every[:, :dim], every[:, dim:])
    grad_ada_bias = jnp.sum(every[:, dim:].astype(F32), 0)
    grad_act = lax.psum(nt(dmod_own, ada_weight), "mp")
    condition_grad = jax.vjp(jax.nn.silu, condition)[1](grad_act)[0]

    back = lambda v: v.astype(F32)
    return (
        block_out,
        latents_grad,
        condition_grad,
        back(grad_qkv).reshape(3, local, dim).transpose(2, 0, 1),
        grad_qv_bias,
        back(grad_proj),
        grad_proj_bias,
        back(grad_fc1),
        grad_fc1_bias,
        back(grad_fc2),
        grad_fc2_bias,
        grad_ada,
        grad_ada_bias,
    )


def solution(mesh):
    in_specs = (
        P("dp", None, None),
        P("dp", None),
        P("dp", None, None),
        P(None, None, "mp"),
        P(None, "mp"),
        P("mp", None),
        P(),
        P(None, "mp"),
        P("mp"),
        P("mp", None),
        P(),
        P(None, "mp"),
        P("mp"),
    )
    out_specs = (
        P("dp", None, None),
        P("dp", None, None),
        P("dp", None),
        P(None, None, "mp"),
        P(None, "mp"),
        P("mp", None),
        P(),
        P(None, "mp"),
        P("mp"),
        P("mp", None),
        P(),
        P(None, "mp"),
        P("mp"),
    )
    body = functools.partial(per_device, mesh.shape["dp"], mesh.shape["mp"])
    return jax.shard_map(body, mesh=mesh, in_specs=in_specs, out_specs=out_specs, check_vma=False)
```

time: 1790 us -> 1120 us (0.63)
  waiting for transfers between devices: 1120 us -> 496 us
  Pallas kernels: 0 us -> 380 us
  matrix products: 300 us -> 55.9 us
  other arithmetic: 201 us -> 26.8 us
    psum x4 -> x2, waiting for transfers between devices: 1120 us -> 329 us  [the longest x1 242 us: per_device(): dh1.append(lax.psum(dh1_i, 'mp'))]
    pallas_call x0 -> x4, Pallas kernels: none -> 380 us  [the longest x1 229 us: mlp_both(): pl.pallas_call(mlp_kernel, grid_spec=pltpu.PrefetchScalarGridSpec(num_sca...]
    dot_general x27 -> x7, matrix products: 300 us -> 55.9 us  [the longest x3 33.7 us: tn(): lax.dot_general(a, b, (((0,), (0,)), ((), ())), preferred_element_type=F32)]
    all_gather x0 -> x1, waiting for transfers between devices: none -> 166 us  [per_device(): lax.all_gather(mine, ('dp', 'mp'), axis=0).reshape(n_dp, n_mp, share, dim)]
    reduce_sum x14 -> x4, other arithmetic: 125 us -> 8.04 us  [the longest x1 4.07 us: per_device(): grad_fc1_bias = jnp.sum(flat(du).astype(F32), 0)]
    convert_element_type x12 -> x6, other arithmetic: 74.9 us -> 8.59 us  [the longest x3 8.49 us: per_device(): back = lambda v: v.astype(F32)]
    pallas_call x0 -> x2, local copies, waits for them, and re-layouts: none -> 38.1 us  [attn_bwd(): pl.pallas_call(functools.partial(attn_bwd_kernel, rows=rows), grid=(1,),...]
    another operation x9 -> x2, local copies, waits for them, and re-layouts: 32.5 us -> 0.16 us  [the longest x1 0.09 us: per_device(): qv_all = small[:, lat, :2 * local].reshape(n_mp, 2, local)]
  transfers between devices with their start and end apart: 4 -> 3, of which waited for: 4 -> 3; matrix products, arithmetic and copies ran while one was open for 6% -> 2% of each run, Pallas kernels for 0% -> 0%
where the time goes in v1:
time: 1120 us
  waiting for transfers between devices  496 us (44%)
  Pallas kernels  380 us (34%)
  local copies, waits for them, and re-layouts  76.4 us (7%)
  blocking collectives  68.1 us (6%)
  matrix products  55.9 us (5%)
  other arithmetic  26.8 us (2%)
  between operations  14.3 us (1%)
    psum x1, waiting for transfers between devices, per_device(): dh1.append(lax.psum(dh1_i, 'mp'))  242 us
    pallas_call x1, Pallas kernels, mlp_both(): pl.pallas_call(mlp_kernel, grid_spec=pltpu.PrefetchScalarGridSpec(num_sca...  229 us
    all_gather x1, waiting for transfers between devices, per_device(): lax.all_gather(mine, ('dp', 'mp'), axis=0).reshape(n_dp, n_mp, share, dim)  166 us
    pallas_call x1, Pallas kernels, attn_fwd(): pl.pallas_call(attn_fwd_kernel, grid_spec=pltpu.PrefetchScalarGridSpec(nu...  116 us
    psum x1, waiting for transfers between devices, per_device(): grad_qkv, grad_proj = lax.psum((grad_qkv, grad_proj), 'dp')  87.5 us
    pallas_call x2, local copies, waits for them, and re-layouts, attn_bwd(): pl.pallas_call(functools.partial(attn_bwd_kernel, rows=rows), grid=(1,),...  38.1 us
    dot_general x3, matrix products, tn(): lax.dot_general(a, b, (((0,), (0,)), ((), ())), preferred_element_type=F32)  33.7 us
    psum x1, blocking collectives, per_device(): lax.psum((grad_fc1_bias, grad_fc2_bias, grad_proj_bias, grad_qv_bias), 'dp')  26.4 us
  transfers between devices with their start and end apart: 3, of which 3 were waited for; matrix products, arithmetic and copies ran while one was open for 2% of the time, Pallas kernels for 0%

profile of v1, /device:TPU:0, one launch (start us, length us, event | category | flops | bytes accessed | tf_op | source)
XLA Modules:
  0.0 1118.2 jit_solution(5682445316923596798)
XLA Ops:
  7.3 5.4 copy.38
  12.7 2.7 fusion.5
  15.7 3.3 convolution_add_fusion
  19.0 15.6 %all-gather.2 = f32[4,4,1728]{2,1,0:T(4,128)S(1)} all-gather(f32[1,4,1728]{2,1,0:T(4,128)S(1)} %maximum_bitcast_fusion.1), channel_id=2, replica_groups=mesh['dp'=8,'mp'=4] {'mp'}, dimensions={0}, use_global_device_ids=true | all-gather | bytes 138240 | tf_op jit(solution)/shard_map/all_gather | solution.py:400
  35.6 2.9 reshape.113.bias_ref
  40.5 166.4 %all-gather.6.cloned.1.call-done = bf16[13824,1152]{1,0:T(8,128)(2,1)} async-done(((bf16[432,1152]{1,0:T(8,128)(2,1)}), bf16[13824,1152]{1,0:T(8,128)(2,1)}) %all-gather.6.cloned.1.call-update) | async-done | bytes 31850512 | tf_op jit(solution)/shard_map/all_gather | solution.py:414
  206.9 22.0 %copy.39 = bf16[8,4,432,1152]{3,2,0,1:T(8,128)(2,1)} copy(bf16[8,4,432,1152]{3,2,1,0:T(8,128)(2,1)} %bitcast.62) | data formatting | bytes 63700992 | tf_op jit(solution)/shard_map/reshape | solution.py:414
  228.9 116.4 %attn_fwd.1 = (bf16[4,3,288,1024]{3,2,1,0:T(8,128)(2,1)}, bf16[3,12,72,1024]{3,2,1,0:T(8,128)(2,1)}, f32[3,4,1024]{2,1,0:T(4,128)}, bf16[3,1024,1152]{2,1,0:T(8,128)(2,1)}) custom-call(s32[1]{0:T(128)} %bitcast.me_ref, bf16[3,1024,1152]{2,1,0:T(8,128)(2,1)} %lat_ref.5, f32[3,6,1152]{2,1,0:T(8,128)} %reshape.92.mod_ref, bf16[4,3456,1152]{2,1,0:T(8,128)(2,1)} %bitcast.54, ...), custom_call_target="tpu_custom_call" | custom-call | tf_op jit(solution)/shard_map/attn_fwd/pallas_call | solution.py:92
  345.3 1.6 dynamic-slice_bitcast_fusion.heads_ref
  347.0 228.6 %mlp_both.1 = (bf16[3,1024,1152]{2,1,0:T(8,128)(2,1)}, bf16[3,1024,1152]{2,1,0:T(8,128)(2,1)}, bf16[3,1024,1152]{2,1,0:T(8,128)(2,1)}, bf16[3,1024,1152]{2,1,0:T...) custom-call(s32[1]{0:T(128)} %bitcast.me_ref, ...), custom_call_target="tpu_custom_call" | custom-call | tf_op jit(solution)/shard_map/mlp_both/pallas_call | solution.py:230
  575.6 6.4 fusion.2
  582.0 20.1 %attn_bwd.3 = (bf16[1,864,1024]{2,1,0:T(8,128)(2,1)}, bf16[1,1024,1152]{2,1,0:T(8,128)(2,1)}) custom-call(bf16[3,1024,1152]{2,1,0:T(8,128)(2,1)} %get-tuple-element.35.da_ref, bf16[3,288,1024]{2,1,0:T(8,128)(2,1)} %copy-done.3, bf16[3,12,72,1024]{3,2,1,0:T(8,128)(2,1)} %get-tuple-element.36.qkv_ref, f32[3,4,1024]{2,1,0:T(4,128)} %get-tuple-element.37.lse_ref, ...), custom_call_target="tpu_custom_call" | custom-call | tf_op jit(solution)/shard_map/attn_bwd/pallas_call | solution.py:310
  602.1 2.8 constant_dynamic-update-slice_fusion.2
  604.9 19.0 %attn_bwd.5 = (bf16[3,864,1024]{2,1,0:T(8,128)(2,1)}, bf16[1,1024,1152]{2,1,0:T(8,128)(2,1)}) fusion(bf16[3,864,1024]{2,1,0:T(8,128)(2,1)} %constant_dynamic-update-slice_fusion.2, bf16[3,1024,1152]{2,1,0:T(8,128)(2,1)} %get-tuple-element.35.da_ref, bf16[3,288,1024]{2,1,0:T(8,128)(2,1)S(1)} %copy-done.4, ...), kind=kCustom, calls=%fused_computation.41 | custom fusion | bytes 20987904 | tf_op jit(solution)/shard_map/attn_bwd/pallas_call | solution.py:310
  623.9 19.1 %attn_bwd.4 = (bf16[3,864,1024]{2,1,0:T(8,128)(2,1)}, bf16[1,1024,1152]{2,1,0:T(8,128)(2,1)}) fusion(bf16[3,864,1024]{2,1,0:T(8,128)(2,1)} %get-tuple-element.58, bf16[3,1024,1152]{2,1,0:T(8,128)(2,1)} %get-tuple-element.35.da_ref, bf16[3,288,1024]{2,1,0:T(8,128)(2,1)S(1)} %copy-done.4, bf16[3,12,72,1024]{3,2,1,0:T(8,128)(2,1)} %get-tuple-element.36.qkv_ref, ...), kind=kCustom, calls=%fused_computation.40 | custom fusion | bytes 20987904 | tf_op jit(solution)/shard_map/attn_bwd/pallas_call | solution.py:310
  643.0 12.0 %bitcast_convert_fusion = bf16[864,1152]{1,0:T(8,128)(2,1)} fusion(bf16[3,864,1024]{2,1,0:T(8,128)(2,1)} %get-tuple-element.54, bf16[3,1024,1152]{2,1,0:T(8,128)(2,1)} %get-tuple-element.48), kind=kOutput, calls=%fused_computation.11 | convolution fusion | flops 6116290560 | bytes 14376960 | tf_op jit(solution)/shard_map/les,lsd->ed/dot_general | solution.py:448
  655.0 14.5 %fusion = bf16[1152,1152]{1,0:T(8,128)(2,1)} fusion(bf16[3,1024,1152]{2,1,0:T(8,128)(2,1)} %get-tuple-element.49, bf16[3,1024,1152]{2,1,0:T(8,128)(2,1)} %get-tuple-element.50), kind=kOutput, calls=%fused_computation.8 | convolution fusion | flops 8155054080 | bytes 16809984 | tf_op jit(solution)/shard_map/dot_general | solution.py:29
  669.5 14.7 %fusion.1 = bf16[1152,1152]{1,0:T(8,128)(2,1)} fusion(bf16[3,1024,1152]{2,1,0:T(8,128)(2,1)} %get-tuple-element.51, bf16[3,1024,1152]{2,1,0:T(8,128)(2,1)} %get-tuple-element.52), kind=kOutput, calls=%fused_computation.9 | convolution fusion | flops 8155054080 | bytes 16809984 | tf_op jit(solution)/shard_map/dot_general | solution.py:29
  685.0 3.3 convert_reduce_fusion.1
  688.4 4.1 convert_reduce_fusion
  692.5 26.4 %all-reduce = (f32[2,288]{1,0:T(2,128)}, f32[1152]{0:T(1024)}, f32[1152]{0:T(1024)}, f32[1152]{0:T(1024)}) all-reduce(f32[2,288]{1,0:T(2,128)S(1)} %pad_maximum_fusion.2, f32[1152]{0:T(1024)S(1)} %get-tuple-element.62, f32[1152]{0:T(1024)S(1)} %convert_reduce_fusion, ...), channel_id=1, replica_groups=mesh['dp'=8,'mp'=4] {'dp'}, use_global_device_ids=true, to_apply=%region_6.7 | all-reduce | flops 4032 | bytes 32256 | tf_op jit(solution)/shard_map/psum | solution.py:453
  718.9 87.5 %all-reduce.6.cloned.1.call-done = (bf16[1152,3,288]{0,2,1:T(8,128)(2,1)}, bf16[288,1152]{1,0:T(8,128)(2,1)}, bf16[1152,1152]{1,0:T(8,128)(2,1)}, bf16[1152,1152]{1,0:T(8,128)(2,1)}) async-done(((bf16[1152,3,288]{0,2,1:T(8,128)(2,1)}, bf16[288,1152]{1,0:T(8,128)(2,1)}, bf16[1152,1152]{1,0:T(8,128)(2,1)}, bf16[1152,1152]{1,0:T(8,128)(2,1)}), (bf16[1152,3,288]{0,2,1:T(8,128)(2,1)}, ...) | async-done | bytes 7962640 | tf_op jit(solution)/shard_map/psum | solution.py:452
  806.5 4.6 convert_element_type.63
  811.1 2.7 convert_element_type.66
  813.8 2.4 transpose.24
  816.2 1.1 convert_element_type.61
  817.4 241.6 %all-reduce.8.cloned.1.call-done = (bf16[1,1024,1152]{2,1,0:T(8,128)(2,1)}, bf16[1,1024,1152]{2,1,0:T(8,128)(2,1)}, bf16[1,1024,1152]{2,1,0:T(8,128)(2,1)}) async-done(((bf16[1,1024,1152]{2,1,0:T(8,128)(2,1)}, bf16[1,1024,1152]{2,1,0:T(8,128)(2,1)}, bf16[1,1024,1152]{2,1,0:T(8,128)(2,1)}), (bf16[1,1024,1152]{2,1,0:T(8,128)(2,1)}, bf16[1,1024,1152]{2,1,0:T(8,128)(2,1)}, ...) | async-done | bytes 7077904 | tf_op jit(solution)/shard_map/psum | solution.py:445
  1058.9 4.2 pad_maximum_fusion.dh1_ref
  1063.3 15.3 %latents_back.1 = (bf16[3,1024,1152]{2,1,0:T(8,128)(2,1)}, f32[3,8,1152]{2,1,0:T(8,128)S(1)}) custom-call(bf16[3,1024,1152]{2,1,0:T(8,128)(2,1)S(1)} %pad_maximum_fusion.dh1_ref, bf16[3,1024,1152]{2,1,0:T(8,128)(2,1)S(1)} %bitcast.53, bf16[3,1024,1152]{2,1,0:T(8,128)(2,1)} %lat_ref.5, f32[3,6,1152]{2,1,0:T(8,128)S(1)} %copy-done), custom_call_target="tpu_custom_call" | custom-call | tf_op jit(solution)/shard_map/latents_back/pallas_call | solution.py:357
  1078.8 9.2 all-gather.3
  1088.2 4.5 fusion.6
  1093.9 16.9 %psum.87 = f32[3,1152]{1,0:T(4,128)S(1)} all-reduce(f32[3,1152]{1,0:T(4,128)S(1)} %fusion.21), channel_id=1, replica_groups=mesh['dp'=8,'mp'=4] {'mp'}, use_global_device_ids=true, to_apply=%region_3.4 | all-reduce | flops 3456 | bytes 27648 | tf_op jit(solution)/shard_map/psum | solution.py:476
  (81 shorter events, 6.6 us)
Async XLA Ops:
  7.2 5.5 copy-start.1
  7.2 5.5 copy-start.6
  7.2 199.7 %all-gather.6.cloned.1.call-start = ((), (), s32[]{:S(2)}) async-start(), calls=%async_computation | async-start | bytes 32845824 | tf_op jit(solution)/shard_map/all_gather | solution.py:414
  12.6 2.8 copy-start.14
  12.6 2.8 copy-start.15
  12.6 2.9 copy-start.18
  12.6 3.0 copy-start.11
  15.4 23.9 %copy-start.16 = (bf16[1152]{0:T(1024)(128)(2,1)S(1)}, bf16[1152]{0:T(1024)(128)(2,1)}, u32[]{:S(2)}) copy-start(bf16[1152]{0:T(1024)(128)(2,1)} %param.23) | copy-start | bytes 6916
  15.4 24.5 %copy-start.17 = (bf16[1152]{0:T(1024)(128)(2,1)S(1)}, bf16[1152]{0:T(1024)(128)(2,1)}, u32[]{:S(2)}) copy-start(bf16[1152]{0:T(1024)(128)(2,1)} %param.19) | copy-start | bytes 6916
  15.4 791.0 %all-reduce.6.cloned.1.call-start = ((), (), s32[]{:S(2)}) async-start(), calls=%async_computation.1 | async-start | bytes 15925248 | tf_op jit(solution)/shard_map/psum | solution.py:452
  346.9 228.6 %copy-start.3 = (bf16[3,288,1024]{2,1,0:T(8,128)(2,1)}, bf16[3,288,1024]{2,1,0:T(8,128)(2,1)S(1)}, u32[]{:S(2)}) copy-start(bf16[3,288,1024]{2,1,0:T(8,128)(2,1)S(1)} %dynamic-slice_bitcast_fusion.heads_ref) | copy-start | bytes 5308420
  581.9 22.9 %copy-start.2 = (bf16[1152,3,288]{0,2,1:T(8,128)(2,1)S(1)}, bf16[1152,3,288]{0,2,1:T(8,128)(2,1)}, u32[]{:S(2)}) copy-start(bf16[1152,3,288]{0,2,1:T(8,128)(2,1)} %param.16) | copy-start | bytes 5971972
  582.0 22.9 %copy-start.4 = (bf16[3,288,1024]{2,1,0:T(8,128)(2,1)S(1)}, bf16[3,288,1024]{2,1,0:T(8,128)(2,1)}, u32[]{:S(2)}) copy-start(bf16[3,288,1024]{2,1,0:T(8,128)(2,1)} %copy-done.3) | copy-start | bytes 5308420
  582.0 22.9 %copy-start.10 = (f32[3,4,1024]{2,1,0:T(4,128)S(1)}, f32[3,4,1024]{2,1,0:T(4,128)}, u32[]{:S(2)}) copy-start(f32[3,4,1024]{2,1,0:T(4,128)} %get-tuple-element.37.lse_ref) | copy-start | bytes 147460
  684.2 374.7 %all-reduce.8.cloned.1.call-start = ((), (), s32[]{:S(2)}) async-start(), calls=%async_computation.2 | async-start | bytes 14155776 | tf_op jit(solution)/shard_map/psum | solution.py:445
  684.3 4.1 copy-start.13
  684.3 4.1 copy-start
  806.5 4.6 copy-start.7
  811.1 2.7 copy-start.8
  811.1 5.1 copy-start.9
  813.8 249.3 %slice-start = ((s8[7077888]{0:T(1024)(128)(4,1)}), s8[2883584]{0:T(1024)(128)(4,1)S(1)}, s32[]{:S(2)}) async-start(s8[7077888]{0:T(1024)(128)(4,1)} %bitcast.52), calls=%async_computation.3 | async-start | bytes 5767168
  1058.9 4.4 slice-start.1
  1088.1 5.1 copy-start.5
  1088.1 22.7 %copy-start.12 = (f32[3,1152]{1,0:T(4,128)S(1)}, f32[3,1152]{1,0:T(4,128)}, u32[]{:S(2)}) copy-start(f32[3,1152]{1,0:T(4,128)} %param.14) | copy-start | bytes 41476
Sparse Core Ops, SparseCore 0:
  15.5 191.3 all-gather.5
  684.3 122.0 all-reduce.5
  809.8 249.0 all-reduce.7

commit v2 on v1

--- a/solution.py
+++ b/solution.py
@@ -41,25 +41,82 @@
     return inv_std * (grad_normed - first - normed * second)
 
 
-def attn_fwd_kernel(
-    me_ref, lat_ref, mod_ref, w_ref, bias_ref, heads_ref, qkv_ref, lse_ref, h1_ref, h1_all
-):
-    slot, lat = pl.program_id(0), pl.program_id(1)
-    n_heads = qkv_ref.shape[1] // 3
-    seq = lat_ref.shape[1]
-
-    @pl.when(slot == 0)
-    def _():
-        normed, _ = norm_stats(lat_ref[0].astype(F32))
-        h1 = (normed * (1.0 + mod_ref[0, 1:2]) + mod_ref[0, 0:1]).astype(BF)
-        h1_all[lat] = h1
-        h1_ref[0] = h1
-
-    flat = nt(w_ref[0], h1_all[lat]) + bias_ref[0]
+def flip(value, bit):
+    step = 1 << bit
+    return value + step - 2 * step * (value // step % 2)
+
+
+def other_part(me, k):
+    return (me + k) % 2 + 2 * ((me // 2 + k // 2) % 2)
+
+
+def line_peers(me, n):
+    return jnp.minimum(me, 1) + jnp.minimum(n - 1 - me, 1)
+
+
+def at_mesh(dp_at, mp_at):
+    return {"device_id": (dp_at, mp_at), "device_id_type": pl.DeviceIdType.MESH}
+
+
+def modulation_kernel(cond_ref, w_ref, bias_ref, row_ref, out_ref, low_ref, send, recv):
+    dp_at, me = lax.axis_index("dp"), lax.axis_index("mp")
+    n_mp = out_ref.shape[0]
+    lat = cond_ref.shape[0]
+    barrier = pltpu.get_barrier_semaphore()
+    for k in range(1, n_mp):
+        pl.semaphore_signal(barrier, inc=1, **at_mesh(dp_at, (me + k) % n_mp))
+    cond = cond_ref[...]
+    low = (cond * jax.nn.sigmoid(cond)).astype(BF)
+    low_ref[...] = low
+    part = mm(low, w_ref[...]) + bias_ref[...]
+    cols = part.shape[1]
+    out_ref[me] = jnp.concatenate([part, row_ref[...], jnp.zeros((8 - lat - 1, cols), F32)], 0)
+    pl.semaphore_wait(barrier, n_mp - 1)
+    copies = []
+    for k in range(1, n_mp):
+        copies.append(
+            pltpu.make_async_remote_copy(
+                out_ref.at[me],
+                out_ref.at[me],
+                send.at[k - 1],
+                recv.at[k - 1],
+                **at_mesh(dp_at, (me + k) % n_mp),
+            )
+        )
+        copies[-1].start()
+    for k in range(1, n_mp):
+        came = out_ref.at[(me + n_mp - k) % n_mp]
+        pltpu.make_async_remote_copy(
+            came, came, send.at[k - 1], recv.at[k - 1], **at_mesh(dp_at, (me + k) % n_mp)
+        ).wait_recv()
+    for copy in copies:
+        copy.wait_send()
+
+
+def modulation_all(condition, ada_weight, ada_bias, bias_row, n_mp):
+    cols = ada_weight.shape[1]
+    vmem = pl.BlockSpec(memory_space=pltpu.VMEM)
+    return pl.pallas_call(
+        modulation_kernel,
+        in_specs=[vmem] * 4,
+        out_specs=[vmem, vmem],
+        out_shape=[
+            jax.ShapeDtypeStruct((n_mp, 8, cols), F32),
+            jax.ShapeDtypeStruct(condition.shape, BF),
+        ],
+        scratch_shapes=[pltpu.SemaphoreType.DMA((n_mp - 1,))] * 2,
+        compiler_params=pltpu.CompilerParams(
+            collective_id=0, has_side_effects=True, vmem_limit_bytes=40 * MIB
+        ),
+        name="modulation",
+    )(condition, ada_weight, ada_bias, bias_row)
+
+
+def attend(flat, n_heads, slot, heads_ref, qkv_ref, lse_ref, between):
+    seq = flat.shape[1]
     parts = flat.reshape(3 * n_heads, HEAD_DIM, seq)
     scaling = LOG2E / HEAD_DIM**0.5
     outs = []
-    lses = []
     for h in range(n_heads):
         q_t = (parts[h] * scaling).astype(BF)
         k_t = parts[n_heads + h]
@@ -71,16 +128,281 @@
         out = mm(v_ext, probs)
         total = out[HEAD_DIM : HEAD_DIM + 1]
         outs.append(out[:HEAD_DIM] * (1.0 / total))
-        lses.append(top + jnp.log2(total))
+        lse = top + jnp.log2(total)
 
         @pl.when(slot == 0)
         def _():
             qkv_ref[0, h] = q_t
             qkv_ref[0, n_heads + h] = k_t.astype(BF)
             qkv_ref[0, 2 * n_heads + h] = v_t.astype(BF)
-            lse_ref[0, h : h + 1] = lses[h]
-
+            lse_ref[0, h : h + 1] = lse
+
+        between(h + 1)
     heads_ref[0, 0] = jnp.concatenate(outs, 0).astype(BF)
+
+
+def mixed_one(lat_ref, mod_ref, h1_ref, h1_all, lat):
+    normed, _ = norm_stats(lat_ref[0].astype(F32))
+    h1 = (normed * (1.0 + mod_ref[0, 1:2]) + mod_ref[0, 0:1]).astype(BF)
+    h1_all[lat] = h1
+    h1_ref[0] = h1
+
+
+def attn_fwd_kernel(
+    me_ref, lat_ref, mod_ref, w_ref, bias_ref, heads_ref, qkv_ref, lse_ref, h1_ref, h1_all
+):
+    slot, lat = pl.program_id(0), pl.program_id(1)
+
+    @pl.when(slot == 0)
+    def _():
+        mixed_one(lat_ref, mod_ref, h1_ref, h1_all, lat)
+
+    flat = nt(w_ref[0], h1_all[lat]) + bias_ref[0]
+    attend(flat, qkv_ref.shape[1] // 3, slot, heads_ref, qkv_ref, lse_ref, lambda h: None)
+
+
+def attn_gather_kernel(
+    lat_ref,
+    mod_ref,
+    bias_ref,
+    own_ref,
+    heads_ref,
+    qkv_ref,
+    lse_ref,
+    h1_ref,
+    all_ref,
+    h1_all,
+    w_buf,
+    local_sem,
+    z_own,
+    z_on,
+    z_got,
+    sends,
+    recvs,
+):
+    n_mp = all_ref.shape[0]
+    lats = h1_all.shape[0]
+    units = 3 * (n_mp - 1)
+    slot, lat = pl.program_id(0), pl.program_id(1)
+    step = slot * lats + lat
+    dp_at, me = lax.axis_index("dp"), lax.axis_index("mp")
+    core, x, y = dp_at % 2, dp_at // 2 % 2, dp_at // 4
+    rows = own_ref.shape[4]
+    cut = rows // 32 * 16 + 16
+    near, far = pl.ds(0, cut), pl.ds(cut, rows - cut)
+    every = pl.ds(0, rows)
+    both = pl.ds(0, 2)
+    core_id = at_mesh(flip(dp_at, 0), me)
+    x_id = at_mesh(flip(dp_at, 1), me)
+    y_id = at_mesh(flip(dp_at, 2), me)
+    right_id, left_id = at_mesh(dp_at, me + 1), at_mesh(dp_at, me - 1)
+
+    def piece(s, c, at_y, at_x, at_core, part):
+        return all_ref.at[s, c, at_y, at_x, at_core, part]
+
+    def own_copy(c, side, target):
+        return pltpu.make_async_remote_copy(
+            own_ref.at[c, y, x, core],
+            piece(me, c, y, x, core, every),
+            z_own.at[side, c],
+            z_got.at[c, me],
+            **target,
+        )
+
+    def pass_on(s, c, target):
+        ref = piece(s, c, y, x, core, every)
+        return pltpu.make_async_remote_copy(
+            ref, ref, z_on.at[c, s], z_got.at[c, s], **target
+        )
+
+    def move(kind, c, s, arrived=False):
+        flipped = lambda v: 1 - v if arrived else v
+        at_y, at_x, at_core, part, target = (
+            (pl.ds(y, 1), pl.ds(flipped(x), 1), pl.ds(core, 1), near, x_id),
+            (pl.ds(flipped(y), 1), pl.ds(x, 1), pl.ds(core, 1), far, y_id),
+            (pl.ds(flipped(y), 1), both, pl.ds(core, 1), near, y_id),
+            (both, pl.ds(flipped(x), 1), pl.ds(core, 1), far, x_id),
+            (both, both, pl.ds(flipped(core), 1), every, core_id),
+        )[kind]
+        ref = piece(s, c, at_y, at_x, at_core, part)
+        return pltpu.make_async_remote_copy(
+            ref, ref, sends.at[kind, c, s], recvs.at[kind, c, s], **target
+        )
+
+    def unit(u):
+        return u // (n_mp - 1), other_part(me, 1 + u % (n_mp - 1))
+
+    def event(stage, u):
+        c, s = unit(u)
+
+        @pl.when((u >= 0) & (u < units))
+        def _():
+            if stage == 1:
+                pass_on(s, c, right_id).wait_recv()
+
+                @pl.when((s < me) & (me < n_mp - 1))
+                def _():
+                    pass_on(s, c, right_id).start()
+
+                @pl.when((s > me) & (me > 0))
+                def _():
+                    pass_on(s, c, left_id).start()
+
+                move(0, c, s).start()
+                move(1, c, s).start()
+            if stage == 2:
+                move(0, c, s, True).wait_recv()
+                move(1, c, s, True).wait_recv()
+                move(2, c, s).start()
+                move(3, c, s).start()
+            if stage == 3:
+                move(2, c, s, True).wait_recv()
+                move(3, c, s, True).wait_recv()
+                move(4, c, s).start()
+            if stage == 4:
+                move(4, c, s, True).wait_recv()
+
+    def send_own(c):
+        @pl.when(me < n_mp - 1)
+        def _():
+            own_copy(c, 0, right_id).start()
+
+        @pl.when(me > 0)
+        def _():
+            own_copy(c, 1, left_id).start()
+
+    @pl.when(step == 0)
+    def _():
+        barrier = pltpu.get_barrier_semaphore()
+        for target in (core_id, x_id, y_id):
+            pl.semaphore_signal(barrier, inc=1, **target)
+
+        @pl.when(me < n_mp - 1)
+        def _():
+            pl.semaphore_signal(barrier, inc=1, **right_id)
+
+        @pl.when(me > 0)
+        def _():
+            pl.semaphore_signal(barrier, inc=1, **left_id)
+
+        pl.semaphore_wait(barrier, 3 + line_peers(me, n_mp))
+        send_own(0)
+
+    for c in (1, 2):
+
+        @pl.when(step == 3 * c - 1)
+        def _():
+            send_own(c)
+
+    event(4, step - 3)
+    event(3, step - 2)
+
+    @pl.when((lat == 0) & (slot == 0))
+    def _():
+        load = pltpu.make_async_copy(own_ref.at[0], w_buf, local_sem.at[0])
+        load.start()
+        load.wait()
+
+    @pl.when((lat == 0) & (slot > 0))
+    def _():
+        load = pltpu.make_async_copy(all_ref.at[other_part(me, slot), 0], w_buf, local_sem.at[0])
+        load.start()
+        load.wait()
+
+    @pl.when(slot == 0)
+    def _():
+        mixed_one(lat_ref, mod_ref, h1_ref, h1_all, lat)
+
+    n_heads = qkv_ref.shape[1] // 3
+    weights = w_buf[...].reshape(8 * rows, w_buf.shape[-1])[: 3 * n_heads * HEAD_DIM]
+    flat = nt(weights, h1_all[lat]) + bias_ref[0]
+
+    def between(h):
+        if h == 1:
+            event(2, step - 1)
+        if h == 3:
+            event(1, step)
+
+    attend(flat, n_heads, slot, heads_ref, qkv_ref, lse_ref, between)
+
+    @pl.when(step == n_mp * lats - 1)
+    def _():
+        for c in range(3):
+
+            @pl.when(me < n_mp - 1)
+            def _():
+                own_copy(c, 0, right_id).wait_send()
+
+            @pl.when(me > 0)
+            def _():
+                own_copy(c, 1, left_id).wait_send()
+
+        def drain(u, carry):
+            c, s = unit(u)
+
+            @pl.when((s < me) & (me < n_mp - 1))
+            def _():
+                pass_on(s, c, right_id).wait_send()
+
+            @pl.when((s > me) & (me > 0))
+            def _():
+                pass_on(s, c, left_id).wait_send()
+
+            for kind in range(5):
+                move(kind, c, s).wait_send()
+            return carry
+
+        lax.fori_loop(0, units, drain, 0)
+
+
+def attn_gather(latents, mod, bias, own, n_mp):
+    lat, seq, dim = latents.shape
+    local = dim // n_mp
+    n_heads = local // HEAD_DIM
+    rows = own.shape[0] // 24
+    own = own.reshape(3, 2, 2, 2, rows, dim)
+    last = lat - 1
+    first = lambda s, l: s // n_mp * 0 + jnp.where(s == 0, l, last)
+    part = lambda s: other_part(lax.axis_index("mp"), s)
+    heads, qkv, lse, h1, gathered = pl.pallas_call(
+        attn_gather_kernel,
+        grid=(n_mp, lat),
+        in_specs=[
+            pl.BlockSpec((1, seq, dim), lambda s, l: (first(s, l), 0, 0)),
+            pl.BlockSpec((1, 6, dim), lambda s, l: (l, 0, 0)),
+            pl.BlockSpec((1, 3 * local, 1), lambda s, l: (part(s), 0, 0)),
+            pl.BlockSpec(memory_space=pl.ANY),
+        ],
+        out_specs=[
+            pl.BlockSpec((1, 1, local, seq), lambda s, l: (part(s), l, 0, 0)),
+            pl.BlockSpec((1, 3 * n_heads, HEAD_DIM, seq), lambda s, l: (first(s, l), 0, 0, 0)),
+            pl.BlockSpec((1, n_heads, seq), lambda s, l: (first(s, l), 0, 0)),
+            pl.BlockSpec((1, seq, dim), lambda s, l: (first(s, l), 0, 0)),
+            pl.BlockSpec(memory_space=pl.ANY),
+        ],
+        out_shape=[
+            jax.ShapeDtypeStruct((n_mp, lat, local, seq), BF),
+            jax.ShapeDtypeStruct((lat, 3 * n_heads, HEAD_DIM, seq), BF),
+            jax.ShapeDtypeStruct((lat, n_heads, seq), F32),
+            jax.ShapeDtypeStruct((lat, seq, dim), BF),
+            jax.ShapeDtypeStruct((n_mp, 3, 2, 2, 2, rows, dim), BF),
+        ],
+        scratch_shapes=[
+            pltpu.VMEM((lat, seq, dim), BF),
+            pltpu.VMEM((2, 2, 2, rows, dim), BF),
+            pltpu.SemaphoreType.DMA((1,)),
+            pltpu.SemaphoreType.DMA((2, 3)),
+            pltpu.SemaphoreType.DMA((3, n_mp)),
+            pltpu.SemaphoreType.DMA((3, n_mp)),
+            pltpu.SemaphoreType.DMA((5, 3, n_mp)),
+            pltpu.SemaphoreType.DMA((5, 3, n_mp)),
+        ],
+        compiler_params=pltpu.CompilerParams(
+            collective_id=1, has_side_effects=True, vmem_limit_bytes=60 * MIB
+        ),
+        name="attn_gather",
+    )(latents, mod, bias, own)
+    return heads, qkv, lse, h1, gathered.reshape(n_mp, 24 * rows, dim)
 
 
 def attn_fwd(me, latents, mod, gathered, bias, n_mp):
@@ -125,35 +447,127 @@
     )(me, latents, mod, gathered, bias)
 
 
-def mlp_kernel(
-    me_ref,
-    heads_ref,
-    lat_ref,
-    cot_ref,
-    mod_ref,
-    wp_ref,
-    w1_ref,
-    w2_ref,
-    bp_ref,
-    b1_ref,
-    b2_ref,
-    out_ref,
-    dx1_ref,
-    da_ref,
-    h2_ref,
-    dm_ref,
-    z_ref,
-    du_ref,
-    stats_ref,
-    macc,
-    dacc,
-):
-    n_mp, hid, dim = w1_ref.shape
+class LineSum:
+    def __init__(self, own_ref, up, down, sems, out_ref):
+        self.own, self.up, self.down, self.sems, self.out = own_ref, up, down, sems, out_ref
+        self.count, self.rows = up.shape[0], up.shape[1]
+        self.me = lax.axis_index("mp")
+        self.n = lax.axis_size("mp")
+        dp_at = lax.axis_index("dp")
+        self.ends = (at_mesh(dp_at, self.me + 1), at_mesh(dp_at, self.me - 1))
+        self.place = (self.me, self.n - 1 - self.me)
+
+    def guarded(self, side, first, action):
+        there = self.place[side] > 0 if first else self.place[side] < self.n - 1
+
+        @pl.when(there)
+        def _():
+            action()
+
+    def barrier(self):
+        sem = pltpu.get_barrier_semaphore()
+        for side in (0, 1):
+            self.guarded(side, False, lambda: pl.semaphore_signal(sem, inc=1, **self.ends[side]))
+        pl.semaphore_wait(sem, line_peers(self.me, self.n))
+
+    def copy(self, side, c):
+        ref = (self.up, self.down)[side].at[c]
+        return pltpu.make_async_remote_copy(
+            ref, ref, self.sems.at[2 * side, c], self.sems.at[2 * side + 1, c], **self.ends[side]
+        )
+
+    def handle(self, side, c):
+        ref = (self.up, self.down)[side]
+        own = self.own[0, pl.ds(pl.multiple_of(c * self.rows, self.rows), self.rows)]
+
+        @pl.when(self.place[side] == 0)
+        def _():
+            ref[c] = own
+
+        @pl.when(self.place[side] > 0)
+        def _():
+            self.copy(side, c).wait_recv()
+            ref[c] = (ref[c].astype(F32) + own.astype(F32)).astype(BF)
+
+        self.guarded(side, False, lambda: self.copy(side, c).start())
+
+    def tick(self, t):
+        for side in (0, 1):
+            at = t - 2 * self.place[side]
+
+            @pl.when((at >= 0) & (at % 3 < 2) & (at - at // 3 < self.count))
+            def _():
+                self.handle(side, at - at // 3)
+
+    def finish(self, ticks):
+        for side in (0, 1):
+            done = jnp.maximum(ticks - 2 * self.place[side], 0)
+            done = jnp.minimum(done - done // 3, self.count)
+
+            def late(c, carry):
+                self.handle(side, c)
+                return carry
+
+            lax.fori_loop(done, self.count, late, 0)
+
+        def add(c, carry):
+            rows = pl.ds(pl.multiple_of(c * self.rows, self.rows), self.rows)
+            total = self.up[c].astype(F32) + self.down[c].astype(F32)
+            self.out[0, rows] = (total - self.own[0, rows].astype(F32)).astype(BF)
+            return carry
+
+        lax.fori_loop(0, self.count, add, 0)
+        for side in (0, 1):
+
+            def sent(c, carry):
+                self.copy(side, c).wait_send()
+                return carry
+
+            self.guarded(side, False, lambda: lax.fori_loop(0, self.count, sent, 0))
+
+
+def mlp_kernel(*refs, summing):
+    heads_ref, lat_ref, cot_ref, mod_ref, own_ref, all_ref, bp_ref, b1_ref, b2_ref = refs[:9]
+    refs = refs[9:]
+    if summing:
+        part_ref, refs = refs[0], refs[1:]
+    out_ref, dx1_ref, da_ref, h2_ref, dm_ref, z_ref, du_ref, stats_ref = refs[:8]
+    refs = refs[8:]
+    if summing:
+        sum_ref, refs = refs[0], refs[1:]
+    macc, dacc, wp, w1, w2, load_sems = refs[:6]
+    n_mp, hid, dim = w1.shape
+    local = wp.shape[1]
     rows = lat_ref.shape[1]
+    me = lax.axis_index("mp")
+    step = pl.program_id(0)
+    line = LineSum(part_ref, refs[6], refs[7], refs[8], sum_ref) if summing else None
+
+    def load(kind, k):
+        at = own_ref if k == 0 else all_ref.at[(me + k) % n_mp]
+        first, count, ref = (
+            (3 * local, local, wp.at[(me + k) % n_mp]),
+            (4 * local, hid, w1.at[k]),
+            (4 * local + hid, hid, w2.at[k]),
+        )[kind]
+        return pltpu.make_async_copy(at.at[pl.ds(first, count)], ref, load_sems.at[kind, k])
+
+    @pl.when(step == 0)
+    def _():
+        if summing:
+            line.barrier()
+        for k in range(n_mp):
+            load(0, k).start()
+        for k in range(n_mp):
+            load(1, k).start()
+            load(2, k).start()
+        for k in range(n_mp):
+            load(0, k).wait()
+
     gate_one, shift_two = mod_ref[0, 2:3], mod_ref[0, 3:4]
     scale_two, gate_two = mod_ref[0, 4:5], mod_ref[0, 5:6]
     heads = heads_ref[:, 0].reshape(dim, rows)
-    attn = tn(heads, wp_ref[...].reshape(dim, dim)) + bp_ref[...]
+    attn = tn(heads, wp[...].reshape(dim, dim)) + bp_ref[...]
     x1 = lat_ref[0].astype(F32) + gate_one * attn
     n2, inv2 = norm_stats(x1)
     h2 = (n2 * (1.0 + scale_two) + shift_two).astype(BF)
@@ -165,11 +579,18 @@
     macc[...] = jnp.zeros_like(macc)
     dacc[...] = jnp.zeros_like(dacc)
 
-    def part(slot, own):
-        w1 = w1_ref[slot]
-        w2 = w2_ref[slot]
-        u = nt(h2_ref[0], w1) + b1_ref[slot]
-        dz = nt(dm_ref[0], w2)
+    def part(k, own):
+        if summing:
+            line.tick(step * n_mp + k)
+
+        @pl.when(step == 0)
+        def _():
+            for kind in (1, 2):
+                ref = (w1, w2)[kind - 1].at[k]
+                pltpu.make_async_copy(ref, ref, load_sems.at[kind, k]).wait()
+
+        u = nt(h2_ref[0], w1[k]) + b1_ref[(me + k) % n_mp]
+        dz = nt(dm_ref[0], w2[k])
         u2 = u * u
         t = jnp.tanh(u * (GELU_A + (GELU_A * GELU_B) * u2))
         half = 0.5 + 0.5 * t
@@ -179,13 +600,13 @@
         if own:
             z_ref[0] = z
             du_ref[0] = du
-        macc[...] += mm(z, w2)
-        dacc[...] += mm(du, w1)
-
-    part(me_ref[0], True)
-
-    def body(s, carry):
-        part(lax.rem(me_ref[0] + s, n_mp), False)
+        macc[...] += mm(z, w2[k])
+        dacc[...] += mm(du, w1[k])
+
+    part(0, True)
+
+    def body(k, carry):
+        part(k, False)
         return carry
 
     lax.fori_loop(1, n_mp, body, 0)
@@ -209,59 +630,116 @@
         0,
     )
 
-    @pl.when(pl.program_id(1) == 0)
+    @pl.when(step == 0)
     def _():
         stats_ref[0] = stats
 
-    @pl.when(pl.program_id(1) > 0)
+    @pl.when(step > 0)
     def _():
         stats_ref[0] += stats
 
-
-def mlp_both(me, heads, latents, cotangent, mod, gathered, bp, b1, b2, n_mp, rows):
+    if summing:
+
+        @pl.when(step == pl.num_programs(0) - 1)
+        def _():
+            line.finish(pl.num_programs(0) * n_mp)
+
+
+LINE_CHUNKS = 8
+
+
+def line_scratch(seq, dim):
+    rows = seq // LINE_CHUNKS
+    return [
+        pltpu.VMEM((LINE_CHUNKS, rows, dim), BF),
+        pltpu.VMEM((LINE_CHUNKS, rows, dim), BF),
+        pltpu.SemaphoreType.DMA((4, LINE_CHUNKS)),
+    ]
+
+
+def mlp_both(index, heads, latents, cotangent, mod, own, gathered, bp, b1, b2, n_mp, rows, part):
     lat, seq, dim = latents.shape
     local = dim // n_mp
     hid = b1.shape[2]
-    tok = pl.BlockSpec((1, rows, dim), lambda l, t, me: (l, t, 0))
-    hidden = pl.BlockSpec((1, rows, hid), lambda l, t, me: (l, t, 0))
-    once = lambda shape, at: pl.BlockSpec(
-        shape, lambda l, t, me: at, pipeline_mode=pl.Buffered(1)
+    tok = pl.BlockSpec((1, rows, dim), lambda t: (index, t, 0))
+    new = pl.BlockSpec((1, rows, dim), lambda t: (0, t, 0))
+    hidden = pl.BlockSpec((1, rows, hid), lambda t: (0, t, 0))
+    once = lambda shape: pl.BlockSpec(
+        shape, lambda t: (0,) * len(shape), pipeline_mode=pl.Buffered(1)
     )
+    any_spec = pl.BlockSpec(memory_space=pl.ANY)
+    summing = part is not None
+    extra = [once((1, seq, dim))] if summing else []
     return pl.pallas_call(
-        mlp_kernel,
-        grid_spec=pltpu.PrefetchScalarGridSpec(
-            num_scalar_prefetch=1,
-            grid=(lat, seq // rows),
-            in_specs=[
-                pl.BlockSpec((n_mp, 1, local, rows), lambda l, t, me: (0, l, 0, t)),
-                tok,
-                tok,
-                pl.BlockSpec((1, 6, dim), lambda l, t, me: (l, 0, 0)),
-                once((n_mp, local, dim), (0, 3, 0)),
-                once((n_mp, hid, dim), (0, 1, 0)),
-                once((n_mp, hid, dim), (0, 2, 0)),
-                once((1, dim), (0, 0)),
-                once((n_mp, 1, hid), (0, 0, 0)),
-                once((1, dim), (0, 0)),
-            ],
-            out_specs=[
-                tok,
-                tok,
-                tok,
-                tok,
-                tok,
-                hidden,
-                hidden,
-                pl.BlockSpec((1, 8, dim), lambda l, t, me: (l, 0, 0)),
-            ],
-            scratch_shapes=[pltpu.VMEM((rows, dim), F32)] * 2,
+        functools.partial(mlp_kernel, summing=summing),
+        grid=(seq // rows,),
+        in_specs=[
+            pl.BlockSpec((n_mp, 1, local, rows), lambda t: (0, index, 0, t)),
+            tok,
+            tok,
+            pl.BlockSpec((1, 6, dim), lambda t: (index, 0, 0)),
+            any_spec,
+            any_spec,
+            once((1, dim)),
+            once((n_mp, 1, hid)),
+            once((1, dim)),
+        ]
+        + extra,
+        out_specs=[new] * 5
+        + [hidden, hidden, pl.BlockSpec((1, 8, dim), lambda t: (0, 0, 0))]
+        + extra,
+        out_shape=[jax.ShapeDtypeStruct((1, seq, dim), BF)] * 5
+        + [jax.ShapeDtypeStruct((1, seq, hid), BF)] * 2
+        + [jax.ShapeDtypeStruct((1, 8, dim), F32)]
+        + ([jax.ShapeDtypeStruct((1, seq, dim), BF)] if summing else []),
+        scratch_shapes=[
+            pltpu.VMEM((rows, dim), F32),
+            pltpu.VMEM((rows, dim), F32),
+            pltpu.VMEM((n_mp, local, dim), BF),
+            pltpu.VMEM((n_mp, hid, dim), BF),
+            pltpu.VMEM((n_mp, hid, dim), BF),
+            pltpu.SemaphoreType.DMA((3, n_mp)),
+        ]
+        + (line_scratch(seq, dim) if summing else []),
+        compiler_params=pltpu.CompilerParams(
+            vmem_limit_bytes=63 * MIB,
+            **(dict(collective_id=3 + index, has_side_effects=True) if summing else {}),
         ),
-        out_shape=[jax.ShapeDtypeStruct((lat, seq, dim), BF)] * 5
-        + [jax.ShapeDtypeStruct((lat, seq, hid), BF)] * 2
-        + [jax.ShapeDtypeStruct((lat, 8, dim), F32)],
-        compiler_params=pltpu.CompilerParams(vmem_limit_bytes=60 * MIB),
-        name="mlp_both",
-    )(me, heads, latents, cotangent, mod, gathered, gathered, gathered, bp, b1, b2)
+        name="mlp_sum" if summing else "mlp_both",
+    )(
+        heads,
+        latents,
+        cotangent,
+        mod,
+        own,
+        gathered,
+        bp,
+        b1,
+        b2,
+        *([part] if summing else []),
+    )
+
+
+def line_kernel(part_ref, sum_ref, up, down, sems):
+    line = LineSum(part_ref, up, down, sems, sum_ref)
+    line.barrier()
+    line.finish(0)
+
+
+def line_sum(part):
+    _, seq, dim = part.shape
+    vmem = pl.BlockSpec(memory_space=pltpu.VMEM)
+    return pl.pallas_call(
+        line_kernel,
+        in_specs=[vmem],
+        out_specs=vmem,
+        out_shape=jax.ShapeDtypeStruct(part.shape, BF),
+        scratch_shapes=line_scratch(seq, dim),
+        compiler_params=pltpu.CompilerParams(
+            collective_id=2, has_side_effects=True, vmem_limit_bytes=40 * MIB
+        ),
+        name="line_sum",
+    )(part)
 
 
 def attn_bwd_kernel(da_ref, heads_ref, qkv_ref, lse_ref, wp_ref, wq_ref, dqkv_ref, dh1_ref, *, rows):
@@ -305,13 +783,14 @@
     n_heads = lse.shape[1]
     local = n_heads * HEAD_DIM
     one = lambda shape: pl.BlockSpec((1,) + shape, lambda i: (index,) + (0,) * len(shape))
+    only = lambda shape: pl.BlockSpec((1,) + shape, lambda i: (0,) * (len(shape) + 1))
     whole = lambda shape: pl.BlockSpec(shape, lambda i: (0,) * len(shape))
     out = lambda shape: pl.BlockSpec((1,) + shape, lambda i: (0,) * (len(shape) + 1))
     return pl.pallas_call(
         functools.partial(attn_bwd_kernel, rows=rows),
         grid=(1,),
         in_specs=[
-            one((seq, dim)),
+            only((seq, dim)),
             one((local, seq)),
             one((3 * n_heads, HEAD_DIM, seq)),
             one((n_heads, seq)),
@@ -342,26 +821,27 @@
         0,
     )
 
-    @pl.when(pl.program_id(1) == 0)
+    @pl.when(pl.program_id(0) == 0)
     def _():
         stats_ref[0] = stats
 
-    @pl.when(pl.program_id(1) > 0)
+    @pl.when(pl.program_id(0) > 0)
     def _():
         stats_ref[0] += stats
 
 
-def latents_back(dh1, dx1, latents, mod, rows):
+def latents_back(dh1, dx1, latents, mod, index, rows):
     lat, seq, dim = latents.shape
-    tok = pl.BlockSpec((1, rows, dim), lambda l, t: (l, t, 0))
+    tok = pl.BlockSpec((1, rows, dim), lambda t: (index, t, 0))
+    new = pl.BlockSpec((1, rows, dim), lambda t: (0, t, 0))
     return pl.pallas_call(
         latents_kernel,
-        grid=(lat, seq // rows),
-        in_specs=[tok, tok, tok, pl.BlockSpec((1, 6, dim), lambda l, t: (l, 0, 0))],
-        out_specs=[tok, pl.BlockSpec((1, 8, dim), lambda l, t: (l, 0, 0))],
+        grid=(seq // rows,),
+        in_specs=[new, new, tok, pl.BlockSpec((1, 6, dim), lambda t: (index, 0, 0))],
+        out_specs=[new, pl.BlockSpec((1, 8, dim), lambda t: (0, 0, 0))],
         out_shape=[
-            jax.ShapeDtypeStruct((lat, seq, dim), BF),
-            jax.ShapeDtypeStruct((lat, 8, dim), F32),
+            jax.ShapeDtypeStruct((1, seq, dim), BF),
+            jax.ShapeDtypeStruct((1, 8, dim), F32),
         ],
         compiler_params=pltpu.CompilerParams(vmem_limit_bytes=40 * MIB),
         name="latents_back",
@@ -394,10 +874,15 @@
     dp_at = lax.axis_index("dp")
     me = jnp.full((1,), mp_at, jnp.int32)
 
-    cond_low = jax.nn.silu(condition).astype(BF)
-    mod_part = mm(cond_low, ada_weight) + ada_bias.astype(F32)
+    direct = n_mp == 4 and n_dp == 8
     bias_row = jnp.concatenate([qv_bias.reshape(-1), fc1_bias]).astype(F32)[None]
-    small = lax.all_gather(jnp.concatenate([mod_part, bias_row], 0), "mp", axis=0)
+    ada_row = ada_bias.astype(F32)[None]
+    if direct:
+        small, cond_low = modulation_all(condition, ada_weight, ada_row, bias_row, n_mp)
+    else:
+        cond_low = jax.nn.silu(condition).astype(BF)
+        mod_part = mm(cond_low, ada_weight) + ada_row
+        small = lax.all_gather(jnp.concatenate([mod_part, bias_row], 0), "mp", axis=0)
     mod = small[:, :lat].transpose(1, 0, 2).reshape(lat, 6, dim)
     qv_all = small[:, lat, : 2 * local].reshape(n_mp, 2, local)
     b_qkv = jnp.stack([qv_all[:, 0], jnp.zeros((n_mp, local), F32), qv_all[:, 1]], 1).reshape(
@@ -409,25 +894,49 @@
         qkv_weight.reshape(dim, 3, n_heads, HEAD_DIM).transpose(1, 2, 3, 0).reshape(3 * local, dim)
     )
     own = jnp.concatenate([wq_own, proj_weight, fc1_weight.T, fc2_weight], 0)
-    share = own.shape[0] // n_dp
-    mine = lax.dynamic_slice_in_dim(own, dp_at * share, share, 0)
-    gathered = lax.all_gather(mine, ("dp", "mp"), axis=0).reshape(n_dp, n_mp, share, dim)
-    gathered = gathered.transpose(1, 0, 2, 3).reshape(n_mp, n_dp * share, dim)
-
-    heads, qkv, lse, h1 = attn_fwd(me, latents, mod, gathered, b_qkv, n_mp)
-    block_out, dx1, da, h2, dm, z, du, stats_two = mlp_both(
-        me,
-        heads,
-        latents,
-        cotangent,
-        mod,
-        gathered,
-        proj_bias.astype(F32)[None],
-        b_fc1,
-        fc2_bias.astype(F32)[None],
-        n_mp,
-        256,
-    )
+    if direct:
+        heads, qkv, lse, h1, gathered = attn_gather(latents, mod, b_qkv, own, n_mp)
+    else:
+        share = own.shape[0] // n_dp
+        mine = lax.dynamic_slice_in_dim(own, dp_at * share, share, 0)
+        gathered = lax.all_gather(mine, ("dp", "mp"), axis=0).reshape(n_dp, n_mp, share, dim)
+        gathered = gathered.transpose(1, 0, 2, 3).reshape(n_mp, n_dp * share, dim)
+        heads, qkv, lse, h1 = attn_fwd(me, latents, mod, gathered, b_qkv, n_mp)
+    heads_own = lax.dynamic_index_in_dim(heads, mp_at, 0, keepdims=False)
+    rows = min(256, seq)
+    results, dqkv, dh1 = [], [], []
+    for i in range(lat):
+        waiting = dqkv and direct
+        outs = mlp_both(
+            i,
+            heads,
+            latents,
+            cotangent,
+            mod,
+            own,
+            gathered,
+            proj_bias.astype(F32)[None],
+            b_fc1,
+            fc2_bias.astype(F32)[None],
+            n_mp,
+            rows,
+            dh1_i if waiting else None,
+        )
+        if waiting:
+            dh1.append(outs[-1])
+        results.append(outs[:8])
+        dqkv_i, dh1_i = attn_bwd(
+            outs[2], heads_own, qkv, lse, proj_weight, wq_own, i, min(512, seq)
+        )
+        dqkv.append(dqkv_i)
+        if not direct:
+            dh1.append(lax.psum(dh1_i, "mp"))
+    if direct:
+        dh1.append(line_sum(dh1_i))
+    dqkv = jnp.concatenate(dqkv, 0)
+    block_out, dx1, da, h2, dm, z, du, stats_two = [
+        jnp.concatenate(parts, 0) for parts in zip(*results)
+    ]
     flat = lambda v: v.reshape(lat * seq, v.shape[-1])
     grad_fc2 = tn(flat(z), flat(dm)).astype(BF)
     grad_fc1 = tn(flat(h2), flat(du)).astype(BF)
@@ -436,26 +945,19 @@
     grad_fc2_bias = jnp.sum(gate_two * stats_two[:, 4], 0)
     grad_proj_bias = jnp.sum(gate_one * stats_two[:, 5], 0)
     grad_fc1, grad_fc2 = lax.psum((grad_fc1, grad_fc2), "dp")
-
-    heads_own = lax.dynamic_index_in_dim(heads, mp_at, 0, keepdims=False)
-    dqkv, dh1 = [], []
-    for i in range(lat):
-        dqkv_i, dh1_i = attn_bwd(da, heads_own, qkv, lse, proj_weight, wq_own, i, min(512, seq))
-        dqkv.append(dqkv_i)
-        dh1.append(lax.psum(dh1_i, "mp"))
-    dqkv = jnp.concatenate(dqkv, 0)
-    dh1 = jnp.concatenate(dh1, 0)
     grad_qkv = jnp.einsum("les,lsd->ed", dqkv, h1, preferred_element_type=F32).astype(BF)
     grad_proj = jnp.einsum("les,lsd->ed", heads_own, da, preferred_element_type=F32).astype(BF)
     bias_sums = jnp.sum(dqkv.astype(F32), (0, 2)).reshape(3, local)
     grad_qv_bias = jnp.stack([bias_sums[0], bias_sums[2]])
     grad_qkv, grad_proj = lax.psum((grad_qkv, grad_proj), "dp")
-    biases = lax.psum(
-        (grad_fc1_bias, grad_fc2_bias, grad_proj_bias, grad_qv_bias), "dp"
-    )
+    biases = lax.psum((grad_fc1_bias, grad_fc2_bias, grad_proj_bias, grad_qv_bias), "dp")
     grad_fc1_bias, grad_fc2_bias, grad_proj_bias, grad_qv_bias = biases
 
-    latents_grad, stats_one = latents_back(dh1, dx1, latents, mod, 256)
+    backs = [
+        latents_back(dh1[i], results[i][1], latents, mod, i, rows) for i in range(lat)
+    ]
+    latents_grad = jnp.concatenate([grad for grad, _ in backs], 0)
+    stats_one = jnp.concatenate([stats for _, stats in backs], 0)
 
     dmod = jnp.stack(
         [

time: 1120 us -> 826 us (0.74)
  waiting for transfers between devices: 496 us -> 0.02 us
  Pallas kernels: 380 us -> 586 us
  blocking collectives: 68.1 us -> 49 us
  other arithmetic: 26.8 us -> 39.6 us
    psum x1 -> x0, waiting for transfers between devices: 242 us -> none  [per_device(): dh1.append(lax.psum(dh1_i, 'mp'))]
    pallas_call x3 -> x9, Pallas kernels: 360 us -> 566 us  [the longest x3 247 us: mlp_both(): pl.pallas_call(functools.partial(mlp_kernel, summing=summing), grid=(seq...]
    all_gather x1 -> x0, waiting for transfers between devices: 166 us -> none  [per_device(): lax.all_gather(mine, ('dp', 'mp'), axis=0).reshape(n_dp, n_mp, share, dim)]
    psum x1, waiting for transfers between devices: 87.5 us -> 0.01 us  [per_device(): grad_qkv, grad_proj = lax.psum((grad_qkv, grad_proj), 'dp')]
    unnamed x46 -> x103, local copies, waits for them, and re-layouts: 8.58 us -> 34.1 us
    reshape x1 -> x0, local copies, waits for them, and re-layouts: 22 us -> none  [per_device(): lax.all_gather(mine, ('dp', 'mp'), axis=0).reshape(n_dp, n_mp, share, dim)]
    all_gather x1 -> x0, blocking collectives: 15.6 us -> none  [per_device(): lax.all_gather(jnp.concatenate([mod_part, bias_row], 0), 'mp', axis=0)]
  transfers between devices with their start and end apart: 3 -> 1, of which waited for: 3 -> 0; matrix products, arithmetic and copies ran while one was open for 2% -> 3% of each run, Pallas kernels for 0% -> 16%
where the time goes in v2:
time: 826 us; the launch traced here: 820 us
  Pallas kernels  586 us (71%)
  local copies, waits for them, and re-layouts  82.1 us (10%)
  blocking collectives  49 us (6%)
  matrix products  48.9 us (6%)
  other arithmetic  39.6 us (5%)
  between operations  14.9 us (2%)
    pallas_call x3, Pallas kernels, mlp_both(): pl.pallas_call(functools.partial(mlp_kernel, summing=summing), grid=(seq...  247 us
    pallas_call x1, Pallas kernels, attn_gather(): pl.pallas_call(attn_gather_kernel, grid=(n_mp, lat), in_specs=[pl.BlockSp...  179 us
    pallas_call x1, Pallas kernels, line_sum(): pl.pallas_call(line_kernel, in_specs=[vmem], out_specs=vmem, out_shape=ja...  118 us
    pallas_call x2, local copies, waits for them, and re-layouts, attn_bwd(): pl.pallas_call(functools.partial(attn_bwd_kernel, rows=rows), grid=(1,),...  37.5 us
    unnamed x103, local copies, waits for them, and re-layouts  34.1 us
    dot_general x3, matrix products, tn(): lax.dot_general(a, b, (((0,), (0,)), ((), ())), preferred_element_type=F32)  29 us
    psum x1, blocking collectives, per_device(): lax.psum((grad_fc1_bias, grad_fc2_bias, grad_proj_bias, grad_qv_bias), 'dp')  24.2 us
    pallas_call x1, Pallas kernels, attn_bwd(): pl.pallas_call(functools.partial(attn_bwd_kernel, rows=rows), grid=(1,),...  19.8 us
  transfers between devices with their start and end apart: 1, of which 0 were waited for; matrix products, arithmetic and copies ran while one was open for 3% of the time, Pallas kernels for 16%

profile of v2, /device:TPU:0, one launch (start us, length us, event | category | flops | bytes accessed | tf_op | source)
XLA Modules:
  0.0 820.5 jit_solution(6634681840355953193)
XLA Ops:
  7.3 6.4 copy.37.w_ref
  16.0 10.3 %modulation.1 = (f32[4,8,1728]{2,1,0:T(8,128)S(1)}, bf16[3,1152]{1,0:T(4,128)(2,1)S(1)}) custom-call(f32[3,1152]{1,0:T(4,128)S(1)} %copy-done.12, bf16[1152,1728]{1,0:T(8,128)(2,1)S(1)} %copy-done.1, f32[1,1728]{1,0:T(1,128)S(1)} %reshape.98.bias_ref, f32[1,1728]{1,0:T(1,128)S(1)} %maximum_convert_fusion.row_ref), custom_call_target="tpu_custom_call" | custom-call | tf_op jit(solution)/shard_map/modulation/pallas_call | solution.py:99
  28.2 2.9 reshape.107.bias_ref
  31.0 5.2 copy.39
  37.4 12.9 %pad_maximum_fusion.refs_4_ = bf16[3456,1152]{1,0:T(8,128)(2,1)} fusion(bf16[1152,1152]{1,0:T(8,128)(2,1)} %param.22, bf16[1152,1152]{1,0:T(8,128)(2,1)} %bitcast.51, bf16[288,1152]{1,0:T(8,128)(2,1)S(1)} %copy-done.18, bf16[864,1152]{1,0:T(8,128)(2,1)S(1)} %bitcast.49), kind=kLoop, calls=%fused_computation.4 | loop fusion | flops 31850496 | bytes 15925248 | tf_op jit(solution)/shard_map/concatenate | solution.py:896
  50.3 179.2 %attn_gather.1 = (bf16[4,3,288,1024]{3,2,1,0:T(8,128)(2,1)}, bf16[3,12,72,1024]{3,2,1,0:T(8,128)(2,1)}, f32[3,4,1024]{2,1,0:T(4,128)}, bf16[3,1024,1152]{2,1,0:T...) custom-call(bf16[3,1024,1152]{2,1,0:T(8,128)(2,1)} %lat_ref.7, f32[3,6,1152]{2,1,0:T(8,128)} %reshape.91.mod_ref.refs_3_, ...), custom_call_target="tpu_custom_call" | custom-call | tf_op jit(solution)/shard_map/attn_gather/pallas_call | solution.py:367
  232.4 77.4 %mlp_both.1 = (bf16[1,1024,1152]{2,1,0:T(8,128)(2,1)}, bf16[1,1024,1152]{2,1,0:T(8,128)(2,1)}, bf16[1,1024,1152]{2,1,0:T(8,128)(2,1)}, bf16[1,1024,1152]{2,1,0:T...) custom-call(bf16[4,3,288,1024]{3,2,1,0:T(8,128)(2,1)} %get-tuple-ele, ...), custom_call_target="tpu_custom_call" | custom-call | tf_op jit(solution)/shard_map/mlp_both/pallas_call | solution.py:673
  309.8 19.8 %attn_bwd.3 = (bf16[1,864,1024]{2,1,0:T(8,128)(2,1)}, bf16[1,1024,1152]{2,1,0:T(8,128)(2,1)}) custom-call(bf16[1,1024,1152]{2,1,0:T(8,128)(2,1)} %get-tuple-element.62.da_ref, bf16[3,288,1024]{2,1,0:T(8,128)(2,1)} %dynamic-slice_bitcast_fusion.heads_ref, bf16[3,12,72,1024]{3,2,1,0:T(8,128)(2,1)} %get-tuple-element.63.qkv_ref, ...), custom_call_target="tpu_custom_call" | custom-call | tf_op jit(solution)/shard_map/attn_bwd/pallas_call | solution.py:789
  329.6 84.0 %mlp_sum.2 = (bf16[1,1024,1152]{2,1,0:T(8,128)(2,1)}, bf16[1,1024,1152]{2,1,0:T(8,128)(2,1)}, bf16[1,1024,1152]{2,1,0:T(8,128)(2,1)}, bf16[1,1024,1152]{2,1,0:T(...) custom-call(bf16[4,3,288,1024]{3,2,1,0:T(8,128)(2,1)} %get-tuple-ele, ...), custom_call_target="tpu_custom_call" | custom-call | tf_op jit(solution)/shard_map/mlp_sum/pallas_call | solution.py:673
  413.6 3.0 constant_dynamic-update-slice_fusion.5
  416.6 19.1 %attn_bwd.5 = (bf16[3,864,1024]{2,1,0:T(8,128)(2,1)}, bf16[1,1024,1152]{2,1,0:T(8,128)(2,1)}) fusion(bf16[3,864,1024]{2,1,0:T(8,128)(2,1)} %constant_dynamic-update-slice_fusion.5, bf16[1,1024,1152]{2,1,0:T(8,128)(2,1)} %get-tuple-element.67, bf16[3,288,1024]{2,1,0:T(8,128)(2,1)} %dynamic-slice_bitcast_fusion.heads_ref, ...), kind=kCustom, calls=%fused_computation.55 | custom fusion | bytes 16269312 | tf_op jit(solution)/shard_map/attn_bwd/pallas_call | solution.py:789
  435.7 85.2 %mlp_sum.3 = (bf16[1,1024,1152]{2,1,0:T(8,128)(2,1)}, bf16[1,1024,1152]{2,1,0:T(8,128)(2,1)}, bf16[1,1024,1152]{2,1,0:T(8,128)(2,1)}, bf16[1,1024,1152]{2,1,0:T(...) custom-call(bf16[4,3,288,1024]{3,2,1,0:T(8,128)(2,1)} %get-tuple-ele, ...), custom_call_target="tpu_custom_call" | custom-call | tf_op jit(solution)/shard_map/mlp_sum/pallas_call | solution.py:673
  520.9 3.4 constant_dynamic-update-slice_fusion.8
  524.3 5.7 fusion.26
  530.0 18.4 %attn_bwd.4 = (bf16[3,864,1024]{2,1,0:T(8,128)(2,1)}, bf16[1,1024,1152]{2,1,0:T(8,128)(2,1)S(1)}) fusion(bf16[3,864,1024]{2,1,0:T(8,128)(2,1)} %get-tuple-element.104, bf16[1,1024,1152]{2,1,0:T(8,128)(2,1)} %get-tuple-element.76, bf16[3,288,1024]{2,1,0:T(8,128)(2,1)} %dynamic-slice_bitcast_fusion.heads_ref, ...), kind=kCustom, calls=%fused_computation.54 | custom fusion | bytes 16269312 | tf_op jit(solution)/shard_map/attn_bwd/pallas_call | solution.py:789
  548.5 3.4 constant_dynamic-update-slice_fusion.7
  553.6 11.4 %bitcast_convert_fusion = bf16[864,1152]{1,0:T(8,128)(2,1)} fusion(bf16[3,864,1024]{2,1,0:T(8,128)(2,1)S(1)} %copy-done.20, bf16[3,1024,1152]{2,1,0:T(8,128)(2,1)} %get-tuple-element.89), kind=kOutput, calls=%fused_computation.30 | convolution fusion | flops 6116290560 | bytes 14376960 | tf_op jit(solution)/shard_map/les,lsd->ed/dot_general | solution.py:948
  565.1 12.5 %fusion = bf16[1152,1152]{1,0:T(8,128)(2,1)} fusion(bf16[3,1024,1152]{2,1,0:T(8,128)(2,1)S(1)} %copy-done.17, bf16[1,1024,1152]{2,1,0:T(8,128)(2,1)} %get-tuple-element.92, bf16[1,1024,1152]{2,1,0:T(8,128)(2,1)S(1)} %copy-done.42, bf16[1,1024,1152]{2,1,0:T(8,128)(2,1)S(1)} %copy-done.39), kind=kOutput, calls=%fused_computation.5 | convolution fusion | flops 8162131968 | bytes 16809984 | tf_op jit(solution)/shard_map/dot_general | solution.py:29
  577.6 11.2 %fusion.1 = bf16[1152,1152]{1,0:T(8,128)(2,1)} fusion(bf16[1,1024,1152]{2,1,0:T(8,128)(2,1)S(1)} %copy-done.44, bf16[1,1024,1152]{2,1,0:T(8,128)(2,1)S(1)} %copy-done.41, bf16[1,1024,1152]{2,1,0:T(8,128)(2,1)S(1)} %copy-done.38, bf16[1,1024,1152]{2,1,0:T(8,128)(2,1)S(1)} %copy-done.43, bf16[1,1024,1152]{2,1,0:T(8,128)(2,1)S(1)} %copy-done.40, ...), kind=kOutput, calls=%fused_computation.6 | convolution fusion | flops 8169209856 | bytes 16809984 | tf_op jit(solution)/shard_map/dot_general | solution.py:29
  588.9 3.4 convert_reduce_fusion.1
  593.0 3.7 copy-done
  596.7 3.8 latents_back.3
  605.8 4.1 latents_back.4
  609.9 118.3 %line_sum.1.dh1_ref = bf16[1,1024,1152]{2,1,0:T(8,128)(2,1)S(1)} custom-call(bf16[1,1024,1152]{2,1,0:T(8,128)(2,1)S(1)} %get-tuple-element.109.part_ref), custom_call_target="tpu_custom_call" | custom-call | tf_op jit(solution)/shard_map/line_sum/pallas_call | solution.py:732
  728.3 3.9 latents_back.5
  732.4 9.1 %all-gather = bf16[8,3,2880]{2,1,0:T(4,128)(2,1)S(1)} all-gather(bf16[1,3,2880]{2,1,0:T(4,128)(2,1)S(1)} %maximum_bitcast_fusion), channel_id=1, replica_groups=mesh['dp'=8,'mp'=4] {'dp'}, dimensions={0}, use_global_device_ids=true | all-gather | bytes 155520 | tf_op jit(solution)/shard_map/all_gather | solution.py:975
  741.7 4.0 convert_reduce_fusion
  745.7 24.2 %all-reduce = (f32[2,288]{1,0:T(2,128)}, f32[1152]{0:T(1024)}, f32[1152]{0:T(1024)}, f32[1152]{0:T(1024)}) all-reduce(f32[2,288]{1,0:T(2,128)S(1)} %pad_maximum_fusion.4, f32[1152]{0:T(1024)S(1)} %get-tuple-element.112, f32[1152]{0:T(1024)S(1)} %convert_reduce_fusion, ...), channel_id=1, replica_groups=mesh['dp'=8,'mp'=4] {'dp'}, use_global_device_ids=true, to_apply=%region_3.4 | all-reduce | flops 4032 | bytes 32256 | tf_op jit(solution)/shard_map/psum | solution.py:953
  772.6 15.8 %psum.63 = f32[3,1152]{1,0:T(4,128)S(1)} all-reduce(f32[3,1152]{1,0:T(4,128)S(1)} %fusion.54), channel_id=1, replica_groups=mesh['dp'=8,'mp'=4] {'mp'}, use_global_device_ids=true, to_apply=%region_0.1 | all-reduce | flops 3456 | bytes 27648 | tf_op jit(solution)/shard_map/psum | solution.py:978
  789.0 5.3 fusion.32
  795.7 7.0 pad_maximum_fusion.1
  802.7 4.6 convert_element_type.60
  (137 shorter events, 27.1 us)
Async XLA Ops:
  7.2 6.5 copy-start.32
  7.2 6.5 copy-start.36
  7.2 6.5 copy-start.35
  7.2 6.6 copy-start.12
  7.2 795.5 %all-reduce.4.cloned.1.call-start = ((), (), s32[]{:S(2)}) async-start(), calls=%async_computation | async-start | bytes 15925248 | tf_op jit(solution)/shard_map/psum | solution.py:952
  26.3 10.0 %copy-start.33 = (bf16[1152]{0:T(1024)(128)(2,1)S(1)}, bf16[1152]{0:T(1024)(128)(2,1)}, u32[]{:S(2)}) copy-start(bf16[1152]{0:T(1024)(128)(2,1)} %param.23) | copy-start | bytes 6916
  26.3 10.6 %copy-start.34 = (bf16[1152]{0:T(1024)(128)(2,1)S(1)}, bf16[1152]{0:T(1024)(128)(2,1)}, u32[]{:S(2)}) copy-start(bf16[1152]{0:T(1024)(128)(2,1)} %param.19) | copy-start | bytes 6916
  26.3 11.2 %copy-start.14 = (bf16[1152,3,288]{0,2,1:T(8,128)(2,1)S(1)}, bf16[1152,3,288]{0,2,1:T(8,128)(2,1)}, u32[]{:S(2)}) copy-start(bf16[1152,3,288]{0,2,1:T(8,128)(2,1)} %param.16) | copy-start | bytes 5971972
  26.3 11.1 %copy-start.18 = (bf16[288,1152]{1,0:T(8,128)(2,1)S(1)}, bf16[288,1152]{1,0:T(8,128)(2,1)}, u32[]{:S(2)}) copy-start(bf16[288,1152]{1,0:T(8,128)(2,1)} %wp_ref.3) | copy-start | bytes 1990660
  329.6 87.0 %copy-start.28 = (f32[3,4,1024]{2,1,0:T(4,128)S(1)}, f32[3,4,1024]{2,1,0:T(4,128)}, u32[]{:S(2)}) copy-start(f32[3,4,1024]{2,1,0:T(4,128)} %get-tuple-element.64.lse_ref) | copy-start | bytes 147460
  548.4 5.2 copy-start.20
  553.6 11.4 %copy-start.17 = (bf16[3,1024,1152]{2,1,0:T(8,128)(2,1)S(1)}, bf16[3,1024,1152]{2,1,0:T(8,128)(2,1)}, u32[]{:S(2)}) copy-start(bf16[3,1024,1152]{2,1,0:T(8,128)(2,1)} %constant_dynamic-update-slice_fusion.6) | copy-start | bytes 21233668
  553.6 11.4 %copy-start.39 = (bf16[1,1024,1152]{2,1,0:T(8,128)(2,1)S(1)}, bf16[1,1024,1152]{2,1,0:T(8,128)(2,1)}, u32[]{:S(2)}) copy-start(bf16[1,1024,1152]{2,1,0:T(8,128)(2,1)} %get-tuple-element.90) | copy-start | bytes 7077892
  553.6 11.4 %copy-start.42 = (bf16[1,1024,1152]{2,1,0:T(8,128)(2,1)S(1)}, bf16[1,1024,1152]{2,1,0:T(8,128)(2,1)}, u32[]{:S(2)}) copy-start(bf16[1,1024,1152]{2,1,0:T(8,128)(2,1)} %get-tuple-element.91) | copy-start | bytes 7077892
  565.0 12.5 %copy-start.37 = (bf16[1,1024,1152]{2,1,0:T(8,128)(2,1)S(1)}, bf16[1,1024,1152]{2,1,0:T(8,128)(2,1)}, u32[]{:S(2)}) copy-start(bf16[1,1024,1152]{2,1,0:T(8,128)(2,1)} %get-tuple-element.99) | copy-start | bytes 7077892
  565.1 12.5 %copy-start.38 = (bf16[1,1024,1152]{2,1,0:T(8,128)(2,1)S(1)}, bf16[1,1024,1152]{2,1,0:T(8,128)(2,1)}, u32[]{:S(2)}) copy-start(bf16[1,1024,1152]{2,1,0:T(8,128)(2,1)} %get-tuple-element.96) | copy-start | bytes 7077892
  565.1 12.5 %copy-start.40 = (bf16[1,1024,1152]{2,1,0:T(8,128)(2,1)S(1)}, bf16[1,1024,1152]{2,1,0:T(8,128)(2,1)}, u32[]{:S(2)}) copy-start(bf16[1,1024,1152]{2,1,0:T(8,128)(2,1)} %get-tuple-element.100) | copy-start | bytes 7077892
  565.1 12.5 %copy-start.41 = (bf16[1,1024,1152]{2,1,0:T(8,128)(2,1)S(1)}, bf16[1,1024,1152]{2,1,0:T(8,128)(2,1)}, u32[]{:S(2)}) copy-start(bf16[1,1024,1152]{2,1,0:T(8,128)(2,1)} %get-tuple-element.97) | copy-start | bytes 7077892
  565.1 12.5 %copy-start.43 = (bf16[1,1024,1152]{2,1,0:T(8,128)(2,1)S(1)}, bf16[1,1024,1152]{2,1,0:T(8,128)(2,1)}, u32[]{:S(2)}) copy-start(bf16[1,1024,1152]{2,1,0:T(8,128)(2,1)} %get-tuple-element.101) | copy-start | bytes 7077892
  565.1 12.5 %copy-start.44 = (bf16[1,1024,1152]{2,1,0:T(8,128)(2,1)S(1)}, bf16[1,1024,1152]{2,1,0:T(8,128)(2,1)}, u32[]{:S(2)}) copy-start(bf16[1,1024,1152]{2,1,0:T(8,128)(2,1)} %get-tuple-element.98) | copy-start | bytes 7077892
  588.9 4.0 copy-start.9
  593.0 3.7 copy-start
  602.0 126.3 %slice-start = ((s8[7077888]{0:T(1024)(128)(4,1)}), s8[4194304]{0:T(1024)(128)(4,1)S(1)}, s32[]{:S(2)}) async-start(s8[7077888]{0:T(1024)(128)(4,1)} %bitcast.41), calls=%async_computation.1 | async-start | bytes 8388608
  605.8 122.5 %slice-start.1 = ((s8[7077888]{0:T(1024)(128)(4,1)}), s8[2883584]{0:T(1024)(128)(4,1)S(1)}, s32[]{:S(2)}) async-start(s8[7077888]{0:T(1024)(128)(4,1)} %bitcast.41), calls=%async_computation.2 | async-start | bytes 5767168
  609.9 118.4 %copy-start.5 = (bf16[1,1024,1152]{2,1,0:T(8,128)(2,1)}, bf16[1,1024,1152]{2,1,0:T(8,128)(2,1)S(1)}, u32[]{:S(2)}) copy-start(bf16[1,1024,1152]{2,1,0:T(8,128)(2,1)S(1)} %get-tuple-element.75) | copy-start | bytes 7077892
  609.9 118.4 %copy-start.10 = (bf16[1,1024,1152]{2,1,0:T(8,128)(2,1)S(1)}, bf16[1,1024,1152]{2,1,0:T(8,128)(2,1)}, u32[]{:S(2)}) copy-start(bf16[1,1024,1152]{2,1,0:T(8,128)(2,1)} %get-tuple-element.78.dx1_ref) | copy-start | bytes 7077892
  789.0 5.3 copy-start.13
  789.0 5.9 copy-start.4
  789.0 5.9 copy-start.6
  789.0 5.9 copy-start.22
  789.0 6.7 copy-start.23
  802.7 4.6 copy-start.21
  (16 other events, 46.6 us)
Sparse Core Ops, SparseCore 0:
  589.0 122.7 all-reduce.3

commit v3 on v2

--- a/solution.py
+++ b/solution.py
@@ -165,7 +165,10 @@
     lat_ref,
     mod_ref,
     bias_ref,
-    own_ref,
+    wq_ref,
+    wp_ref,
+    w1_ref,
+    w2_ref,
     heads_ref,
     qkv_ref,
     lse_ref,
@@ -187,7 +190,8 @@
     step = slot * lats + lat
     dp_at, me = lax.axis_index("dp"), lax.axis_index("mp")
     core, x, y = dp_at % 2, dp_at // 2 % 2, dp_at // 4
-    rows = own_ref.shape[4]
+    rows = all_ref.shape[5]
+    upper = wq_ref.shape[0] // rows
     cut = rows // 32 * 16 + 16
     near, far = pl.ds(0, cut), pl.ds(cut, rows - cut)
     every = pl.ds(0, rows)
@@ -200,10 +204,11 @@
     def piece(s, c, at_y, at_x, at_core, part):
         return all_ref.at[s, c, at_y, at_x, at_core, part]
 
-    def own_copy(c, side, target):
+    def own_copy(c, side, target, source=None):
+        ref = piece(me, c, y, x, core, every)
         return pltpu.make_async_remote_copy(
-            own_ref.at[c, y, x, core],
-            piece(me, c, y, x, core, every),
+            ref if source is None else source,
+            ref,
             z_own.at[side, c],
             z_got.at[c, me],
             **target,
@@ -262,14 +267,23 @@
             if stage == 4:
                 move(4, c, s, True).wait_recv()
 
-    def send_own(c):
+    def send_from(c, ref, at):
+        source = ref.at[pl.ds(at * rows, rows)]
+
         @pl.when(me < n_mp - 1)
         def _():
-            own_copy(c, 0, right_id).start()
+            own_copy(c, 0, right_id, source).start()
 
         @pl.when(me > 0)
         def _():
-            own_copy(c, 1, left_id).start()
+            own_copy(c, 1, left_id, source).start()
+
+    def send_own(c):
+        if c > 0:
+            send_from(c, (w1_ref, w2_ref)[c - 1], dp_at)
+        else:
+            pl.when(dp_at < upper)(lambda: send_from(0, wq_ref, dp_at))
+            pl.when(dp_at >= upper)(lambda: send_from(0, wp_ref, dp_at - upper))
 
     @pl.when(step == 0)
     def _():
@@ -299,9 +313,17 @@
 
     @pl.when((lat == 0) & (slot == 0))
     def _():
-        load = pltpu.make_async_copy(own_ref.at[0], w_buf, local_sem.at[0])
-        load.start()
-        load.wait()
+        def load(at):
+            return pltpu.make_async_copy(
+                wq_ref.at[pl.ds(at * rows, rows)],
+                w_buf.at[at // 4, at // 2 % 2, at % 2],
+                local_sem.at[at],
+            )
+
+        for at in range(upper):
+            load(at).start()
+        for at in range(upper):
+            load(at).wait()
 
     @pl.when((lat == 0) & (slot > 0))
     def _():
@@ -359,8 +381,7 @@
     lat, seq, dim = latents.shape
     local = dim // n_mp
     n_heads = local // HEAD_DIM
-    rows = own.shape[0] // 24
-    own = own.reshape(3, 2, 2, 2, rows, dim)
+    rows = dim // 8
     last = lat - 1
     first = lambda s, l: s // n_mp * 0 + jnp.where(s == 0, l, last)
     part = lambda s: other_part(lax.axis_index("mp"), s)
@@ -371,8 +392,8 @@
             pl.BlockSpec((1, seq, dim), lambda s, l: (first(s, l), 0, 0)),
             pl.BlockSpec((1, 6, dim), lambda s, l: (l, 0, 0)),
             pl.BlockSpec((1, 3 * local, 1), lambda s, l: (part(s), 0, 0)),
-            pl.BlockSpec(memory_space=pl.ANY),
-        ],
+        ]
+        + [pl.BlockSpec(memory_space=pl.ANY)] * 4,
         out_specs=[
             pl.BlockSpec((1, 1, local, seq), lambda s, l: (part(s), l, 0, 0)),
             pl.BlockSpec((1, 3 * n_heads, HEAD_DIM, seq), lambda s, l: (first(s, l), 0, 0, 0)),
@@ -390,7 +411,7 @@
         scratch_shapes=[
             pltpu.VMEM((lat, seq, dim), BF),
             pltpu.VMEM((2, 2, 2, rows, dim), BF),
-            pltpu.SemaphoreType.DMA((1,)),
+            pltpu.SemaphoreType.DMA((8,)),
             pltpu.SemaphoreType.DMA((2, 3)),
             pltpu.SemaphoreType.DMA((3, n_mp)),
             pltpu.SemaphoreType.DMA((3, n_mp)),
@@ -401,8 +422,8 @@
             collective_id=1, has_side_effects=True, vmem_limit_bytes=60 * MIB
         ),
         name="attn_gather",
-    )(latents, mod, bias, own)
-    return heads, qkv, lse, h1, gathered.reshape(n_mp, 24 * rows, dim)
+    )(latents, mod, bias, *own)
+    return heads, qkv, lse, h1, gathered.reshape(n_mp, 3, dim, dim)
 
 
 def attn_fwd(me, latents, mod, gathered, bias, n_mp):
@@ -464,11 +485,14 @@
         def _():
             action()
 
-    def barrier(self):
+    def greet(self):
         sem = pltpu.get_barrier_semaphore()
         for side in (0, 1):
             self.guarded(side, False, lambda: pl.semaphore_signal(sem, inc=1, **self.ends[side]))
-        pl.semaphore_wait(sem, line_peers(self.me, self.n))
+
+    def barrier(self):
+        self.greet()
+        pl.semaphore_wait(pltpu.get_barrier_semaphore(), line_peers(self.me, self.n))
 
     def copy(self, side, c):
         ref = (self.up, self.down)[side].at[c]
@@ -527,8 +551,8 @@
 
 
 def mlp_kernel(*refs, summing):
-    heads_ref, lat_ref, cot_ref, mod_ref, own_ref, all_ref, bp_ref, b1_ref, b2_ref = refs[:9]
-    refs = refs[9:]
+    heads_ref, lat_ref, cot_ref, mod_ref, bp_ref, b1_ref, b2_ref = refs[:7]
+    own_refs, (wq_all, w1_all, w2_all), refs = refs[7:10], refs[10:13], refs[13:]
     if summing:
         part_ref, refs = refs[0], refs[1:]
     out_ref, dx1_ref, da_ref, h2_ref, dm_ref, z_ref, du_ref, stats_ref = refs[:8]
@@ -536,7 +560,7 @@
     if summing:
         sum_ref, refs = refs[0], refs[1:]
     macc, dacc, wp, w1, w2, load_sems = refs[:6]
-    n_mp, hid, dim = w1.shape
+    n_mp, hid, dim = w2.shape
     local = wp.shape[1]
     rows = lat_ref.shape[1]
     me = lax.axis_index("mp")
@@ -544,13 +568,15 @@
     line = LineSum(part_ref, refs[6], refs[7], refs[8], sum_ref) if summing else None
 
     def load(kind, k):
-        at = own_ref if k == 0 else all_ref.at[(me + k) % n_mp]
-        first, count, ref = (
-            (3 * local, local, wp.at[(me + k) % n_mp]),
-            (4 * local, hid, w1.at[k]),
-            (4 * local + hid, hid, w2.at[k]),
-        )[kind]
-        return pltpu.make_async_copy(at.at[pl.ds(first, count)], ref, load_sems.at[kind, k])
+        slot = (me + k) % n_mp
+        source = own_refs[kind]
+        if k > 0:
+            stack = (wq_all, w1_all, w2_all)[kind]
+            source = stack.at[slot, kind] if len(stack.shape) == 4 else stack.at[slot]
+        if k > 0 and kind == 0:
+            source = source.at[pl.ds(3 * local, local)]
+        ref = (wp.at[slot], w1.at[k], w2.at[k])[kind]
+        return pltpu.make_async_copy(source, ref, load_sems.at[kind, k])
 
     @pl.when(step == 0)
     def _():
@@ -589,7 +615,7 @@
                 ref = (w1, w2)[kind - 1].at[k]
                 pltpu.make_async_copy(ref, ref, load_sems.at[kind, k]).wait()
 
-        u = nt(h2_ref[0], w1[k]) + b1_ref[(me + k) % n_mp]
+        u = mm(h2_ref[0], w1[k]) + b1_ref[(me + k) % n_mp]
         dz = nt(dm_ref[0], w2[k])
         u2 = u * u
         t = jnp.tanh(u * (GELU_A + (GELU_A * GELU_B) * u2))
@@ -601,7 +627,7 @@
             z_ref[0] = z
             du_ref[0] = du
         macc[...] += mm(z, w2[k])
-        dacc[...] += mm(du, w1[k])
+        dacc[...] += nt(du, w1[k])
 
     part(0, True)
 
@@ -657,10 +683,10 @@
     ]
 
 
-def mlp_both(index, heads, latents, cotangent, mod, own, gathered, bp, b1, b2, n_mp, rows, part):
+def mlp_both(index, heads, latents, cotangent, mod, biases, own, gathered, n_mp, rows, part):
     lat, seq, dim = latents.shape
     local = dim // n_mp
-    hid = b1.shape[2]
+    hid = biases[1].shape[2]
     tok = pl.BlockSpec((1, rows, dim), lambda t: (index, t, 0))
     new = pl.BlockSpec((1, rows, dim), lambda t: (0, t, 0))
     hidden = pl.BlockSpec((1, rows, hid), lambda t: (0, t, 0))
@@ -678,12 +704,11 @@
             tok,
             tok,
             pl.BlockSpec((1, 6, dim), lambda t: (index, 0, 0)),
-            any_spec,
-            any_spec,
             once((1, dim)),
             once((n_mp, 1, hid)),
             once((1, dim)),
         ]
+        + [any_spec] * 6
         + extra,
         out_specs=[new] * 5
         + [hidden, hidden, pl.BlockSpec((1, 8, dim), lambda t: (0, 0, 0))]
@@ -696,14 +721,14 @@
             pltpu.VMEM((rows, dim), F32),
             pltpu.VMEM((rows, dim), F32),
             pltpu.VMEM((n_mp, local, dim), BF),
-            pltpu.VMEM((n_mp, hid, dim), BF),
+            pltpu.VMEM((n_mp, dim, hid), BF),
             pltpu.VMEM((n_mp, hid, dim), BF),
             pltpu.SemaphoreType.DMA((3, n_mp)),
         ]
         + (line_scratch(seq, dim) if summing else []),
         compiler_params=pltpu.CompilerParams(
             vmem_limit_bytes=63 * MIB,
-            **(dict(collective_id=3 + index, has_side_effects=True) if summing else {}),
+            **(dict(collective_id=4 + index, has_side_effects=True) if summing else {}),
         ),
         name="mlp_sum" if summing else "mlp_both",
     )(
@@ -711,35 +736,214 @@
         latents,
         cotangent,
         mod,
-        own,
-        gathered,
-        bp,
-        b1,
-        b2,
+        *biases,
+        *own,
+        *gathered,
         *([part] if summing else []),
     )
 
 
-def line_kernel(part_ref, sum_ref, up, down, sems):
-    line = LineSum(part_ref, up, down, sems, sum_ref)
-    line.barrier()
-    line.finish(0)
-
-
-def line_sum(part):
+class CubeSum:
+    def __init__(self, terms, full, halves, firsts, seconds, sems):
+        self.terms, self.full = terms, full
+        self.halves, self.firsts, self.seconds, self.sems = halves, firsts, seconds, sems
+        self.units = terms.shape[0]
+        dp_at, me = lax.axis_index("dp"), lax.axis_index("mp")
+        self.core, x, y = dp_at % 2, dp_at // 2 % 2, dp_at // 4
+        self.core_id = at_mesh(flip(dp_at, 0), me)
+        x_id, y_id = at_mesh(flip(dp_at, 1), me), at_mesh(flip(dp_at, 2), me)
+        self.ids = ((x_id, y_id), (y_id, x_id))
+        self.place = ((x, y), (y, x))
+
+    def barrier(self):
+        sem = pltpu.get_barrier_semaphore()
+        for target in (self.core_id,) + self.ids[0]:
+            pl.semaphore_signal(sem, inc=1, **target)
+
+    def send(self, stage, u, q, arrived=False):
+        core = self.core
+        terms, full = self.terms, self.full
+        first, second = self.place[q]
+        if stage == 0:
+            pair, target = (terms.at[u, 1 - core], self.halves.at[u]), self.core_id
+        elif stage == 1:
+            pair = (terms.at[u, core, q, 1 - first], self.firsts.at[u, q])
+            target = self.ids[q][0]
+        elif stage == 2:
+            pair = (terms.at[u, core, q, first, 1 - second], self.seconds.at[u, q])
+            target = self.ids[q][1]
+        elif stage == 3:
+            at = 1 - second if arrived else second
+            pair = (full.at[u, core, q, first, at],) * 2
+            target = self.ids[q][1]
+        elif stage == 4:
+            at = 1 - first if arrived else first
+            pair = (full.at[u, core, q, at],) * 2
+            target = self.ids[q][0]
+        else:
+            at = 1 - core if arrived else core
+            pair, target = (full.at[u, at],) * 2, self.core_id
+        return pltpu.make_async_remote_copy(
+            *pair, self.sems.at[0, stage, q, u], self.sems.at[1, stage, q, u], **target
+        )
+
+    def quarters(self, stage):
+        return (0,) if stage in (0, 5) else (0, 1)
+
+    def event(self, stage, u):
+        terms, core = self.terms, self.core
+
+        @pl.when((u >= 0) & (u < self.units))
+        def _():
+            if stage > 0:
+                for q in self.quarters(stage - 1):
+                    self.send(stage - 1, u, q, True).wait_recv()
+            if stage == 1:
+                total = terms[u, core].astype(F32) + self.halves[u].astype(F32)
+                terms[u, core] = total.astype(BF)
+            for q in (0, 1):
+                first, second = self.place[q]
+                if stage == 2:
+                    total = terms[u, core, q, first].astype(F32) + self.firsts[u, q].astype(F32)
+                    terms[u, core, q, first] = total.astype(BF)
+                if stage == 3:
+                    total = terms[u, core, q, first, second].astype(F32)
+                    total = total + self.seconds[u, q].astype(F32)
+                    self.full[u, core, q, first, second] = total.astype(BF)
+            if stage < 6:
+                for q in self.quarters(stage):
+                    self.send(stage, u, q).start()
+
+    def finish(self):
+        def sent(u, carry):
+            for stage in range(6):
+                for q in self.quarters(stage):
+                    self.send(stage, u, q).wait_send()
+            return carry
+
+        lax.fori_loop(0, self.units, sent, 0)
+
+
+def tail_kernel(
+    part_ref, terms_ref, sum_ref, full_ref, up, down, line_sems, terms, full, *refs
+):
+    halves, firsts, seconds, cube_sems, local_sem = refs
+    line = LineSum(part_ref, up, down, line_sems, sum_ref)
+    cube = CubeSum(terms, full, halves, firsts, seconds, cube_sems)
+    load = pltpu.make_async_copy(terms_ref, terms, local_sem.at[0])
+    load.start()
+    cube.barrier()
+    line.greet()
+    pl.semaphore_wait(pltpu.get_barrier_semaphore(), 3 + line_peers(line.me, line.n))
+    load.wait()
+    rounds = cube.units + 6
+
+    def advance(t, carry):
+        line.tick(2 * t)
+        for stage in (6, 5, 4, 3):
+            cube.event(stage, t - stage)
+        line.tick(2 * t + 1)
+        for stage in (2, 1, 0):
+            cube.event(stage, t - stage)
+        return carry
+
+    lax.fori_loop(0, rounds, advance, 0)
+    store = pltpu.make_async_copy(full, full_ref, local_sem.at[0])
+    store.start()
+    line.finish(2 * rounds)
+    cube.finish()
+    store.wait()
+
+
+def tail_sums(part, terms):
     _, seq, dim = part.shape
+    units, rows, _ = terms.shape
+    rows = rows // 16
+    vmem = pl.BlockSpec(memory_space=pltpu.VMEM)
+    any_spec = pl.BlockSpec(memory_space=pl.ANY)
+    shape = (units, 2, 2, 2, 2, rows, dim)
+    total, full = pl.pallas_call(
+        tail_kernel,
+        in_specs=[vmem, any_spec],
+        out_specs=[vmem, any_spec],
+        out_shape=[jax.ShapeDtypeStruct(part.shape, BF), jax.ShapeDtypeStruct(shape, BF)],
+        scratch_shapes=line_scratch(seq, dim)
+        + [
+            pltpu.VMEM(shape, BF),
+            pltpu.VMEM(shape, BF),
+            pltpu.VMEM((units, 2, 2, 2, rows, dim), BF),
+            pltpu.VMEM((units, 2, 2, rows, dim), BF),
+            pltpu.VMEM((units, 2, rows, dim), BF),
+            pltpu.SemaphoreType.DMA((2, 6, 2, units)),
+            pltpu.SemaphoreType.DMA((1,)),
+        ],
+        compiler_params=pltpu.CompilerParams(
+            collective_id=2, has_side_effects=True, vmem_limit_bytes=60 * MIB
+        ),
+        name="tail_sums",
+    )(part, terms.reshape(shape))
+    return total, full.reshape(units * rows * 16, dim)
+
+
+def rows_kernel(rows_ref, act_ref, every_ref, total_ref, acts, sems):
+    dp_at, me = lax.axis_index("dp"), lax.axis_index("mp")
+    n_dp, n_mp = every_ref.shape[0], acts.shape[0]
+    barrier = pltpu.get_barrier_semaphore()
+    for k in range(1, n_dp):
+        pl.semaphore_signal(barrier, inc=1, **at_mesh((dp_at + k) % n_dp, me))
+    for k in range(1, n_mp):
+        pl.semaphore_signal(barrier, inc=1, **at_mesh(dp_at, (me + k) % n_mp))
+    every_ref[dp_at] = rows_ref[...]
+    acts[me] = act_ref[...]
+    pl.semaphore_wait(barrier, n_dp + n_mp - 2)
+
+    def copy(ref, k, target):
+        return pltpu.make_async_remote_copy(ref, ref, sems.at[0, k], sems.at[1, k], **target)
+
+    def act_copy(k, source):
+        return copy(acts.at[source % n_mp], k - 1, at_mesh(dp_at, (me + k) % n_mp))
+
+    def row_copy(k, source):
+        target = at_mesh((dp_at + k) % n_dp, me)
+        return copy(every_ref.at[source % n_dp], n_mp + k - 2, target)
+
+    for k in range(1, n_mp):
+        act_copy(k, me).start()
+    for k in range(1, n_dp):
+        row_copy(k, dp_at).start()
+    for k in range(1, n_mp):
+        act_copy(k, me + n_mp - k).wait_recv()
+    total = acts[0]
+    for i in range(1, n_mp):
+        total = total + acts[i]
+    total_ref[...] = total
+    for k in range(1, n_dp):
+        row_copy(k, dp_at + n_dp - k).wait_recv()
+    for k in range(1, n_mp):
+        act_copy(k, me).wait_send()
+    for k in range(1, n_dp):
+        row_copy(k, dp_at).wait_send()
+
+
+def rows_exchange(rows, act, n_dp, n_mp):
     vmem = pl.BlockSpec(memory_space=pltpu.VMEM)
     return pl.pallas_call(
-        line_kernel,
-        in_specs=[vmem],
-        out_specs=vmem,
-        out_shape=jax.ShapeDtypeStruct(part.shape, BF),
-        scratch_shapes=line_scratch(seq, dim),
+        rows_kernel,
+        in_specs=[vmem, vmem],
+        out_specs=[vmem, vmem],
+        out_shape=[
+            jax.ShapeDtypeStruct((n_dp,) + rows.shape, rows.dtype),
+            jax.ShapeDtypeStruct(act.shape, act.dtype),
+        ],
+        scratch_shapes=[
+            pltpu.VMEM((n_mp,) + act.shape, act.dtype),
+            pltpu.SemaphoreType.DMA((2, n_dp + n_mp - 2)),
+        ],
         compiler_params=pltpu.CompilerParams(
-            collective_id=2, has_side_effects=True, vmem_limit_bytes=40 * MIB
+            collective_id=3, has_side_effects=True, vmem_limit_bytes=40 * MIB
         ),
-        name="line_sum",
-    )(part)
+        name="rows_exchange",
+    )(rows, act)
 
 
 def attn_bwd_kernel(da_ref, heads_ref, qkv_ref, lse_ref, wp_ref, wq_ref, dqkv_ref, dh1_ref, *, rows):
@@ -893,15 +1097,25 @@
     wq_own = (
         qkv_weight.reshape(dim, 3, n_heads, HEAD_DIM).transpose(1, 2, 3, 0).reshape(3 * local, dim)
     )
-    own = jnp.concatenate([wq_own, proj_weight, fc1_weight.T, fc2_weight], 0)
     if direct:
+        own = (wq_own, proj_weight, fc1_weight, fc2_weight)
         heads, qkv, lse, h1, gathered = attn_gather(latents, mod, b_qkv, own, n_mp)
+        gathered = (gathered,) * 3
     else:
-        share = own.shape[0] // n_dp
-        mine = lax.dynamic_slice_in_dim(own, dp_at * share, share, 0)
-        gathered = lax.all_gather(mine, ("dp", "mp"), axis=0).reshape(n_dp, n_mp, share, dim)
-        gathered = gathered.transpose(1, 0, 2, 3).reshape(n_mp, n_dp * share, dim)
-        heads, qkv, lse, h1 = attn_fwd(me, latents, mod, gathered, b_qkv, n_mp)
+
+        def gather(weight):
+            share = weight.shape[0] // n_dp
+            mine = lax.dynamic_slice_in_dim(weight, dp_at * share, share, 0)
+            whole = lax.all_gather(mine, ("dp", "mp"), axis=0)
+            whole = whole.reshape(n_dp, n_mp, share, weight.shape[1]).transpose(1, 0, 2, 3)
+            return whole.reshape(n_mp, weight.shape[0], weight.shape[1])
+
+        gathered = (
+            gather(jnp.concatenate([wq_own, proj_weight], 0)),
+            gather(fc1_weight),
+            gather(fc2_weight),
+        )
+        heads, qkv, lse, h1 = attn_fwd(me, latents, mod, gathered[0], b_qkv, n_mp)
     heads_own = lax.dynamic_index_in_dim(heads, mp_at, 0, keepdims=False)
     rows = min(256, seq)
     results, dqkv, dh1 = [], [], []
@@ -913,11 +1127,9 @@
             latents,
             cotangent,
             mod,
-            own,
+            (proj_bias.astype(F32)[None], b_fc1, fc2_bias.astype(F32)[None]),
+            (proj_weight, fc1_weight, fc2_weight),
             gathered,
-            proj_bias.astype(F32)[None],
-            b_fc1,
-            fc2_bias.astype(F32)[None],
             n_mp,
             rows,
             dh1_i if waiting else None,
@@ -931,8 +1143,6 @@
         dqkv.append(dqkv_i)
         if not direct:
             dh1.append(lax.psum(dh1_i, "mp"))
-    if direct:
-        dh1.append(line_sum(dh1_i))
     dqkv = jnp.concatenate(dqkv, 0)
     block_out, dx1, da, h2, dm, z, du, stats_two = [
         jnp.concatenate(parts, 0) for parts in zip(*results)
@@ -944,14 +1154,35 @@
     gate_one, gate_two = mod[:, 2], mod[:, 5]
     grad_fc2_bias = jnp.sum(gate_two * stats_two[:, 4], 0)
     grad_proj_bias = jnp.sum(gate_one * stats_two[:, 5], 0)
-    grad_fc1, grad_fc2 = lax.psum((grad_fc1, grad_fc2), "dp")
     grad_qkv = jnp.einsum("les,lsd->ed", dqkv, h1, preferred_element_type=F32).astype(BF)
     grad_proj = jnp.einsum("les,lsd->ed", heads_own, da, preferred_element_type=F32).astype(BF)
     bias_sums = jnp.sum(dqkv.astype(F32), (0, 2)).reshape(3, local)
     grad_qv_bias = jnp.stack([bias_sums[0], bias_sums[2]])
-    grad_qkv, grad_proj = lax.psum((grad_qkv, grad_proj), "dp")
-    biases = lax.psum((grad_fc1_bias, grad_fc2_bias, grad_proj_bias, grad_qv_bias), "dp")
-    grad_fc1_bias, grad_fc2_bias, grad_proj_bias, grad_qv_bias = biases
+    if direct:
+        bias_rows = jnp.stack(
+            [
+                grad_fc1_bias,
+                grad_fc2_bias,
+                grad_proj_bias,
+                jnp.pad(grad_qv_bias.reshape(-1), (0, dim - 2 * local)),
+            ]
+        ).astype(BF)
+        unit = 512
+        terms = jnp.concatenate([grad_fc1, grad_fc2, grad_qkv, grad_proj, bias_rows], 0)
+        terms = jnp.pad(terms, ((0, -terms.shape[0] % unit), (0, 0))).reshape(-1, unit, dim)
+        dh1_i, sums = tail_sums(dh1_i, terms)
+        dh1.append(dh1_i)
+        grad_fc1, grad_fc2 = sums[:dim], sums[dim : 2 * dim]
+        grad_qkv = sums[2 * dim : 2 * dim + 3 * local]
+        grad_proj = sums[2 * dim + 3 * local : 3 * dim]
+        bias_rows = sums[3 * dim : 3 * dim + 4].astype(F32)
+        grad_fc1_bias, grad_fc2_bias, grad_proj_bias = bias_rows[:3]
+        grad_qv_bias = bias_rows[3, : 2 * local].reshape(2, local)
+    else:
+        grad_fc1, grad_fc2 = lax.psum((grad_fc1, grad_fc2), "dp")
+        grad_qkv, grad_proj = lax.psum((grad_qkv, grad_proj), "dp")
+        biases = lax.psum((grad_fc1_bias, grad_fc2_bias, grad_proj_bias, grad_qv_bias), "dp")
+        grad_fc1_bias, grad_fc2_bias, grad_proj_bias, grad_qv_bias = biases
 
     backs = [
         latents_back(dh1[i], results[i][1], latents, mod, i, rows) for i in range(lat)
@@ -972,10 +1203,18 @@
     )
     dmod = dmod.reshape(lat, 6 * dim).astype(BF)
     dmod_own = lax.dynamic_slice_in_dim(dmod, mp_at * cols, cols, 1)
-    every = lax.all_gather(jnp.concatenate([cond_low, dmod_own], 1), "dp", axis=0, tiled=True)
+    both = jnp.concatenate([cond_low, dmod_own], 1)
+    grad_act = nt(dmod_own, ada_weight)
+    if direct:
+        both = jnp.pad(both, ((0, 16 - lat), (0, 0)))
+        grad_act = jnp.pad(grad_act, ((0, 8 - lat), (0, 0)))
+        every, grad_act = rows_exchange(both, grad_act, n_dp, n_mp)
+        every, grad_act = every.reshape(n_dp * 16, dim + cols), grad_act[:lat]
+    else:
+        every = lax.all_gather(both, "dp", axis=0, tiled=True)
+        grad_act = lax.psum(grad_act, "mp")
     grad_ada = tn(every[:, :dim], every[:, dim:])
     grad_ada_bias = jnp.sum(every[:, dim:].astype(F32), 0)
-    grad_act = lax.psum(nt(dmod_own, ada_weight), "mp")
     condition_grad = jax.vjp(jax.nn.silu, condition)[1](grad_act)[0]
 
     back = lambda v: v.astype(F32)

time: 826 us -> 805 us (0.975)
  blocking collectives: 49 us -> 0 us
  Pallas kernels: 586 us -> 626 us
  between operations: 14.9 us -> 1.67 us
  other arithmetic: 39.6 us -> 27.7 us
    psum x2 -> x0, blocking collectives: 39.9 us -> none  [the longest x1 24.2 us: per_device(): lax.psum((grad_fc1_bias, grad_fc2_bias, grad_proj_bias, grad_qv_bias), 'dp')]
    pallas_call x1 -> x3, Pallas kernels: 19.8 us -> 59.4 us  [attn_bwd(): pl.pallas_call(functools.partial(attn_bwd_kernel, rows=rows), grid=(1,),...]
    pallas_call x2 -> x0, local copies, waits for them, and re-layouts: 37.5 us -> none  [attn_bwd(): pl.pallas_call(functools.partial(attn_bwd_kernel, rows=rows), grid=(1,),...]
    concatenate x0 -> x1, local copies, waits for them, and re-layouts: none -> 36.2 us  [per_device(): jnp.concatenate([grad_fc1, grad_fc2, grad_qkv, grad_proj, bias_rows], 0)]
    concatenate x1, other arithmetic: 12.9 us -> 0.02 us  [per_device(): both = jnp.concatenate([cond_low, dmod_own], 1)]
    all_gather x1 -> x0, blocking collectives: 9.11 us -> none  [per_device(): lax.all_gather(jnp.concatenate([cond_low, dmod_own], 1), 'dp', axis=0, ti...]
    pallas_call x1 -> x2, Pallas kernels: 118 us -> 114 us  [the longest x1 101 us: tail_sums(): pl.pallas_call(tail_kernel, in_specs=[vmem, any_spec], out_specs=[vmem, a...]
    unnamed x103 -> x86, local copies, waits for them, and re-layouts: 34.1 us -> 31.1 us
  transfers between devices with their start and end apart: 1 -> 0, of which waited for: 0 -> 0; matrix products, arithmetic and copies ran while one was open for 3% -> 0% of each run, Pallas kernels for 16% -> 0%
where the time goes in v3:
time: 805 us; the launch traced here: 794 us
  Pallas kernels  626 us (78%)
  local copies, waits for them, and re-layouts  84.9 us (11%)
  matrix products  53.8 us (7%)
  other arithmetic  27.7 us (3%)
    pallas_call x3, Pallas kernels, mlp_both(): pl.pallas_call(functools.partial(mlp_kernel, summing=summing), grid=(seq...  251 us
    pallas_call x1, Pallas kernels, attn_gather(): pl.pallas_call(attn_gather_kernel, grid=(n_mp, lat), in_specs=[pl.BlockSp...  179 us
    pallas_call x1, Pallas kernels, tail_sums(): pl.pallas_call(tail_kernel, in_specs=[vmem, any_spec], out_specs=[vmem, a...  101 us
    pallas_call x3, Pallas kernels, attn_bwd(): pl.pallas_call(functools.partial(attn_bwd_kernel, rows=rows), grid=(1,),...  59.4 us
    concatenate x1, local copies, waits for them, and re-layouts, per_device(): jnp.concatenate([grad_fc1, grad_fc2, grad_qkv, grad_proj, bias_rows], 0)  36.2 us
    dot_general x3, matrix products, tn(): lax.dot_general(a, b, (((0,), (0,)), ((), ())), preferred_element_type=F32)  33.3 us
    unnamed x86, local copies, waits for them, and re-layouts  31.1 us

profile of v3, /device:TPU:0, one launch (start us, length us, event | category | flops | bytes accessed | tf_op | source)
XLA Modules:
  0.0 793.7 jit_solution(1915133285701040427)
XLA Ops:
  0.7 6.4 copy.30.w_ref
  7.3 2.2 copy-done.3
  9.4 10.3 %modulation.1 = (f32[4,8,1728]{2,1,0:T(8,128)S(1)}, bf16[3,1152]{1,0:T(4,128)(2,1)S(1)}) custom-call(f32[3,1152]{1,0:T(4,128)S(1)} %copy-done.16, bf16[1152,1728]{1,0:T(8,128)(2,1)S(1)} %copy-done.3, f32[1,1728]{1,0:T(1,128)S(1)} %reshape.109.bias_ref, f32[1,1728]{1,0:T(1,128)S(1)} %maximum_convert_fusion.row_ref), custom_call_target="tpu_custom_call" | custom-call | tf_op jit(solution)/shard_map/modulation/pallas_call | solution.py:99
  20.8 2.9 reshape.117.bias_ref
  23.7 178.9 %attn_gather.1 = (bf16[4,3,288,1024]{3,2,1,0:T(8,128)(2,1)}, bf16[3,12,72,1024]{3,2,1,0:T(8,128)(2,1)}, f32[3,4,1024]{2,1,0:T(4,128)}, bf16[3,1024,1152]{2,1,0:T...) custom-call(bf16[3,1024,1152]{2,1,0:T(8,128)(2,1)} %lat_ref.7, f32[3,6,1152]{2,1,0:T(8,128)} %reshape.100.mod_ref.refs_3_, ...), custom_call_target="tpu_custom_call" | custom-call | tf_op jit(solution)/shard_map/attn_gather/pallas_call | solution.py:388
  204.5 79.3 %mlp_both.1 = (bf16[1,1024,1152]{2,1,0:T(8,128)(2,1)}, bf16[1,1024,1152]{2,1,0:T(8,128)(2,1)}, bf16[1,1024,1152]{2,1,0:T(8,128)(2,1)}, bf16[1,1024,1152]{2,1,0:T...) custom-call(bf16[4,3,288,1024]{3,2,1,0:T(8,128)(2,1)} %get-tuple-ele, ...), custom_call_target="tpu_custom_call" | custom-call | tf_op jit(solution)/shard_map/mlp_both/pallas_call | solution.py:699
  283.8 2.8 dynamic-slice_bitcast_fusion.heads_ref
  286.6 19.7 %attn_bwd.3 = (bf16[1,864,1024]{2,1,0:T(8,128)(2,1)}, bf16[1,1024,1152]{2,1,0:T(8,128)(2,1)}) custom-call(bf16[1,1024,1152]{2,1,0:T(8,128)(2,1)} %get-tuple-element.66.da_ref, bf16[3,288,1024]{2,1,0:T(8,128)(2,1)} %dynamic-slice_bitcast_fusion.heads_ref, bf16[3,12,72,1024]{3,2,1,0:T(8,128)(2,1)} %get-tuple-element.67.qkv_ref, ...), custom_call_target="tpu_custom_call" | custom-call | tf_op jit(solution)/shard_map/attn_bwd/pallas_call | solution.py:993
  306.3 85.0 %mlp_sum.2 = (bf16[1,1024,1152]{2,1,0:T(8,128)(2,1)}, bf16[1,1024,1152]{2,1,0:T(8,128)(2,1)}, bf16[1,1024,1152]{2,1,0:T(8,128)(2,1)}, bf16[1,1024,1152]{2,1,0:T(...) custom-call(bf16[4,3,288,1024]{3,2,1,0:T(8,128)(2,1)} %get-tuple-ele, ...), custom_call_target="tpu_custom_call" | custom-call | tf_op jit(solution)/shard_map/mlp_sum/pallas_call | solution.py:699
  391.3 3.0 copy-done
  397.7 4.3 latents_back.3
  403.3 19.8 %attn_bwd.4 = (bf16[1,864,1024]{2,1,0:T(8,128)(2,1)}, bf16[1,1024,1152]{2,1,0:T(8,128)(2,1)}) custom-call(bf16[1,1024,1152]{2,1,0:T(8,128)(2,1)} %get-tuple-element.71.da_ref, bf16[3,288,1024]{2,1,0:T(8,128)(2,1)} %dynamic-slice_bitcast_fusion.heads_ref, bf16[3,12,72,1024]{3,2,1,0:T(8,128)(2,1)} %get-tuple-element.67.qkv_ref, ...), custom_call_target="tpu_custom_call" | custom-call | tf_op jit(solution)/shard_map/attn_bwd/pallas_call | solution.py:993
  423.1 86.9 %mlp_sum.3 = (bf16[1,1024,1152]{2,1,0:T(8,128)(2,1)}, bf16[1,1024,1152]{2,1,0:T(8,128)(2,1)}, bf16[1,1024,1152]{2,1,0:T(8,128)(2,1)}, bf16[1,1024,1152]{2,1,0:T(...) custom-call(bf16[4,3,288,1024]{3,2,1,0:T(8,128)(2,1)} %get-tuple-ele, ...), custom_call_target="tpu_custom_call" | custom-call | tf_op jit(solution)/shard_map/mlp_sum/pallas_call | solution.py:699
  510.0 3.0 copy-done.1
  516.3 4.1 latents_back.4
  520.5 20.0 %attn_bwd.5 = (bf16[1,864,1024]{2,1,0:T(8,128)(2,1)}, bf16[1,1024,1152]{2,1,0:T(8,128)(2,1)}) custom-call(bf16[1,1024,1152]{2,1,0:T(8,128)(2,1)} %get-tuple-element.80.da_ref, bf16[3,288,1024]{2,1,0:T(8,128)(2,1)} %dynamic-slice_bitcast_fusion.heads_ref, bf16[3,12,72,1024]{3,2,1,0:T(8,128)(2,1)} %get-tuple-element.67.qkv_ref, ...), custom_call_target="tpu_custom_call" | custom-call | tf_op jit(solution)/shard_map/attn_bwd/pallas_call | solution.py:993
  546.2 2.1 reduce.7
  552.5 6.2 fusion.39
  558.7 11.5 %bitcast_convert_fusion = bf16[864,1152]{1,0:T(8,128)(2,1)} fusion(bf16[3,1024,1152]{2,1,0:T(8,128)(2,1)} %get-tuple-element.97, bf16[1,864,1024]{2,1,0:T(8,128)(2,1)S(1)} %copy-done.26, bf16[1,864,1024]{2,1,0:T(8,128)(2,1)S(1)} %copy-done.25, bf16[1,864,1024]{2,1,0:T(8,128)(2,1)S(1)} %copy-done.24), kind=kOutput, calls=%fused_computation.39 | convolution fusion | flops 6121598976 | bytes 14376960 | tf_op jit(solution)/shard_map/les,lsd->ed/dot_general | solution.py:1157
  570.3 14.9 %fusion.1 = bf16[1152,1152]{1,0:T(8,128)(2,1)} fusion(bf16[1,1024,1152]{2,1,0:T(8,128)(2,1)} %get-tuple-element.90, bf16[1,1024,1152]{2,1,0:T(8,128)(2,1)} %get-tuple-element.89, bf16[1,1024,1152]{2,1,0:T(8,128)(2,1)S(1)} %copy-done.37, bf16[1,1024,1152]{2,1,0:T(8,128)(2,1)} %get-tuple-element.93, bf16[1,1024,1152]{2,1,0:T(8,128)(2,1)} %get-tuple-element.92, ...), kind=kOutput, calls=%fused_computation.3 | convolution fusion | flops 8169209856 | bytes 16809984 | tf_op jit(solution)/shard_map/dot_general | solution.py:29
  585.3 13.1 %fusion = bf16[1152,1152]{1,0:T(8,128)(2,1)} fusion(bf16[1,1024,1152]{2,1,0:T(8,128)(2,1)} %get-tuple-element.84, bf16[1,1024,1152]{2,1,0:T(8,128)(2,1)S(1)} %copy-done.38, bf16[1,1024,1152]{2,1,0:T(8,128)(2,1)S(1)} %copy-done.35, bf16[1,1024,1152]{2,1,0:T(8,128)(2,1)S(1)} %copy-done.23, bf16[1,1024,1152]{2,1,0:T(8,128)(2,1)S(1)} %copy-done.22, ...), kind=kOutput, calls=%fused_computation.2 | convolution fusion | flops 8169209856 | bytes 16809984 | tf_op jit(solution)/shard_map/dot_general | solution.py:29
  598.4 36.2 %concatenate.63 = bf16[3460,1152]{1,0:T(8,128)(2,1)} concatenate(bf16[1152,1152]{1,0:T(8,128)(2,1)} %fusion, bf16[1152,1152]{1,0:T(8,128)(2,1)} %fusion.1, bf16[864,1152]{1,0:T(8,128)(2,1)} %bitcast_convert_fusion, bf16[288,1152]{1,0:T(8,128)(2,1)S(1)} %fusion.39, bf16[1,1152]{1,0:T(2,128)(2,1)S(1)} %stack.31, bf16[1,1152]{1,0:T(2,128)(2,1)S(1)} %stack.32, ...), dimensions={0} | concatenate | bytes 15943680 | tf_op jit(solution)/shard_map/concatenate | solution.py:1171
  634.6 7.1 pad.18
  641.7 101.4 %tail_sums.1 = (bf16[1,1024,1152]{2,1,0:T(8,128)(2,1)}, bf16[7,2,2,2,2,32,1152]{6,5,4,3,2,1,0:T(8,128)(2,1)}) custom-call(bf16[1,1024,1152]{2,1,0:T(8,128)(2,1)} %get-tuple-element.81.part_ref, bf16[7,2,2,2,2,32,1152]{6,5,4,3,2,1,0:T(8,128)(2,1)} %bitcast.50), custom_call_target="tpu_custom_call" | custom-call | tf_op jit(solution)/shard_map/tail_sums/pallas_call | solution.py:865
  743.1 3.0 copy-done.2
  749.5 3.9 latents_back.5
  755.0 2.8 fusion.65
  757.8 12.2 %rows_exchange.1 = (bf16[8,16,2880]{2,1,0:T(8,128)(2,1)S(1)}, f32[8,1152]{1,0:T(8,128)S(1)}) custom-call(bf16[16,2880]{1,0:T(8,128)(2,1)S(1)} %fusion.50.rows_ref, f32[8,1152]{1,0:T(8,128)S(1)} %pad.20.act_ref), custom_call_target="tpu_custom_call" | custom-call | tf_op jit(solution)/shard_map/rows_exchange/pallas_call | solution.py:930
  770.0 5.3 fusion.42
  777.3 6.3 pad_maximum_fusion
  783.7 4.8 slice_convert_fusion
  788.6 2.2 convert_bitcast_fusion
  (132 shorter events, 30.7 us)
Async XLA Ops:
  0.6 6.4 copy-start.30
  0.7 6.4 copy-start.34
  0.7 6.6 copy-start.33
  0.7 6.6 copy-start.16
  23.7 179.6 %copy-start.31 = (bf16[1152]{0:T(1024)(128)(2,1)S(1)}, bf16[1152]{0:T(1024)(128)(2,1)}, u32[]{:S(2)}) copy-start(bf16[1152]{0:T(1024)(128)(2,1)} %param.19) | copy-start | bytes 6916
  23.7 180.2 %copy-start.32 = (bf16[1152]{0:T(1024)(128)(2,1)S(1)}, bf16[1152]{0:T(1024)(128)(2,1)}, u32[]{:S(2)}) copy-start(bf16[1152]{0:T(1024)(128)(2,1)} %param.23) | copy-start | bytes 6916
  306.3 85.0 %copy-start.4 = (f32[3,6,1152]{2,1,0:T(8,128)S(1)}, f32[3,6,1152]{2,1,0:T(8,128)}, u32[]{:S(2)}) copy-start(f32[3,6,1152]{2,1,0:T(8,128)} %reshape.100.mod_ref.refs_3_) | copy-start | bytes 248836
  391.3 3.0 copy-start
  423.1 86.9 %copy-start.5 = (f32[3,6,1152]{2,1,0:T(8,128)S(1)}, f32[3,6,1152]{2,1,0:T(8,128)}, u32[]{:S(2)}) copy-start(f32[3,6,1152]{2,1,0:T(8,128)} %reshape.100.mod_ref.refs_3_) | copy-start | bytes 248836
  510.0 3.0 copy-start.1
  540.4 5.6 copy-start.27
  540.4 5.6 copy-start.28
  540.4 5.7 copy-start.29
  552.4 6.2 copy-start.24
  552.4 6.3 copy-start.25
  552.5 6.3 copy-start.26
  558.7 11.6 %copy-start.36 = (bf16[1,1024,1152]{2,1,0:T(8,128)(2,1)S(1)}, bf16[1,1024,1152]{2,1,0:T(8,128)(2,1)}, u32[]{:S(2)}) copy-start(bf16[1,1024,1152]{2,1,0:T(8,128)(2,1)} %get-tuple-element.91) | copy-start | bytes 7077892
  558.7 11.6 %copy-start.37 = (bf16[1,1024,1152]{2,1,0:T(8,128)(2,1)S(1)}, bf16[1,1024,1152]{2,1,0:T(8,128)(2,1)}, u32[]{:S(2)}) copy-start(bf16[1,1024,1152]{2,1,0:T(8,128)(2,1)} %get-tuple-element.88) | copy-start | bytes 7077892
  570.3 15.0 %copy-start.21 = (bf16[1,1024,1152]{2,1,0:T(8,128)(2,1)S(1)}, bf16[1,1024,1152]{2,1,0:T(8,128)(2,1)}, u32[]{:S(2)}) copy-start(bf16[1,1024,1152]{2,1,0:T(8,128)(2,1)} %get-tuple-element.85) | copy-start | bytes 7077892
  570.3 15.0 %copy-start.22 = (bf16[1,1024,1152]{2,1,0:T(8,128)(2,1)S(1)}, bf16[1,1024,1152]{2,1,0:T(8,128)(2,1)}, u32[]{:S(2)}) copy-start(bf16[1,1024,1152]{2,1,0:T(8,128)(2,1)} %get-tuple-element.86) | copy-start | bytes 7077892
  570.3 15.0 %copy-start.23 = (bf16[1,1024,1152]{2,1,0:T(8,128)(2,1)S(1)}, bf16[1,1024,1152]{2,1,0:T(8,128)(2,1)}, u32[]{:S(2)}) copy-start(bf16[1,1024,1152]{2,1,0:T(8,128)(2,1)} %get-tuple-element.87) | copy-start | bytes 7077892
  570.3 15.0 %copy-start.35 = (bf16[1,1024,1152]{2,1,0:T(8,128)(2,1)S(1)}, bf16[1,1024,1152]{2,1,0:T(8,128)(2,1)}, u32[]{:S(2)}) copy-start(bf16[1,1024,1152]{2,1,0:T(8,128)(2,1)} %get-tuple-element.82) | copy-start | bytes 7077892
  570.3 15.0 %copy-start.38 = (bf16[1,1024,1152]{2,1,0:T(8,128)(2,1)S(1)}, bf16[1,1024,1152]{2,1,0:T(8,128)(2,1)}, u32[]{:S(2)}) copy-start(bf16[1,1024,1152]{2,1,0:T(8,128)(2,1)} %get-tuple-element.83) | copy-start | bytes 7077892
  743.1 3.0 copy-start.2
  770.0 5.4 copy-start.17
  770.0 6.7 copy-start.7
  770.0 6.7 copy-start.9
  770.0 6.6 copy-start.18
  770.0 6.6 copy-start.19
  770.0 7.3 copy-start.20
  776.6 7.0 slice-start
  777.3 6.3 slice-start.1
  (9 other events, 14.9 us)

commit v4 on v3

--- a/solution.py
+++ b/solution.py
@@ -46,8 +46,11 @@
     return value + step - 2 * step * (value // step % 2)
 
 
-def other_part(me, k):
-    return (me + k) % 2 + 2 * ((me // 2 + k // 2) % 2)
+def near_part(me, k):
+    side = me // 2
+    end = jnp.minimum(me, 3 - me)
+    at = k + end * (1 - 2 * k) * ((3 - k) // 2)
+    return at + side * (3 - 2 * at)
 
 
 def line_peers(me, n):
@@ -185,7 +188,7 @@
 ):
     n_mp = all_ref.shape[0]
     lats = h1_all.shape[0]
-    units = 3 * (n_mp - 1)
+    units, pace = 3 * (n_mp - 1), 4
     slot, lat = pl.program_id(0), pl.program_id(1)
     step = slot * lats + lat
     dp_at, me = lax.axis_index("dp"), lax.axis_index("mp")
@@ -235,23 +238,26 @@
         )
 
     def unit(u):
-        return u // (n_mp - 1), other_part(me, 1 + u % (n_mp - 1))
+        return u // (n_mp - 1), near_part(me, 1 + u % (n_mp - 1))
 
     def event(stage, u):
         c, s = unit(u)
 
         @pl.when((u >= 0) & (u < units))
         def _():
+            if stage == 0:
+
+                @pl.when((me > 0) & (me < n_mp - 1))
+                def _():
+                    pass_on(s, c, right_id).wait_recv()
+                    pl.when(s < me)(lambda: pass_on(s, c, right_id).start())
+                    pl.when(s > me)(lambda: pass_on(s, c, left_id).start())
+
             if stage == 1:
-                pass_on(s, c, right_id).wait_recv()
-
-                @pl.when((s < me) & (me < n_mp - 1))
+
+                @pl.when((me == 0) | (me == n_mp - 1))
                 def _():
-                    pass_on(s, c, right_id).start()
-
-                @pl.when((s > me) & (me > 0))
-                def _():
-                    pass_on(s, c, left_id).start()
+                    pass_on(s, c, right_id).wait_recv()
 
                 move(0, c, s).start()
                 move(1, c, s).start()
@@ -302,14 +308,20 @@
         pl.semaphore_wait(barrier, 3 + line_peers(me, n_mp))
         send_own(0)
 
-    for c in (1, 2):
-
-        @pl.when(step == 3 * c - 1)
-        def _():
-            send_own(c)
-
-    event(4, step - 3)
-    event(3, step - 2)
+    def next_weights(k):
+        return pltpu.make_async_copy(all_ref.at[near_part(me, k), 0], w_buf, local_sem.at[0])
+
+    def tick(t):
+        def due(at, every):
+            return jnp.where((t - at) % every == 0, (t - at) // every, -1)
+
+        for k, at in ((0, 3), (1, 4), (2, 7)):
+            nth = due(at, 3 * pace)
+            event(0, jnp.where(nth < 0, -1, nth * 3 + k))
+        for stage, at in ((1, 3), (3, 8), (2, 5), (4, 11)):
+            event(stage, due(at, pace))
+        for c in (1, 2):
+            pl.when(t == 3 * pace * c - 3)(lambda: send_own(c))
 
     @pl.when((lat == 0) & (slot == 0))
     def _():
@@ -327,9 +339,7 @@
 
     @pl.when((lat == 0) & (slot > 0))
     def _():
-        load = pltpu.make_async_copy(all_ref.at[other_part(me, slot), 0], w_buf, local_sem.at[0])
-        load.start()
-        load.wait()
+        next_weights(slot).wait()
 
     @pl.when(slot == 0)
     def _():
@@ -340,15 +350,21 @@
     flat = nt(weights, h1_all[lat]) + bias_ref[0]
 
     def between(h):
-        if h == 1:
-            event(2, step - 1)
-        if h == 3:
-            event(1, step)
+        tick(step * n_heads + h - 1)
+
+        @pl.when((lat == lats - 1) & (slot < n_mp - 1) & (h == n_heads))
+        def _():
+            next_weights(slot + 1).start()
 
     attend(flat, n_heads, slot, heads_ref, qkv_ref, lse_ref, between)
 
     @pl.when(step == n_mp * lats - 1)
     def _():
+        def rest(t, carry):
+            tick(t)
+            return carry
+
+        lax.fori_loop(n_mp * lats * n_heads, pace * units + 11, rest, 0)
         for c in range(3):
 
             @pl.when(me < n_mp - 1)
@@ -362,13 +378,9 @@
         def drain(u, carry):
             c, s = unit(u)
 
-            @pl.when((s < me) & (me < n_mp - 1))
+            @pl.when((me > 0) & (me < n_mp - 1))
             def _():
                 pass_on(s, c, right_id).wait_send()
-
-            @pl.when((s > me) & (me > 0))
-            def _():
-                pass_on(s, c, left_id).wait_send()
 
             for kind in range(5):
                 move(kind, c, s).wait_send()
@@ -384,7 +396,7 @@
     rows = dim // 8
     last = lat - 1
     first = lambda s, l: s // n_mp * 0 + jnp.where(s == 0, l, last)
-    part = lambda s: other_part(lax.axis_index("mp"), s)
+    part = lambda s: near_part(lax.axis_index("mp"), s)
     heads, qkv, lse, h1, gathered = pl.pallas_call(
         attn_gather_kernel,
         grid=(n_mp, lat),
@@ -555,8 +567,8 @@
     own_refs, (wq_all, w1_all, w2_all), refs = refs[7:10], refs[10:13], refs[13:]
     if summing:
         part_ref, refs = refs[0], refs[1:]
-    out_ref, dx1_ref, da_ref, h2_ref, dm_ref, z_ref, du_ref, stats_ref = refs[:8]
-    refs = refs[8:]
+    out_ref, dx1_ref, da_ref, h2_ref, dm_ref, z_ref, du_ref, stats_ref, dusum_ref = refs[:9]
+    refs = refs[9:]
     if summing:
         sum_ref, refs = refs[0], refs[1:]
     macc, dacc, wp, w1, w2, load_sems = refs[:6]
@@ -622,7 +634,11 @@
         half = 0.5 + 0.5 * t
         z = (u * half).astype(BF)
         slope = half + u * (1.0 - t * t) * (0.5 * GELU_A + (1.5 * GELU_A * GELU_B) * u2)
-        du = (dz * slope).astype(BF)
+        du = dz * slope
+        if own:
+            before = jnp.where(step == 0, 0.0, dusum_ref[0])
+            dusum_ref[0] = before + jnp.sum(du, 0, keepdims=True)
+        du = du.astype(BF)
         if own:
             z_ref[0] = z
             du_ref[0] = du
@@ -711,11 +727,16 @@
         + [any_spec] * 6
         + extra,
         out_specs=[new] * 5
-        + [hidden, hidden, pl.BlockSpec((1, 8, dim), lambda t: (0, 0, 0))]
+        + [
+            hidden,
+            hidden,
+            pl.BlockSpec((1, 8, dim), lambda t: (0, 0, 0)),
+            pl.BlockSpec((1, 1, hid), lambda t: (0, 0, 0)),
+        ]
         + extra,
         out_shape=[jax.ShapeDtypeStruct((1, seq, dim), BF)] * 5
         + [jax.ShapeDtypeStruct((1, seq, hid), BF)] * 2
-        + [jax.ShapeDtypeStruct((1, 8, dim), F32)]
+        + [jax.ShapeDtypeStruct((1, 8, dim), F32), jax.ShapeDtypeStruct((1, 1, hid), F32)]
         + ([jax.ShapeDtypeStruct((1, seq, dim), BF)] if summing else []),
         scratch_shapes=[
             pltpu.VMEM((rows, dim), F32),
@@ -747,7 +768,7 @@
     def __init__(self, terms, full, halves, firsts, seconds, sems):
         self.terms, self.full = terms, full
         self.halves, self.firsts, self.seconds, self.sems = halves, firsts, seconds, sems
-        self.units = terms.shape[0]
+        self.units = halves.shape[0]
         dp_at, me = lax.axis_index("dp"), lax.axis_index("mp")
         self.core, x, y = dp_at % 2, dp_at // 2 % 2, dp_at // 4
         self.core_id = at_mesh(flip(dp_at, 0), me)
@@ -760,29 +781,34 @@
         for target in (self.core_id,) + self.ids[0]:
             pl.semaphore_signal(sem, inc=1, **target)
 
+    def blocks(self, u, core, q=None, first=None, second=None):
+        at, count = 16 * u + 8 * core, 8
+        if q is not None:
+            at, count = at + 4 * q, 4
+        if first is not None:
+            at, count = at + 2 * first, 2
+        if second is not None:
+            at, count = at + second, 1
+        return pl.ds(at, count)
+
     def send(self, stage, u, q, arrived=False):
-        core = self.core
-        terms, full = self.terms, self.full
+        core, blocks = self.core, self.blocks
         first, second = self.place[q]
+        other = lambda v: 1 - v if arrived else v
         if stage == 0:
-            pair, target = (terms.at[u, 1 - core], self.halves.at[u]), self.core_id
+            pair = (self.terms.at[blocks(u, 1 - core)], self.halves.at[u])
         elif stage == 1:
-            pair = (terms.at[u, core, q, 1 - first], self.firsts.at[u, q])
-            target = self.ids[q][0]
+            pair = (self.terms.at[blocks(u, core, q, 1 - first)], self.firsts.at[u, q])
         elif stage == 2:
-            pair = (terms.at[u, core, q, first, 1 - second], self.seconds.at[u, q])
-            target = self.ids[q][1]
+            pair = (self.terms.at[blocks(u, core, q, first, 1 - second)], self.seconds.at[u, q])
         elif stage == 3:
-            at = 1 - second if arrived else second
-            pair = (full.at[u, core, q, first, at],) * 2
-            target = self.ids[q][1]
+            pair = (self.full.at[blocks(u, core, q, first, other(second))],) * 2
         elif stage == 4:
-            at = 1 - first if arrived else first
-            pair = (full.at[u, core, q, at],) * 2
-            target = self.ids[q][0]
+            pair = (self.full.at[blocks(u, core, q, other(first))],) * 2
         else:
-            at = 1 - core if arrived else core
-            pair, target = (full.at[u, at],) * 2, self.core_id
+            pair = (self.full.at[blocks(u, other(core))],) * 2
+        near, far = self.ids[q]
+        target = (self.core_id, near, far, far, near, self.core_id)[stage]
         return pltpu.make_async_remote_copy(
             *pair, self.sems.at[0, stage, q, u], self.sems.at[1, stage, q, u], **target
         )
@@ -791,7 +817,7 @@
         return (0,) if stage in (0, 5) else (0, 1)
 
     def event(self, stage, u):
-        terms, core = self.terms, self.core
+        terms, core, blocks = self.terms, self.core, self.blocks
 
         @pl.when((u >= 0) & (u < self.units))
         def _():
@@ -799,17 +825,17 @@
                 for q in self.quarters(stage - 1):
                     self.send(stage - 1, u, q, True).wait_recv()
             if stage == 1:
-                total = terms[u, core].astype(F32) + self.halves[u].astype(F32)
-                terms[u, core] = total.astype(BF)
+                at = blocks(u, core)
+                terms[at] = (terms[at].astype(F32) + self.halves[u].astype(F32)).astype(BF)
             for q in (0, 1):
                 first, second = self.place[q]
                 if stage == 2:
-                    total = terms[u, core, q, first].astype(F32) + self.firsts[u, q].astype(F32)
-                    terms[u, core, q, first] = total.astype(BF)
+                    at = blocks(u, core, q, first)
+                    terms[at] = (terms[at].astype(F32) + self.firsts[u, q].astype(F32)).astype(BF)
                 if stage == 3:
-                    total = terms[u, core, q, first, second].astype(F32)
-                    total = total + self.seconds[u, q].astype(F32)
-                    self.full[u, core, q, first, second] = total.astype(BF)
+                    at = blocks(u, core, q, first, second)
+                    total = terms[at].astype(F32) + self.seconds[u, q].astype(F32)
+                    self.full[at] = total.astype(BF)
             if stage < 6:
                 for q in self.quarters(stage):
                     self.send(stage, u, q).start()
@@ -824,65 +850,169 @@
         lax.fori_loop(0, self.units, sent, 0)
 
 
-def tail_kernel(
-    part_ref, terms_ref, sum_ref, full_ref, up, down, line_sems, terms, full, *refs
-):
-    halves, firsts, seconds, cube_sems, local_sem = refs
+BLOCK = 32
+
+
+class WeightGrads:
+    def __init__(self, operands, terms, right, left_cols, left_rows, right_sems, left_sems):
+        self.operands, self.terms, self.right = operands, terms, right
+        self.left_cols, self.left_rows = left_cols, left_rows
+        self.right_sems, self.left_sems = right_sems, left_sems
+        self.lats = right.shape[1]
+        dim = right.shape[3]
+        qkv_blocks = operands[2][0][0].shape[0] // BLOCK
+        half = (qkv_blocks + 1) // 2 * BLOCK
+        third = dim // 3
+        self.pieces = [(job, i * third, third) for job in (0, 1) for i in range(3)]
+        self.pieces += [(2, 0, half), (2, half, qkv_blocks * BLOCK - half)]
+        self.pieces += [(3, 0, operands[3][0][0].shape[0])]
+
+    def right_copies(self, job):
+        slot = job % 2
+        return [
+            pltpu.make_async_copy(
+                self.operands[job][1][i], self.right.at[slot, i], self.right_sems.at[slot, i]
+            )
+            for i in range(self.lats)
+        ]
+
+    def left_copies(self, at):
+        job, first, count = self.pieces[at]
+        copies = []
+        for i in range(self.lats):
+            source = self.operands[job][0][i]
+            if job < 2:
+                source = source.at[:, pl.ds(first, count)]
+                ref = self.left_cols.at[at % 2, i]
+            else:
+                source = source.at[pl.ds(first, count)]
+                ref = self.left_rows.at[at % 2, i, pl.ds(0, count)]
+            copies.append(pltpu.make_async_copy(source, ref, self.left_sems.at[at % 2, i]))
+        return copies
+
+    def begin(self):
+        for copy in self.right_copies(0) + self.left_copies(0):
+            copy.start()
+
+    def compute(self, at):
+        job, _, count = self.pieces[at]
+        opens = at == 0 or self.pieces[at - 1][0] != job
+        if at + 1 < len(self.pieces):
+            for copy in self.left_copies(at + 1):
+                copy.start()
+        if opens:
+            if job + 1 < len(self.operands):
+                for copy in self.right_copies(job + 1):
+                    copy.start()
+            for copy in self.right_copies(job):
+                copy.wait()
+        for copy in self.left_copies(at):
+            copy.wait()
+        slot, dim = job % 2, self.right.shape[3]
+        if job < 2:
+            left = self.left_cols[at % 2].reshape(-1, count)
+            total = tn(left, self.right[slot].reshape(-1, dim))
+        else:
+            total = mm(self.left_rows[at % 2, 0, :count], self.right[slot, 0])
+            for i in range(1, self.lats):
+                total = total + mm(self.left_rows[at % 2, i, :count], self.right[slot, i])
+        done = sum(rows for _, _, rows in self.pieces[:at]) // BLOCK
+        self.terms[pl.ds(done, count // BLOCK)] = total.reshape(-1, BLOCK, dim).astype(BF)
+
+
+def tail_kernel(*refs, lats):
+    part_ref, bias_ref, heads_ref, h1_ref = refs[:4]
+    lists = [refs[4 + i * lats : 4 + (i + 1) * lats] for i in range(6)]
+    h2s, dus, zs, dms, dqkvs, das = [[ref.at[0] for ref in group] for group in lists]
+    sum_ref, full_ref = refs[4 + 6 * lats : 6 + 6 * lats]
+    refs = refs[6 + 6 * lats :]
+    up, down, line_sems, terms, full, halves, firsts, seconds, cube_sems = refs[:9]
+    right, left_cols, left_rows, right_sems, left_sems, local_sem = refs[9:]
     line = LineSum(part_ref, up, down, line_sems, sum_ref)
     cube = CubeSum(terms, full, halves, firsts, seconds, cube_sems)
-    load = pltpu.make_async_copy(terms_ref, terms, local_sem.at[0])
-    load.start()
+    heads = [heads_ref.at[line.me, i] for i in range(lats)]
+    h1s = [h1_ref.at[i] for i in range(lats)]
+    grads = WeightGrads(
+        ((h2s, dus), (zs, dms), (dqkvs, h1s), (heads, das)),
+        terms,
+        right,
+        left_cols,
+        left_rows,
+        right_sems,
+        left_sems,
+    )
+    grads.begin()
     cube.barrier()
     line.greet()
     pl.semaphore_wait(pltpu.get_barrier_semaphore(), 3 + line_peers(line.me, line.n))
-    load.wait()
-    rounds = cube.units + 6
+    spare = bias_ref.shape[0]
+    terms[pl.ds(terms.shape[0] - spare, spare)] = bias_ref[...]
+    line.tick(0)
+    unit_rows = 16 * BLOCK
+    ready = 0
+    for t in range(cube.units):
+        line.tick(2 * t + 1)
+        while ready < len(grads.pieces) and (
+            sum(rows for _, _, rows in grads.pieces[:ready]) < (t + 1) * unit_rows
+        ):
+            grads.compute(ready)
+            ready += 1
+        line.tick(2 * t + 2)
+        for stage in range(min(t, 6), -1, -1):
+            cube.event(stage, t - stage)
 
     def advance(t, carry):
-        line.tick(2 * t)
-        for stage in (6, 5, 4, 3):
+        line.tick(2 * t + 1)
+        for stage in range(6, 0, -1):
             cube.event(stage, t - stage)
-        line.tick(2 * t + 1)
-        for stage in (2, 1, 0):
-            cube.event(stage, t - stage)
+        line.tick(2 * t + 2)
         return carry
 
-    lax.fori_loop(0, rounds, advance, 0)
+    lax.fori_loop(cube.units, cube.units + 6, advance, 0)
     store = pltpu.make_async_copy(full, full_ref, local_sem.at[0])
     store.start()
-    line.finish(2 * rounds)
+    line.finish(2 * (cube.units + 6) + 1)
     cube.finish()
     store.wait()
 
 
-def tail_sums(part, terms):
-    _, seq, dim = part.shape
-    units, rows, _ = terms.shape
-    rows = rows // 16
+def tail_sums(part, biases, heads, h1, lists):
+    n_mp, lats, local, seq = heads.shape
+    dim = h1.shape[2]
+    rows = 2 * dim + 4 * local
+    units = -(-(rows + BLOCK) // (16 * BLOCK))
+    spare = units * 16 - rows // BLOCK
+    biases = jnp.pad(biases, ((0, spare * BLOCK - biases.shape[0]), (0, 0)))
     vmem = pl.BlockSpec(memory_space=pltpu.VMEM)
     any_spec = pl.BlockSpec(memory_space=pl.ANY)
-    shape = (units, 2, 2, 2, 2, rows, dim)
+    shape = (units * 16, BLOCK, dim)
+    flat = [array for group in lists for array in group]
     total, full = pl.pallas_call(
-        tail_kernel,
-        in_specs=[vmem, any_spec],
+        functools.partial(tail_kernel, lats=lats),
+        in_specs=[vmem, vmem] + [any_spec] * (2 + len(flat)),
         out_specs=[vmem, any_spec],
         out_shape=[jax.ShapeDtypeStruct(part.shape, BF), jax.ShapeDtypeStruct(shape, BF)],
         scratch_shapes=line_scratch(seq, dim)
         + [
             pltpu.VMEM(shape, BF),
             pltpu.VMEM(shape, BF),
-            pltpu.VMEM((units, 2, 2, 2, rows, dim), BF),
-            pltpu.VMEM((units, 2, 2, rows, dim), BF),
-            pltpu.VMEM((units, 2, rows, dim), BF),
+            pltpu.VMEM((units, 8, BLOCK, dim), BF),
+            pltpu.VMEM((units, 2, 2, BLOCK, dim), BF),
+            pltpu.VMEM((units, 2, 1, BLOCK, dim), BF),
             pltpu.SemaphoreType.DMA((2, 6, 2, units)),
+            pltpu.VMEM((2, lats, seq, dim), BF),
+            pltpu.VMEM((2, lats, seq, dim // 3), BF),
+            pltpu.VMEM((2, lats, (3 * local // BLOCK + 1) // 2 * BLOCK, seq), BF),
+            pltpu.SemaphoreType.DMA((2, lats)),
+            pltpu.SemaphoreType.DMA((2, lats)),
             pltpu.SemaphoreType.DMA((1,)),
         ],
         compiler_params=pltpu.CompilerParams(
-            collective_id=2, has_side_effects=True, vmem_limit_bytes=60 * MIB
+            collective_id=2, has_side_effects=True, vmem_limit_bytes=63 * MIB
         ),
         name="tail_sums",
-    )(part, terms.reshape(shape))
-    return total, full.reshape(units * rows * 16, dim)
+    )(part, biases.reshape(spare, BLOCK, dim), heads, h1, *flat)
+    return total, full.reshape(units * 16 * BLOCK, dim)
 
 
 def rows_kernel(rows_ref, act_ref, every_ref, total_ref, acts, sems):
@@ -946,7 +1076,7 @@
     )(rows, act)
 
 
-def attn_bwd_kernel(da_ref, heads_ref, qkv_ref, lse_ref, wp_ref, wq_ref, dqkv_ref, dh1_ref, *, rows):
+def attn_bwd_kernel(da_ref, heads_ref, qkv_ref, lse_ref, wp_ref, wq_ref, dqkv_ref, dh1_ref, bias_ref, *, rows):
     n_heads = lse_ref.shape[1]
     seq = da_ref.shape[1]
     dheads = nt(wp_ref[...], da_ref[0]).reshape(n_heads, HEAD_DIM, seq)
@@ -977,7 +1107,9 @@
         dq_list.append(jnp.concatenate(dq_parts, 1) * scaling)
         dk_list.append(dk.T * (1.0 / LOG2E))
         dv_list.append(dv.T)
-    dqkv = jnp.concatenate(dq_list + dk_list + dv_list, 0).astype(BF)
+    dqkv = jnp.concatenate(dq_list + dk_list + dv_list, 0)
+    bias_ref[0] = jnp.sum(dqkv, 1, keepdims=True)
+    dqkv = dqkv.astype(BF)
     dqkv_ref[0] = dqkv
     dh1_ref[0] = tn(dqkv, wq_ref[...]).astype(BF)
 
@@ -1001,10 +1133,11 @@
             whole((local, dim)),
             whole((3 * local, dim)),
         ],
-        out_specs=[out((3 * local, seq)), out((seq, dim))],
+        out_specs=[out((3 * local, seq)), out((seq, dim)), out((3 * local, 1))],
         out_shape=[
             jax.ShapeDtypeStruct((1, 3 * local, seq), BF),
             jax.ShapeDtypeStruct((1, seq, dim), BF),
+            jax.ShapeDtypeStruct((1, 3 * local, 1), F32),
         ],
         compiler_params=pltpu.CompilerParams(vmem_limit_bytes=60 * MIB),
         name="attn_bwd",
@@ -1118,7 +1251,7 @@
         heads, qkv, lse, h1 = attn_fwd(me, latents, mod, gathered[0], b_qkv, n_mp)
     heads_own = lax.dynamic_index_in_dim(heads, mp_at, 0, keepdims=False)
     rows = min(256, seq)
-    results, dqkv, dh1 = [], [], []
+    results, dqkv, dh1, bias_sums = [], [], [], []
     for i in range(lat):
         waiting = dqkv and direct
         outs = mlp_both(
@@ -1136,27 +1269,24 @@
         )
         if waiting:
             dh1.append(outs[-1])
-        results.append(outs[:8])
-        dqkv_i, dh1_i = attn_bwd(
+        results.append(outs[:9])
+        dqkv_i, dh1_i, sums_i = attn_bwd(
             outs[2], heads_own, qkv, lse, proj_weight, wq_own, i, min(512, seq)
         )
         dqkv.append(dqkv_i)
+        bias_sums.append(sums_i)
         if not direct:
             dh1.append(lax.psum(dh1_i, "mp"))
-    dqkv = jnp.concatenate(dqkv, 0)
-    block_out, dx1, da, h2, dm, z, du, stats_two = [
-        jnp.concatenate(parts, 0) for parts in zip(*results)
-    ]
-    flat = lambda v: v.reshape(lat * seq, v.shape[-1])
-    grad_fc2 = tn(flat(z), flat(dm)).astype(BF)
-    grad_fc1 = tn(flat(h2), flat(du)).astype(BF)
-    grad_fc1_bias = jnp.sum(flat(du).astype(F32), 0)
+    outs_by_kind = list(zip(*results))
+    h2, dm, z, du = outs_by_kind[3:7]
+    da = outs_by_kind[2]
+    block_out = jnp.concatenate(outs_by_kind[0], 0)
+    stats_two = jnp.concatenate(outs_by_kind[7], 0)
+    grad_fc1_bias = sum(outs_by_kind[8])[0, 0]
     gate_one, gate_two = mod[:, 2], mod[:, 5]
     grad_fc2_bias = jnp.sum(gate_two * stats_two[:, 4], 0)
     grad_proj_bias = jnp.sum(gate_one * stats_two[:, 5], 0)
-    grad_qkv = jnp.einsum("les,lsd->ed", dqkv, h1, preferred_element_type=F32).astype(BF)
-    grad_proj = jnp.einsum("les,lsd->ed", heads_own, da, preferred_element_type=F32).astype(BF)
-    bias_sums = jnp.sum(dqkv.astype(F32), (0, 2)).reshape(3, local)
+    bias_sums = sum(bias_sums).reshape(3, local)
     grad_qv_bias = jnp.stack([bias_sums[0], bias_sums[2]])
     if direct:
         bias_rows = jnp.stack(
@@ -1167,10 +1297,7 @@
                 jnp.pad(grad_qv_bias.reshape(-1), (0, dim - 2 * local)),
             ]
         ).astype(BF)
-        unit = 512
-        terms = jnp.concatenate([grad_fc1, grad_fc2, grad_qkv, grad_proj, bias_rows], 0)
-        terms = jnp.pad(terms, ((0, -terms.shape[0] % unit), (0, 0))).reshape(-1, unit, dim)
-        dh1_i, sums = tail_sums(dh1_i, terms)
+        dh1_i, sums = tail_sums(dh1_i, bias_rows, heads, h1, (h2, du, z, dm, dqkv, da))
         dh1.append(dh1_i)
         grad_fc1, grad_fc2 = sums[:dim], sums[dim : 2 * dim]
         grad_qkv = sums[2 * dim : 2 * dim + 3 * local]
@@ -1179,8 +1306,13 @@
         grad_fc1_bias, grad_fc2_bias, grad_proj_bias = bias_rows[:3]
         grad_qv_bias = bias_rows[3, : 2 * local].reshape(2, local)
     else:
-        grad_fc1, grad_fc2 = lax.psum((grad_fc1, grad_fc2), "dp")
-        grad_qkv, grad_proj = lax.psum((grad_qkv, grad_proj), "dp")
+        flat = lambda parts: jnp.concatenate(parts, 0).reshape(lat * seq, -1)
+        grad_fc2 = tn(flat(z), flat(dm))
+        grad_fc1 = tn(flat(h2), flat(du))
+        grad_qkv = sum(mm(dqkv[i][0], h1[i]) for i in range(lat))
+        grad_proj = sum(mm(heads_own[i], da[i][0]) for i in range(lat))
+        grads = [grad.astype(BF) for grad in (grad_fc1, grad_fc2, grad_qkv, grad_proj)]
+        grad_fc1, grad_fc2, grad_qkv, grad_proj = lax.psum(grads, "dp")
         biases = lax.psum((grad_fc1_bias, grad_fc2_bias, grad_proj_bias, grad_qv_bias), "dp")
         grad_fc1_bias, grad_fc2_bias, grad_proj_bias, grad_qv_bias = biases
 

time: 805 us -> 692 us (0.86)
  matrix products: 53.8 us -> 7.4 us
  local copies, waits for them, and re-layouts: 84.9 us -> 45.8 us
  Pallas kernels: 626 us -> 613 us
    concatenate x2 -> x1, local copies, waits for them, and re-layouts: 36.2 us -> 0.01 us  [per_device(): stats_two = jnp.concatenate(outs_by_kind[7], 0)]
    pallas_call x1, Pallas kernels: 179 us -> 150 us  [attn_gather(): pl.pallas_call(attn_gather_kernel, grid=(n_mp, lat), in_specs=[pl.BlockSp...]
    dot_general x3 -> x1, matrix products: 33.3 us -> 4.5 us  [tn(): lax.dot_general(a, b, (((0,), (0,)), ((), ())), preferred_element_type=F32)]
    dot_general x2 -> x0, matrix products: 17.7 us -> none  [the longest x1 11.5 us: per_device(): jnp.einsum('les,lsd->ed', dqkv, h1, preferred_element_type=F32).astype(BF)]
    pallas_call x1, Pallas kernels: 101 us -> 114 us  [tail_sums(): pl.pallas_call(functools.partial(tail_kernel, lats=lats), in_specs=[vmem,...]
    reduce_sum x9 -> x1, other arithmetic: 11.7 us -> 0.08 us  [per_device(): grad_fc2_bias = jnp.sum(gate_two * stats_two[:, 4], 0)]
    unnamed x86 -> x58, local copies, waits for them, and re-layouts: 31.1 us -> 30.3 us
where the time goes in v4:
time: 692 us; the launch traced here: 687 us
  Pallas kernels  613 us (89%)
  local copies, waits for them, and re-layouts  45.8 us (7%)
  other arithmetic  20 us (3%)
  matrix products  7.4 us (1%)
    pallas_call x3, Pallas kernels, mlp_both(): pl.pallas_call(functools.partial(mlp_kernel, summing=summing), grid=(seq...  252 us
    pallas_call x1, Pallas kernels, attn_gather(): pl.pallas_call(attn_gather_kernel, grid=(n_mp, lat), in_specs=[pl.BlockSp...  150 us
    pallas_call x1, Pallas kernels, tail_sums(): pl.pallas_call(functools.partial(tail_kernel, lats=lats), in_specs=[vmem,...  114 us
    pallas_call x3, Pallas kernels, attn_bwd(): pl.pallas_call(functools.partial(attn_bwd_kernel, rows=rows), grid=(1,),...  60.2 us
    unnamed x58, local copies, waits for them, and re-layouts  30.3 us
    pallas_call x1, Pallas kernels, rows_exchange(): pl.pallas_call(rows_kernel, in_specs=[vmem, vmem], out_specs=[vmem, vmem]...  13.9 us

profile of v4, /device:TPU:0, one launch (start us, length us, event | category | flops | bytes accessed | tf_op | source)
XLA Modules:
  0.0 687.3 jit_solution(14896979344722636997)
XLA Ops:
  5.5 6.4 copy.28.w_ref
  11.9 2.2 copy-done.3
  14.1 10.3 %modulation.1 = (f32[4,8,1728]{2,1,0:T(8,128)S(1)}, bf16[3,1152]{1,0:T(4,128)(2,1)S(1)}) custom-call(f32[3,1152]{1,0:T(4,128)S(1)} %copy-done.16, bf16[1152,1728]{1,0:T(8,128)(2,1)S(1)} %copy-done.3, f32[1,1728]{1,0:T(1,128)S(1)} %reshape.117.bias_ref, f32[1,1728]{1,0:T(1,128)S(1)} %maximum_convert_fusion.row_ref), custom_call_target="tpu_custom_call" | custom-call | tf_op jit(solution)/shard_map/modulation/pallas_call | solution.py:102
  26.1 2.9 reshape.124.bias_ref
  28.9 150.0 %attn_gather.1 = (bf16[4,3,288,1024]{3,2,1,0:T(8,128)(2,1)}, bf16[3,12,72,1024]{3,2,1,0:T(8,128)(2,1)}, f32[3,4,1024]{2,1,0:T(4,128)}, bf16[3,1024,1152]{2,1,0:T...) custom-call(bf16[3,1024,1152]{2,1,0:T(8,128)(2,1)} %lat_ref.7, f32[3,6,1152]{2,1,0:T(8,128)} %reshape.108.mod_ref.refs_3_, ...), custom_call_target="tpu_custom_call" | custom-call | tf_op jit(solution)/shard_map/attn_gather/pallas_call | solution.py:400
  178.9 2.8 dynamic-slice_bitcast_fusion.heads_ref
  181.8 79.4 %mlp_both.1 = (bf16[1,1024,1152]{2,1,0:T(8,128)(2,1)}, bf16[1,1024,1152]{2,1,0:T(8,128)(2,1)}, bf16[1,1024,1152]{2,1,0:T(8,128)(2,1)}, bf16[1,1024,1152]{2,1,0:T...) custom-call(bf16[4,3,288,1024]{3,2,1,0:T(8,128)(2,1)} %get-tuple-ele, ...), custom_call_target="tpu_custom_call" | custom-call | tf_op jit(solution)/shard_map/mlp_both/pallas_call | solution.py:715
  261.9 19.9 %attn_bwd.3 = (bf16[1,864,1024]{2,1,0:T(8,128)(2,1)}, bf16[1,1024,1152]{2,1,0:T(8,128)(2,1)}, f32[1,864,1]{2,1,0:T(8,128)}) custom-call(bf16[1,1024,1152]{2,1,0:T(8,128)(2,1)} %get-tuple-element.72.da_ref.refs_19_, bf16[3,288,1024]{2,1,0:T(8,128)(2,1)} %dynamic-slice_bitcast_fusion.heads_ref, bf16[3,12,72,1024]{3,2,1,0:T(8,128)(2,1)} %get-tuple-element.73.qkv_ref, ...), custom_call_target="tpu_custom_call" | custom-call | tf_op jit(solution)/shard_map/attn_bwd/pallas_call | solution.py:1125
  281.8 87.8 %mlp_sum.2 = (bf16[1,1024,1152]{2,1,0:T(8,128)(2,1)}, bf16[1,1024,1152]{2,1,0:T(8,128)(2,1)}, bf16[1,1024,1152]{2,1,0:T(8,128)(2,1)}, bf16[1,1024,1152]{2,1,0:T(...) custom-call(bf16[4,3,288,1024]{3,2,1,0:T(8,128)(2,1)} %get-tuple-ele, ...), custom_call_target="tpu_custom_call" | custom-call | tf_op jit(solution)/shard_map/mlp_sum/pallas_call | solution.py:715
  370.5 3.0 copy-done
  373.5 1.7 copy-done.13
  375.1 1.7 copy-done.15
  376.8 4.3 latents_back.3
  381.1 1.4 copy-done.6
  382.5 20.0 %attn_bwd.4 = (bf16[1,864,1024]{2,1,0:T(8,128)(2,1)}, bf16[1,1024,1152]{2,1,0:T(8,128)(2,1)}, f32[1,864,1]{2,1,0:T(8,128)}) custom-call(bf16[1,1024,1152]{2,1,0:T(8,128)(2,1)} %get-tuple-element.77.da_ref.refs_20_, bf16[3,288,1024]{2,1,0:T(8,128)(2,1)} %dynamic-slice_bitcast_fusion.heads_ref, bf16[3,12,72,1024]{3,2,1,0:T(8,128)(2,1)} %get-tuple-element.73.qkv_ref, ...), custom_call_target="tpu_custom_call" | custom-call | tf_op jit(solution)/shard_map/attn_bwd/pallas_call | solution.py:1125
  402.4 85.2 %mlp_sum.3 = (bf16[1,1024,1152]{2,1,0:T(8,128)(2,1)}, bf16[1,1024,1152]{2,1,0:T(8,128)(2,1)}, bf16[1,1024,1152]{2,1,0:T(8,128)(2,1)}, bf16[1,1024,1152]{2,1,0:T(...) custom-call(bf16[4,3,288,1024]{3,2,1,0:T(8,128)(2,1)} %get-tuple-ele, ...), custom_call_target="tpu_custom_call" | custom-call | tf_op jit(solution)/shard_map/mlp_sum/pallas_call | solution.py:715
  487.7 20.3 %attn_bwd.5 = (bf16[1,864,1024]{2,1,0:T(8,128)(2,1)}, bf16[1,1024,1152]{2,1,0:T(8,128)(2,1)}, f32[1,864,1]{2,1,0:T(8,128)}) custom-call(bf16[1,1024,1152]{2,1,0:T(8,128)(2,1)} %get-tuple-element.86.da_ref.refs_21_, bf16[3,288,1024]{2,1,0:T(8,128)(2,1)} %dynamic-slice_bitcast_fusion.heads_ref, bf16[3,12,72,1024]{3,2,1,0:T(8,128)(2,1)} %get-tuple-element.73.qkv_ref, ...), custom_call_target="tpu_custom_call" | custom-call | tf_op jit(solution)/shard_map/attn_bwd/pallas_call | solution.py:1125
  509.6 3.0 copy-done.1
  512.7 1.7 copy-done.12
  514.3 3.9 latents_back.4
  518.2 1.4 copy-done.8
  520.4 113.8 %tail_sums.1 = (bf16[1,1024,1152]{2,1,0:T(8,128)(2,1)}, bf16[112,32,1152]{2,1,0:T(8,128)(2,1)}) custom-call(bf16[1,1024,1152]{2,1,0:T(8,128)(2,1)} %get-tuple-element.87.refs_0_, bf16[4,32,1152]{2,1,0:T(8,128)(2,1)} %bitcast.53, bf16[4,3,288,1024]{3,2,1,0:T(8,128)(2,1)} %get-tuple-element.69.refs_0_.refs_2_, ...), custom_call_target="tpu_custom_call" | custom-call | tf_op jit(solution)/shard_map/tail_sums/pallas_call | solution.py:990
  634.3 3.0 copy-done.2
  637.3 1.7 copy-done.10
  638.9 1.7 copy-done.14
  640.6 3.9 latents_back.5
  644.6 7.1 %pad_maximum_fusion = (bf16[3,1024,1152]{2,1,0:T(8,128)(2,1)}, bf16[3,1024,1152]{2,1,0:T(8,128)(2,1)}) fusion(bf16[1,1024,1152]{2,1,0:T(8,128)(2,1)} %get-tuple-element.79, bf16[1,1024,1152]{2,1,0:T(8,128)(2,1)S(1)} %copy-done.20, bf16[1,1024,1152]{2,1,0:T(8,128)(2,1)S(1)} %copy-done.19, bf16[1,1024,1152]{2,1,0:T(8,128)(2,1)S(1)} %get-tuple-element.115, ...), kind=kLoop, calls=%fused_computation | loop fusion | flops 14155776 | bytes 28311552 | tf_op jit(solution)/shard_map/concatenate | solution.py:1283
  653.9 2.9 fusion.26
  656.9 13.9 %rows_exchange.1 = (bf16[8,16,2880]{2,1,0:T(8,128)(2,1)S(1)}, f32[8,1152]{1,0:T(8,128)S(1)}) custom-call(bf16[16,2880]{1,0:T(8,128)(2,1)S(1)} %fusion.15.rows_ref, f32[8,1152]{1,0:T(8,128)S(1)} %pad.20.act_ref), custom_call_target="tpu_custom_call" | custom-call | tf_op jit(solution)/shard_map/rows_exchange/pallas_call | solution.py:1060
  675.1 2.2 convert_bitcast_fusion
  677.3 5.2 bitcast_convert_fusion
  682.5 4.5 fusion.4
  (93 shorter events, 17.0 us)
Async XLA Ops:
  5.5 6.4 copy-start.16
  11.9 2.2 copy-start.3
  281.8 88.6 %copy-start.4 = (f32[3,6,1152]{2,1,0:T(8,128)S(1)}, f32[3,6,1152]{2,1,0:T(8,128)}, u32[]{:S(2)}) copy-start(f32[3,6,1152]{2,1,0:T(8,128)} %reshape.108.mod_ref.refs_3_) | copy-start | bytes 248836
  370.5 3.0 copy-start
  373.5 1.7 copy-start.13
  375.1 1.7 copy-start.15
  381.1 1.4 copy-start.6
  487.7 20.4 %copy-start.21 = (f32[1,864,1]{2,1,0:T(8,128)S(1)}, f32[1,864,1]{2,1,0:T(8,128)}, u32[]{:S(2)}) copy-start(f32[1,864,1]{2,1,0:T(8,128)} %get-tuple-element.94) | copy-start | bytes 10372
  487.7 20.4 %copy-start.22 = (f32[1,864,1]{2,1,0:T(8,128)S(1)}, f32[1,864,1]{2,1,0:T(8,128)}, u32[]{:S(2)}) copy-start(f32[1,864,1]{2,1,0:T(8,128)} %get-tuple-element.95) | copy-start | bytes 10372
  487.7 21.6 %copy-start.23 = (f32[1,8,1152]{2,1,0:T(8,128)S(1)}, f32[1,8,1152]{2,1,0:T(8,128)}, u32[]{:S(2)}) copy-start(f32[1,8,1152]{2,1,0:T(8,128)} %get-tuple-element.93) | copy-start | bytes 110596
  487.7 21.7 %copy-start.24 = (f32[1,1,1152]{2,1,0:T(1,128)S(1)}, f32[1,1,1152]{2,1,0:T(1,128)}, u32[]{:S(2)}) copy-start(f32[1,1,1152]{2,1,0:T(1,128)} %get-tuple-element.88) | copy-start | bytes 13828
  487.7 21.7 %copy-start.25 = (f32[1,1,1152]{2,1,0:T(1,128)S(1)}, f32[1,1,1152]{2,1,0:T(1,128)}, u32[]{:S(2)}) copy-start(f32[1,1,1152]{2,1,0:T(1,128)} %get-tuple-element.89) | copy-start | bytes 13828
  487.7 21.7 %copy-start.26 = (f32[1,1,1152]{2,1,0:T(1,128)S(1)}, f32[1,1,1152]{2,1,0:T(1,128)}, u32[]{:S(2)}) copy-start(f32[1,1,1152]{2,1,0:T(1,128)} %get-tuple-element.90) | copy-start | bytes 13828
  487.7 21.8 %copy-start.5 = (f32[3,6,1152]{2,1,0:T(8,128)S(1)}, f32[3,6,1152]{2,1,0:T(8,128)}, u32[]{:S(2)}) copy-start(f32[3,6,1152]{2,1,0:T(8,128)} %reshape.108.mod_ref.refs_3_) | copy-start | bytes 248836
  487.7 21.9 %copy-start.11 = (bf16[1,1024,1152]{2,1,0:T(8,128)(2,1)S(1)}, bf16[1,1024,1152]{2,1,0:T(8,128)(2,1)}, u32[]{:S(2)}) copy-start(bf16[1,1024,1152]{2,1,0:T(8,128)(2,1)} %get-tuple-element.84.dx1_ref) | copy-start | bytes 7077892
  509.6 3.0 copy-start.1
  512.6 1.7 copy-start.12
  518.2 1.4 copy-start.8
  634.2 3.0 copy-start.2
  637.3 1.7 copy-start.10
  638.9 1.7 copy-start.14
  640.6 3.9 copy-start.7
  640.6 3.9 copy-start.9
  640.6 4.0 copy-start.19
  640.6 4.0 copy-start.20
  652.4 18.4 %copy-start.17 = (f32[3,1152]{1,0:T(4,128)S(1)}, f32[3,1152]{1,0:T(4,128)}, u32[]{:S(2)}) copy-start(f32[3,1152]{1,0:T(4,128)} %cond_ref.1) | copy-start | bytes 41476
  653.8 20.7 %copy-start.18 = (bf16[112,32,1152]{2,1,0:T(8,128)(2,1)S(1)}, bf16[112,32,1152]{2,1,0:T(8,128)(2,1)}, u32[]{:S(2)}) copy-start(bf16[112,32,1152]{2,1,0:T(8,128)(2,1)} %get-tuple-element.121) | copy-start | bytes 24772612

commit v5 on v4

--- a/solution.py
+++ b/solution.py
@@ -71,7 +71,7 @@
     cond = cond_ref[...]
     low = (cond * jax.nn.sigmoid(cond)).astype(BF)
     low_ref[...] = low
-    part = mm(low, w_ref[...]) + bias_ref[...]
+    part = nt(low, w_ref[...]) + bias_ref[...]
     cols = part.shape[1]
     out_ref[me] = jnp.concatenate([part, row_ref[...], jnp.zeros((8 - lat - 1, cols), F32)], 0)
     pl.semaphore_wait(barrier, n_mp - 1)
@@ -96,8 +96,8 @@
         copy.wait_send()
 
 
-def modulation_all(condition, ada_weight, ada_bias, bias_row, n_mp):
-    cols = ada_weight.shape[1]
+def modulation_all(condition, ada_rows, ada_bias, bias_row, n_mp):
+    cols = ada_rows.shape[0]
     vmem = pl.BlockSpec(memory_space=pltpu.VMEM)
     return pl.pallas_call(
         modulation_kernel,
@@ -112,7 +112,7 @@
             collective_id=0, has_side_effects=True, vmem_limit_bytes=40 * MIB
         ),
         name="modulation",
-    )(condition, ada_weight, ada_bias, bias_row)
+    )(condition, ada_rows, ada_bias, bias_row)
 
 
 def attend(flat, n_heads, slot, heads_ref, qkv_ref, lse_ref, between):
@@ -144,6 +144,10 @@
     heads_ref[0, 0] = jnp.concatenate(outs, 0).astype(BF)
 
 
+def as_column(row):
+    return jnp.broadcast_to(row, (8, row.shape[1])).T[:, :1]
+
+
 def mixed_one(lat_ref, mod_ref, h1_ref, h1_all, lat):
     normed, _ = norm_stats(lat_ref[0].astype(F32))
     h1 = (normed * (1.0 + mod_ref[0, 1:2]) + mod_ref[0, 0:1]).astype(BF)
@@ -160,7 +164,7 @@
     def _():
         mixed_one(lat_ref, mod_ref, h1_ref, h1_all, lat)
 
-    flat = nt(w_ref[0], h1_all[lat]) + bias_ref[0]
+    flat = nt(w_ref[0], h1_all[lat]) + as_column(bias_ref[0])
     attend(flat, qkv_ref.shape[1] // 3, slot, heads_ref, qkv_ref, lse_ref, lambda h: None)
 
 
@@ -347,7 +351,7 @@
 
     n_heads = qkv_ref.shape[1] // 3
     weights = w_buf[...].reshape(8 * rows, w_buf.shape[-1])[: 3 * n_heads * HEAD_DIM]
-    flat = nt(weights, h1_all[lat]) + bias_ref[0]
+    flat = nt(weights, h1_all[lat]) + as_column(bias_ref[0])
 
     def between(h):
         tick(step * n_heads + h - 1)
@@ -403,7 +407,7 @@
         in_specs=[
             pl.BlockSpec((1, seq, dim), lambda s, l: (first(s, l), 0, 0)),
             pl.BlockSpec((1, 6, dim), lambda s, l: (l, 0, 0)),
-            pl.BlockSpec((1, 3 * local, 1), lambda s, l: (part(s), 0, 0)),
+            pl.BlockSpec((1, 1, 3 * local), lambda s, l: (part(s), 0, 0)),
         ]
         + [pl.BlockSpec(memory_space=pl.ANY)] * 4,
         out_specs=[
@@ -455,7 +459,7 @@
                 pl.BlockSpec(
                     (1, 3 * local, dim), lambda s, l, me: (lax.rem(me[0] + s, n_mp), 0, 0)
                 ),
-                pl.BlockSpec((1, 3 * local, 1), lambda s, l, me: (lax.rem(me[0] + s, n_mp), 0, 0)),
+                pl.BlockSpec((1, 1, 3 * local), lambda s, l, me: (lax.rem(me[0] + s, n_mp), 0, 0)),
             ],
             out_specs=[
                 pl.BlockSpec(
@@ -647,11 +651,8 @@
 
     part(0, True)
 
-    def body(k, carry):
+    for k in range(1, n_mp):
         part(k, False)
-        return carry
-
-    lax.fori_loop(1, n_mp, body, 0)
     mlp = macc[...] + b2_ref[...]
     out_ref[0] = (x1 + gate_two * mlp).astype(BF)
     dh2 = dacc[...]
@@ -1080,7 +1081,7 @@
     n_heads = lse_ref.shape[1]
     seq = da_ref.shape[1]
     dheads = nt(wp_ref[...], da_ref[0]).reshape(n_heads, HEAD_DIM, seq)
-    heads = heads_ref[0].astype(F32).reshape(n_heads, HEAD_DIM, seq)
+    heads = heads_ref[0, 0].astype(F32).reshape(n_heads, HEAD_DIM, seq)
     scaling = 1.0 / HEAD_DIM**0.5
     dq_list, dk_list, dv_list = [], [], []
     for h in range(n_heads):
@@ -1114,7 +1115,7 @@
     dh1_ref[0] = tn(dqkv, wq_ref[...]).astype(BF)
 
 
-def attn_bwd(da, heads_own, qkv, lse, wp, wq, index, rows):
+def attn_bwd(da, heads, qkv, lse, wp, wq, index, rows):
     lat, seq, dim = da.shape
     n_heads = lse.shape[1]
     local = n_heads * HEAD_DIM
@@ -1127,7 +1128,7 @@
         grid=(1,),
         in_specs=[
             only((seq, dim)),
-            one((local, seq)),
+            pl.BlockSpec((1, 1, local, seq), lambda i: (lax.axis_index("mp"), index, 0, 0)),
             one((3 * n_heads, HEAD_DIM, seq)),
             one((n_heads, seq)),
             whole((local, dim)),
@@ -1141,10 +1142,11 @@
         ],
         compiler_params=pltpu.CompilerParams(vmem_limit_bytes=60 * MIB),
         name="attn_bwd",
-    )(da, heads_own, qkv, lse, wp, wq)
-
-
-def latents_kernel(dh1_ref, dx1_ref, lat_ref, mod_ref, grad_ref, stats_ref):
+    )(da, heads, qkv, lse, wp, wq)
+
+
+def latents_kernel(dh1_ref, dx1_ref, lat_ref, mod_ref, *refs):
+    grad_ref, stats_ref = refs[-2:]
     n1, inv1 = norm_stats(lat_ref[0].astype(F32))
     dh1 = dh1_ref[0].astype(F32)
     grad = dx1_ref[0].astype(F32) + norm_back(n1, inv1, dh1 * (1.0 + mod_ref[0, 1:2]))
@@ -1167,22 +1169,24 @@
         stats_ref[0] += stats
 
 
-def latents_back(dh1, dx1, latents, mod, index, rows):
+def latents_back(dh1, dx1, latents, mod, index, rows, before):
     lat, seq, dim = latents.shape
     tok = pl.BlockSpec((1, rows, dim), lambda t: (index, t, 0))
     new = pl.BlockSpec((1, rows, dim), lambda t: (0, t, 0))
     return pl.pallas_call(
         latents_kernel,
         grid=(seq // rows,),
-        in_specs=[new, new, tok, pl.BlockSpec((1, 6, dim), lambda t: (index, 0, 0))],
-        out_specs=[new, pl.BlockSpec((1, 8, dim), lambda t: (0, 0, 0))],
+        in_specs=[new, new, tok, pl.BlockSpec((1, 6, dim), lambda t: (index, 0, 0))]
+        + [pl.BlockSpec(memory_space=pl.ANY)] * len(before),
+        out_specs=[tok, pl.BlockSpec((1, 8, dim), lambda t: (0, 0, 0))],
         out_shape=[
-            jax.ShapeDtypeStruct((1, seq, dim), BF),
+            jax.ShapeDtypeStruct((lat, seq, dim), BF),
             jax.ShapeDtypeStruct((1, 8, dim), F32),
         ],
-        compiler_params=pltpu.CompilerParams(vmem_limit_bytes=40 * MIB),
+        input_output_aliases={4: 0} if before else {},
+        compiler_params=pltpu.CompilerParams(vmem_limit_bytes=63 * MIB),
         name="latents_back",
-    )(dh1, dx1, latents, mod)
+    )(dh1, dx1, latents, mod, *before)
 
 
 def per_device(
@@ -1215,7 +1219,7 @@
     bias_row = jnp.concatenate([qv_bias.reshape(-1), fc1_bias]).astype(F32)[None]
     ada_row = ada_bias.astype(F32)[None]
     if direct:
-        small, cond_low = modulation_all(condition, ada_weight, ada_row, bias_row, n_mp)
+        small, cond_low = modulation_all(condition, ada_weight.T, ada_row, bias_row, n_mp)
     else:
         cond_low = jax.nn.silu(condition).astype(BF)
         mod_part = mm(cond_low, ada_weight) + ada_row
@@ -1223,7 +1227,7 @@
     mod = small[:, :lat].transpose(1, 0, 2).reshape(lat, 6, dim)
     qv_all = small[:, lat, : 2 * local].reshape(n_mp, 2, local)
     b_qkv = jnp.stack([qv_all[:, 0], jnp.zeros((n_mp, local), F32), qv_all[:, 1]], 1).reshape(
-        n_mp, 3 * local, 1
+        n_mp, 1, 3 * local
     )
     b_fc1 = small[:, lat, 2 * local :].reshape(n_mp, 1, hid)
 
@@ -1249,7 +1253,6 @@
             gather(fc2_weight),
         )
         heads, qkv, lse, h1 = attn_fwd(me, latents, mod, gathered[0], b_qkv, n_mp)
-    heads_own = lax.dynamic_index_in_dim(heads, mp_at, 0, keepdims=False)
     rows = min(256, seq)
     results, dqkv, dh1, bias_sums = [], [], [], []
     for i in range(lat):
@@ -1271,7 +1274,7 @@
             dh1.append(outs[-1])
         results.append(outs[:9])
         dqkv_i, dh1_i, sums_i = attn_bwd(
-            outs[2], heads_own, qkv, lse, proj_weight, wq_own, i, min(512, seq)
+            outs[2], heads, qkv, lse, proj_weight, wq_own, i, min(512, seq)
         )
         dqkv.append(dqkv_i)
         bias_sums.append(sums_i)
@@ -1310,17 +1313,19 @@
         grad_fc2 = tn(flat(z), flat(dm))
         grad_fc1 = tn(flat(h2), flat(du))
         grad_qkv = sum(mm(dqkv[i][0], h1[i]) for i in range(lat))
+        heads_own = lax.dynamic_index_in_dim(heads, mp_at, 0, keepdims=False)
         grad_proj = sum(mm(heads_own[i], da[i][0]) for i in range(lat))
         grads = [grad.astype(BF) for grad in (grad_fc1, grad_fc2, grad_qkv, grad_proj)]
         grad_fc1, grad_fc2, grad_qkv, grad_proj = lax.psum(grads, "dp")
         biases = lax.psum((grad_fc1_bias, grad_fc2_bias, grad_proj_bias, grad_qv_bias), "dp")
         grad_fc1_bias, grad_fc2_bias, grad_proj_bias, grad_qv_bias = biases
 
-    backs = [
-        latents_back(dh1[i], results[i][1], latents, mod, i, rows) for i in range(lat)
-    ]
-    latents_grad = jnp.concatenate([grad for grad, _ in backs], 0)
-    stats_one = jnp.concatenate([stats for _, stats in backs], 0)
+    before, stats_one = [], []
+    for i in range(lat):
+        latents_grad, stats = latents_back(dh1[i], results[i][1], latents, mod, i, rows, before)
+        before = [latents_grad]
+        stats_one.append(stats)
+    stats_one = jnp.concatenate(stats_one, 0)
 
     dmod = jnp.stack(
         [

time: 692 us -> 665 us (0.961)
  local copies, waits for them, and re-layouts: 45.8 us -> 17.1 us
    unnamed x58 -> x31, local copies, waits for them, and re-layouts: 30.3 us -> 2.93 us
    pallas_call x3, Pallas kernels: 252 us -> 240 us  [mlp_both(): pl.pallas_call(functools.partial(mlp_kernel, summing=summing), grid=(seq...]
    pallas_call x3, Pallas kernels: 12.1 us -> 21.5 us  [latents_back(): pl.pallas_call(latents_kernel, grid=(seq // rows,), in_specs=[new, new, t...]
where the time goes in v5:
time: 665 us; the launch traced here: 655 us
  Pallas kernels  608 us (91%)
  other arithmetic  21.1 us (3%)
  local copies, waits for them, and re-layouts  17.1 us (3%)
  matrix products  7.25 us (1%)
    pallas_call x3, Pallas kernels, mlp_both(): pl.pallas_call(functools.partial(mlp_kernel, summing=summing), grid=(seq...  240 us
    pallas_call x1, Pallas kernels, attn_gather(): pl.pallas_call(attn_gather_kernel, grid=(n_mp, lat), in_specs=[pl.BlockSp...  150 us
    pallas_call x1, Pallas kernels, tail_sums(): pl.pallas_call(functools.partial(tail_kernel, lats=lats), in_specs=[vmem,...  114 us
    pallas_call x3, Pallas kernels, attn_bwd(): pl.pallas_call(functools.partial(attn_bwd_kernel, rows=rows), grid=(1,),...  59.6 us
    pallas_call x3, Pallas kernels, latents_back(): pl.pallas_call(latents_kernel, grid=(seq // rows,), in_specs=[new, new, t...  21.5 us

profile of v5, /device:TPU:0, one launch (start us, length us, event | category | flops | bytes accessed | tf_op | source)
XLA Modules:
  0.0 654.6 jit_solution(10775794411131551611)
XLA Ops:
  1.3 0.8 concatenate.27
  2.9 2.1 copy-done
  5.0 0.7 copy-done.1
  5.7 10.4 %modulation.1 = (f32[4,8,1728]{2,1,0:T(8,128)S(1)}, bf16[3,1152]{1,0:T(4,128)(2,1)S(1)}) custom-call(f32[3,1152]{1,0:T(4,128)S(1)} %copy-done.1, bf16[1728,1152]{1,0:T(8,128)(2,1)S(1)} %bitcast.35, f32[1,1728]{1,0:T(1,128)S(1)} %reshape.117.bias_ref, f32[1,1728]{1,0:T(1,128)S(1)} %maximum_convert_fusion.row_ref), custom_call_target="tpu_custom_call" | custom-call | tf_op jit(solution)/shard_map/modulation/pallas_call | solution.py:102
  16.2 0.8 reshape.108.mod_ref.refs_3_
  17.9 149.8 %attn_gather.1 = (bf16[4,3,288,1024]{3,2,1,0:T(8,128)(2,1)}, bf16[3,12,72,1024]{3,2,1,0:T(8,128)(2,1)}, f32[3,4,1024]{2,1,0:T(4,128)}, bf16[3,1024,1152]{2,1,0:T...) custom-call(bf16[3,1024,1152]{2,1,0:T(8,128)(2,1)} %lat_ref.7, f32[3,6,1152]{2,1,0:T(8,128)} %reshape.108.mod_ref.refs_3_, ...), custom_call_target="tpu_custom_call" | custom-call | tf_op jit(solution)/shard_map/attn_gather/pallas_call | solution.py:404
  169.6 73.9 %mlp_both.1 = (bf16[1,1024,1152]{2,1,0:T(8,128)(2,1)}, bf16[1,1024,1152]{2,1,0:T(8,128)(2,1)}, bf16[1,1024,1152]{2,1,0:T(8,128)(2,1)}, bf16[1,1024,1152]{2,1,0:T...) custom-call(bf16[4,3,288,1024]{3,2,1,0:T(8,128)(2,1)} %get-tuple-ele, ...), custom_call_target="tpu_custom_call" | custom-call | tf_op jit(solution)/shard_map/mlp_both/pallas_call | solution.py:716
  243.5 19.8 %attn_bwd.3 = (bf16[1,864,1024]{2,1,0:T(8,128)(2,1)}, bf16[1,1024,1152]{2,1,0:T(8,128)(2,1)}, f32[1,864,1]{2,1,0:T(8,128)}) custom-call(bf16[1,1024,1152]{2,1,0:T(8,128)(2,1)} %get-tuple-element.72.da_ref.refs_19_, bf16[4,3,288,1024]{3,2,1,0:T(8,128)(2,1)} %get-tuple-element.69.refs_0_.heads_ref.refs_2_, ...), custom_call_target="tpu_custom_call" | custom-call | tf_op jit(solution)/shard_map/attn_bwd/pallas_call | solution.py:1126
  263.3 83.9 %mlp_sum.2 = (bf16[1,1024,1152]{2,1,0:T(8,128)(2,1)}, bf16[1,1024,1152]{2,1,0:T(8,128)(2,1)}, bf16[1,1024,1152]{2,1,0:T(8,128)(2,1)}, bf16[1,1024,1152]{2,1,0:T(...) custom-call(bf16[4,3,288,1024]{3,2,1,0:T(8,128)(2,1)} %get-tuple-ele, ...), custom_call_target="tpu_custom_call" | custom-call | tf_op jit(solution)/shard_map/mlp_sum/pallas_call | solution.py:716
  347.2 19.8 %attn_bwd.4 = (bf16[1,864,1024]{2,1,0:T(8,128)(2,1)}, bf16[1,1024,1152]{2,1,0:T(8,128)(2,1)}, f32[1,864,1]{2,1,0:T(8,128)}) custom-call(bf16[1,1024,1152]{2,1,0:T(8,128)(2,1)} %get-tuple-element.77.da_ref.refs_20_, bf16[4,3,288,1024]{3,2,1,0:T(8,128)(2,1)} %get-tuple-element.69.refs_0_.heads_ref.refs_2_, ...), custom_call_target="tpu_custom_call" | custom-call | tf_op jit(solution)/shard_map/attn_bwd/pallas_call | solution.py:1126
  367.0 81.9 %mlp_sum.3 = (bf16[1,1024,1152]{2,1,0:T(8,128)(2,1)}, bf16[1,1024,1152]{2,1,0:T(8,128)(2,1)}, bf16[1,1024,1152]{2,1,0:T(8,128)(2,1)}, bf16[1,1024,1152]{2,1,0:T(...) custom-call(bf16[4,3,288,1024]{3,2,1,0:T(8,128)(2,1)} %get-tuple-ele, ...), custom_call_target="tpu_custom_call" | custom-call | tf_op jit(solution)/shard_map/mlp_sum/pallas_call | solution.py:716
  449.7 0.8 constant_dynamic-update-slice_fusion
  450.5 1.1 fusion.22
  451.6 20.1 %attn_bwd.5 = (bf16[1,864,1024]{2,1,0:T(8,128)(2,1)}, bf16[1,1024,1152]{2,1,0:T(8,128)(2,1)}, f32[1,864,1]{2,1,0:T(8,128)}) custom-call(bf16[1,1024,1152]{2,1,0:T(8,128)(2,1)} %get-tuple-element.80.da_ref.refs_21_, bf16[4,3,288,1024]{3,2,1,0:T(8,128)(2,1)} %get-tuple-element.69.refs_0_.heads_ref.refs_2_, ...), custom_call_target="tpu_custom_call" | custom-call | tf_op jit(solution)/shard_map/attn_bwd/pallas_call | solution.py:1126
  471.7 1.1 add_convert_fusion
  473.1 0.8 fusion.8
  473.8 114.4 %tail_sums.1 = (bf16[1,1024,1152]{2,1,0:T(8,128)(2,1)}, bf16[112,32,1152]{2,1,0:T(8,128)(2,1)}) custom-call(bf16[1,1024,1152]{2,1,0:T(8,128)(2,1)} %get-tuple-element.81.refs_0_, bf16[4,32,1152]{2,1,0:T(8,128)(2,1)} %bitcast.53, bf16[4,3,288,1024]{3,2,1,0:T(8,128)(2,1)} %get-tuple-element.69.refs_0_.heads_ref.refs_2_, ...), custom_call_target="tpu_custom_call" | custom-call | tf_op jit(solution)/shard_map/tail_sums/pallas_call | solution.py:991
  588.2 3.0 fusion.24
  591.2 5.2 bitcast_convert_fusion
  596.4 7.1 %latents_back.3 = (bf16[3,1024,1152]{2,1,0:T(8,128)(2,1)}, f32[1,8,1152]{2,1,0:T(8,128)}) custom-call(bf16[1,1024,1152]{2,1,0:T(8,128)(2,1)} %get-tuple-element.111.dh1_ref, bf16[1,1024,1152]{2,1,0:T(8,128)(2,1)} %get-tuple-element.112.dx1_ref, bf16[3,1024,1152]{2,1,0:T(8,128)(2,1)} %lat_ref.7, f32[3,6,1152]{2,1,0:T(8,128)} %reshape.108.mod_ref.refs_3_), custom_call_target="tpu_custom_call" | custom-call | tf_op jit(solution)/shard_map/latents_back/pallas_call | solution.py:1176
  603.5 7.1 %latents_back.4 = (bf16[3,1024,1152]{2,1,0:T(8,128)(2,1)}, f32[1,8,1152]{2,1,0:T(8,128)}) custom-call(bf16[1,1024,1152]{2,1,0:T(8,128)(2,1)} %get-tuple-element.109.dh1_ref, bf16[1,1024,1152]{2,1,0:T(8,128)(2,1)} %get-tuple-element.110.dx1_ref, bf16[3,1024,1152]{2,1,0:T(8,128)(2,1)} %lat_ref.7, ...), custom_call_target="tpu_custom_call", output_to_operand_aliasing={{0}: (4, {})} | custom-call | tf_op jit(solution)/shard_map/latents_back/pallas_call | solution.py:1176
  610.7 7.2 %latents_back.5 = (bf16[3,1024,1152]{2,1,0:T(8,128)(2,1)}, f32[1,8,1152]{2,1,0:T(8,128)}) custom-call(bf16[1,1024,1152]{2,1,0:T(8,128)(2,1)} %get-tuple-element.107.dh1_ref, bf16[1,1024,1152]{2,1,0:T(8,128)(2,1)} %get-tuple-element.108.dx1_ref, bf16[3,1024,1152]{2,1,0:T(8,128)(2,1)} %lat_ref.7, ...), custom_call_target="tpu_custom_call", output_to_operand_aliasing={{0}: (4, {})} | custom-call | tf_op jit(solution)/shard_map/latents_back/pallas_call | solution.py:1176
  617.9 0.8 convert.54
  618.9 2.8 fusion.26
  621.7 12.6 %rows_exchange.1 = (bf16[8,16,2880]{2,1,0:T(8,128)(2,1)S(1)}, f32[8,1152]{1,0:T(8,128)S(1)}) custom-call(bf16[16,2880]{1,0:T(8,128)(2,1)S(1)} %fusion.15.rows_ref, f32[8,1152]{1,0:T(8,128)S(1)} %pad.20.act_ref), custom_call_target="tpu_custom_call" | custom-call | tf_op jit(solution)/shard_map/rows_exchange/pallas_call | solution.py:1061
  634.2 4.5 fusion.4
  640.0 1.7 slice.107
  641.7 2.2 convert_bitcast_fusion
  643.9 1.3 slice.110
  645.2 1.2 bitcast_convert_fusion.2
  646.4 0.7 slice_convert_fusion.1
  648.5 5.9 pad_maximum_fusion
  (65 shorter events, 8.3 us)
Async XLA Ops:
  2.9 2.1 copy-start
  5.0 0.7 copy-start.1
  17.9 150.5 %copy-start.12 = (bf16[1152]{0:T(1024)(128)(2,1)S(1)}, bf16[1152]{0:T(1024)(128)(2,1)}, u32[]{:S(2)}) copy-start(bf16[1152]{0:T(1024)(128)(2,1)} %param.19) | copy-start | bytes 6916
  17.9 151.1 %copy-start.13 = (bf16[1152]{0:T(1024)(128)(2,1)S(1)}, bf16[1152]{0:T(1024)(128)(2,1)}, u32[]{:S(2)}) copy-start(bf16[1152]{0:T(1024)(128)(2,1)} %param.23) | copy-start | bytes 6916
  367.0 81.9 %copy-start.10 = (f32[1,1,1152]{2,1,0:T(1,128)S(1)}, f32[1,1,1152]{2,1,0:T(1,128)}, u32[]{:S(2)}) copy-start(f32[1,1,1152]{2,1,0:T(1,128)} %get-tuple-element.82) | copy-start | bytes 13828
  367.0 82.0 %copy-start.11 = (f32[1,1,1152]{2,1,0:T(1,128)S(1)}, f32[1,1,1152]{2,1,0:T(1,128)}, u32[]{:S(2)}) copy-start(f32[1,1,1152]{2,1,0:T(1,128)} %get-tuple-element.83) | copy-start | bytes 13828
  367.0 82.7 %copy-start.6 = (f32[1,8,1152]{2,1,0:T(8,128)S(1)}, f32[1,8,1152]{2,1,0:T(8,128)}, u32[]{:S(2)}) copy-start(f32[1,8,1152]{2,1,0:T(8,128)} %get-tuple-element.85) | copy-start | bytes 110596
  367.0 82.7 %copy-start.7 = (f32[1,8,1152]{2,1,0:T(8,128)S(1)}, f32[1,8,1152]{2,1,0:T(8,128)}, u32[]{:S(2)}) copy-start(f32[1,8,1152]{2,1,0:T(8,128)} %get-tuple-element.86) | copy-start | bytes 110596
  451.6 20.1 %copy-start.4 = (f32[1,864,1]{2,1,0:T(8,128)S(1)}, f32[1,864,1]{2,1,0:T(8,128)}, u32[]{:S(2)}) copy-start(f32[1,864,1]{2,1,0:T(8,128)} %get-tuple-element.88) | copy-start | bytes 10372
  451.6 20.1 %copy-start.5 = (f32[1,864,1]{2,1,0:T(8,128)S(1)}, f32[1,864,1]{2,1,0:T(8,128)}, u32[]{:S(2)}) copy-start(f32[1,864,1]{2,1,0:T(8,128)} %get-tuple-element.89) | copy-start | bytes 10372
  610.7 7.9 %copy-start.9 = (f32[1,8,1152]{2,1,0:T(8,128)S(1)}, f32[1,8,1152]{2,1,0:T(8,128)}, u32[]{:S(2)}) copy-start(f32[1,8,1152]{2,1,0:T(8,128)} %get-tuple-element.118) | copy-start | bytes 110596
  610.7 8.0 %copy-start.8 = (f32[1,8,1152]{2,1,0:T(8,128)S(1)}, f32[1,8,1152]{2,1,0:T(8,128)}, u32[]{:S(2)}) copy-start(f32[1,8,1152]{2,1,0:T(8,128)} %get-tuple-element.117) | copy-start | bytes 110596
  634.2 4.5 copy-start.2
  643.9 4.5 copy-start.3

commit v6 on v5

--- a/solution.py
+++ b/solution.py
@@ -61,58 +61,13 @@
     return {"device_id": (dp_at, mp_at), "device_id_type": pl.DeviceIdType.MESH}
 
 
-def modulation_kernel(cond_ref, w_ref, bias_ref, row_ref, out_ref, low_ref, send, recv):
-    dp_at, me = lax.axis_index("dp"), lax.axis_index("mp")
-    n_mp = out_ref.shape[0]
-    lat = cond_ref.shape[0]
-    barrier = pltpu.get_barrier_semaphore()
-    for k in range(1, n_mp):
-        pl.semaphore_signal(barrier, inc=1, **at_mesh(dp_at, (me + k) % n_mp))
-    cond = cond_ref[...]
-    low = (cond * jax.nn.sigmoid(cond)).astype(BF)
-    low_ref[...] = low
-    part = nt(low, w_ref[...]) + bias_ref[...]
-    cols = part.shape[1]
-    out_ref[me] = jnp.concatenate([part, row_ref[...], jnp.zeros((8 - lat - 1, cols), F32)], 0)
-    pl.semaphore_wait(barrier, n_mp - 1)
-    copies = []
-    for k in range(1, n_mp):
-        copies.append(
-            pltpu.make_async_remote_copy(
-                out_ref.at[me],
-                out_ref.at[me],
-                send.at[k - 1],
-                recv.at[k - 1],
-                **at_mesh(dp_at, (me + k) % n_mp),
-            )
-        )
-        copies[-1].start()
-    for k in range(1, n_mp):
-        came = out_ref.at[(me + n_mp - k) % n_mp]
-        pltpu.make_async_remote_copy(
-            came, came, send.at[k - 1], recv.at[k - 1], **at_mesh(dp_at, (me + k) % n_mp)
-        ).wait_recv()
-    for copy in copies:
-        copy.wait_send()
-
-
-def modulation_all(condition, ada_rows, ada_bias, bias_row, n_mp):
-    cols = ada_rows.shape[0]
-    vmem = pl.BlockSpec(memory_space=pltpu.VMEM)
-    return pl.pallas_call(
-        modulation_kernel,
-        in_specs=[vmem] * 4,
-        out_specs=[vmem, vmem],
-        out_shape=[
-            jax.ShapeDtypeStruct((n_mp, 8, cols), F32),
-            jax.ShapeDtypeStruct(condition.shape, BF),
-        ],
-        scratch_shapes=[pltpu.SemaphoreType.DMA((n_mp - 1,))] * 2,
-        compiler_params=pltpu.CompilerParams(
-            collective_id=0, has_side_effects=True, vmem_limit_bytes=40 * MIB
-        ),
-        name="modulation",
-    )(condition, ada_rows, ada_bias, bias_row)
+def modulation_start(dp_at, me, n_mp, small, sems):
+    def copy(k, arrived=False):
+        at = small.at[(me + n_mp - k) % n_mp if arrived else me]
+        target = at_mesh(dp_at, (me + k) % n_mp)
+        return pltpu.make_async_remote_copy(at, at, sems.at[0, k - 1], sems.at[1, k - 1], **target)
+
+    return copy
 
 
 def attend(flat, n_heads, slot, heads_ref, qkv_ref, lse_ref, between):
@@ -148,9 +103,9 @@
     return jnp.broadcast_to(row, (8, row.shape[1])).T[:, :1]
 
 
-def mixed_one(lat_ref, mod_ref, h1_ref, h1_all, lat):
+def mixed_one(lat_ref, shift, scale, h1_ref, h1_all, lat):
     normed, _ = norm_stats(lat_ref[0].astype(F32))
-    h1 = (normed * (1.0 + mod_ref[0, 1:2]) + mod_ref[0, 0:1]).astype(BF)
+    h1 = (normed * (1.0 + scale) + shift).astype(BF)
     h1_all[lat] = h1
     h1_ref[0] = h1
 
@@ -162,7 +117,7 @@
 
     @pl.when(slot == 0)
     def _():
-        mixed_one(lat_ref, mod_ref, h1_ref, h1_all, lat)
+        mixed_one(lat_ref, mod_ref[0, 0:1], mod_ref[0, 1:2], h1_ref, h1_all, lat)
 
     flat = nt(w_ref[0], h1_all[lat]) + as_column(bias_ref[0])
     attend(flat, qkv_ref.shape[1] // 3, slot, heads_ref, qkv_ref, lse_ref, lambda h: None)
@@ -170,8 +125,9 @@
 
 def attn_gather_kernel(
     lat_ref,
-    mod_ref,
-    bias_ref,
+    cond_ref,
+    rows_ref,
+    ada_ref,
     wq_ref,
     wp_ref,
     w1_ref,
@@ -180,15 +136,20 @@
     qkv_ref,
     lse_ref,
     h1_ref,
+    small_ref,
+    low_ref,
     all_ref,
     h1_all,
     w_buf,
+    ada_buf,
+    small,
     local_sem,
     z_own,
     z_on,
     z_got,
     sends,
     recvs,
+    small_sems,
 ):
     n_mp = all_ref.shape[0]
     lats = h1_all.shape[0]
@@ -295,6 +256,9 @@
             pl.when(dp_at < upper)(lambda: send_from(0, wq_ref, dp_at))
             pl.when(dp_at >= upper)(lambda: send_from(0, wp_ref, dp_at - upper))
 
+    small_copy = modulation_start(dp_at, me, n_mp, small, small_sems)
+    ada_load = lambda: pltpu.make_async_copy(ada_ref, ada_buf, local_sem.at[8])
+
     @pl.when(step == 0)
     def _():
         barrier = pltpu.get_barrier_semaphore()
@@ -309,8 +273,23 @@
         def _():
             pl.semaphore_signal(barrier, inc=1, **left_id)
 
-        pl.semaphore_wait(barrier, 3 + line_peers(me, n_mp))
+        for k in range(1, n_mp):
+            pl.semaphore_signal(barrier, inc=1, **at_mesh(dp_at, (me + k) % n_mp))
+        ada_load().start()
+        pl.semaphore_wait(barrier, 3 + line_peers(me, n_mp) + n_mp - 1)
         send_own(0)
+        cond = cond_ref[...]
+        low = (cond * jax.nn.sigmoid(cond)).astype(BF)
+        low_ref[...] = low
+        ada_load().wait()
+        part = nt(low, ada_buf[...]) + rows_ref[0:1]
+        pad = jnp.zeros((8 - lats - 1, part.shape[1]), F32)
+        small[me] = jnp.concatenate([part, rows_ref[1:2], pad], 0)
+        for k in range(1, n_mp):
+            small_copy(k).start()
+        for k in range(1, n_mp):
+            small_copy(k, True).wait_recv()
+        small_ref[...] = small[...]
 
     def next_weights(k):
         return pltpu.make_async_copy(all_ref.at[near_part(me, k), 0], w_buf, local_sem.at[0])
@@ -345,13 +324,22 @@
     def _():
         next_weights(slot).wait()
 
+    n_heads = qkv_ref.shape[1] // 3
+    local = n_heads * HEAD_DIM
+
     @pl.when(slot == 0)
     def _():
-        mixed_one(lat_ref, mod_ref, h1_ref, h1_all, lat)
-
-    n_heads = qkv_ref.shape[1] // 3
-    weights = w_buf[...].reshape(8 * rows, w_buf.shape[-1])[: 3 * n_heads * HEAD_DIM]
-    flat = nt(weights, h1_all[lat]) + as_column(bias_ref[0])
+        dim, cols = h1_all.shape[2], small.shape[2]
+        shift = small[0, pl.ds(lat, 1), :dim]
+        scale = jnp.concatenate(
+            [small[0, pl.ds(lat, 1), dim:], small[1, pl.ds(lat, 1), : 2 * dim - cols]], 1
+        )
+        mixed_one(lat_ref, shift, scale, h1_ref, h1_all, lat)
+
+    weights = w_buf[...].reshape(8 * rows, w_buf.shape[-1])[: 3 * local]
+    biases = as_column(small[near_part(me, slot), lats : lats + 1, : 2 * local])
+    bias = jnp.concatenate([biases[:local], jnp.zeros((local, 1), F32), biases[local:]], 0)
+    flat = nt(weights, h1_all[lat]) + bias
 
     def between(h):
         tick(step * n_heads + h - 1)
@@ -369,6 +357,8 @@
             return carry
 
         lax.fori_loop(n_mp * lats * n_heads, pace * units + 11, rest, 0)
+        for k in range(1, n_mp):
+            small_copy(k).wait_send()
         for c in range(3):
 
             @pl.when(me < n_mp - 1)
@@ -393,53 +383,63 @@
         lax.fori_loop(0, units, drain, 0)
 
 
-def attn_gather(latents, mod, bias, own, n_mp):
+def attn_gather(latents, condition, small_rows, ada_rows, own, n_mp):
     lat, seq, dim = latents.shape
     local = dim // n_mp
     n_heads = local // HEAD_DIM
     rows = dim // 8
+    cols = ada_rows.shape[0]
     last = lat - 1
-    first = lambda s, l: s // n_mp * 0 + jnp.where(s == 0, l, last)
+    first = lambda s, l: jnp.where(s == 0, l, last)
     part = lambda s: near_part(lax.axis_index("mp"), s)
-    heads, qkv, lse, h1, gathered = pl.pallas_call(
+    whole = lambda shape: pl.BlockSpec(shape, lambda s, l: (0,) * len(shape))
+    any_spec = pl.BlockSpec(memory_space=pl.ANY)
+    heads, qkv, lse, h1, small, cond_low, gathered = pl.pallas_call(
         attn_gather_kernel,
         grid=(n_mp, lat),
         in_specs=[
             pl.BlockSpec((1, seq, dim), lambda s, l: (first(s, l), 0, 0)),
-            pl.BlockSpec((1, 6, dim), lambda s, l: (l, 0, 0)),
-            pl.BlockSpec((1, 1, 3 * local), lambda s, l: (part(s), 0, 0)),
+            whole(condition.shape),
+            whole(small_rows.shape),
         ]
-        + [pl.BlockSpec(memory_space=pl.ANY)] * 4,
+        + [any_spec] * 5,
         out_specs=[
             pl.BlockSpec((1, 1, local, seq), lambda s, l: (part(s), l, 0, 0)),
             pl.BlockSpec((1, 3 * n_heads, HEAD_DIM, seq), lambda s, l: (first(s, l), 0, 0, 0)),
             pl.BlockSpec((1, n_heads, seq), lambda s, l: (first(s, l), 0, 0)),
             pl.BlockSpec((1, seq, dim), lambda s, l: (first(s, l), 0, 0)),
-            pl.BlockSpec(memory_space=pl.ANY),
+            whole((n_mp, 8, cols)),
+            whole(condition.shape),
+            any_spec,
         ],
         out_shape=[
             jax.ShapeDtypeStruct((n_mp, lat, local, seq), BF),
             jax.ShapeDtypeStruct((lat, 3 * n_heads, HEAD_DIM, seq), BF),
             jax.ShapeDtypeStruct((lat, n_heads, seq), F32),
             jax.ShapeDtypeStruct((lat, seq, dim), BF),
+            jax.ShapeDtypeStruct((n_mp, 8, cols), F32),
+            jax.ShapeDtypeStruct(condition.shape, BF),
             jax.ShapeDtypeStruct((n_mp, 3, 2, 2, 2, rows, dim), BF),
         ],
         scratch_shapes=[
             pltpu.VMEM((lat, seq, dim), BF),
             pltpu.VMEM((2, 2, 2, rows, dim), BF),
-            pltpu.SemaphoreType.DMA((8,)),
+            pltpu.VMEM(ada_rows.shape, BF),
+            pltpu.VMEM((n_mp, 8, cols), F32),
+            pltpu.SemaphoreType.DMA((9,)),
             pltpu.SemaphoreType.DMA((2, 3)),
             pltpu.SemaphoreType.DMA((3, n_mp)),
             pltpu.SemaphoreType.DMA((3, n_mp)),
             pltpu.SemaphoreType.DMA((5, 3, n_mp)),
             pltpu.SemaphoreType.DMA((5, 3, n_mp)),
+            pltpu.SemaphoreType.DMA((2, n_mp - 1)),
         ],
         compiler_params=pltpu.CompilerParams(
-            collective_id=1, has_side_effects=True, vmem_limit_bytes=60 * MIB
+            collective_id=1, has_side_effects=True, vmem_limit_bytes=62 * MIB
         ),
         name="attn_gather",
-    )(latents, mod, bias, *own)
-    return heads, qkv, lse, h1, gathered.reshape(n_mp, 3, dim, dim)
+    )(latents, condition, small_rows, ada_rows, *own)
+    return heads, qkv, lse, h1, small, cond_low, gathered.reshape(n_mp, 3, dim, dim)
 
 
 def attn_fwd(me, latents, mod, gathered, bias, n_mp):
@@ -485,7 +485,8 @@
 
 
 class LineSum:
-    def __init__(self, own_ref, up, down, sems, out_ref):
+    def __init__(self, own_ref, up, down, sems, out_ref, lag=2):
+        self.lag = lag
         self.own, self.up, self.down, self.sems, self.out = own_ref, up, down, sems, out_ref
         self.count, self.rows = up.shape[0], up.shape[1]
         self.me = lax.axis_index("mp")
@@ -533,7 +534,7 @@
 
     def tick(self, t):
         for side in (0, 1):
-            at = t - 2 * self.place[side]
+            at = t - self.lag * self.place[side]
 
             @pl.when((at >= 0) & (at % 3 < 2) & (at - at // 3 < self.count))
             def _():
@@ -541,7 +542,7 @@
 
     def finish(self, ticks):
         for side in (0, 1):
-            done = jnp.maximum(ticks - 2 * self.place[side], 0)
+            done = jnp.maximum(ticks - self.lag * self.place[side], 0)
             done = jnp.minimum(done - done // 3, self.count)
 
             def late(c, carry):
@@ -929,7 +930,7 @@
     refs = refs[6 + 6 * lats :]
     up, down, line_sems, terms, full, halves, firsts, seconds, cube_sems = refs[:9]
     right, left_cols, left_rows, right_sems, left_sems, local_sem = refs[9:]
-    line = LineSum(part_ref, up, down, line_sems, sum_ref)
+    line = LineSum(part_ref, up, down, line_sems, sum_ref, 3)
     cube = CubeSum(terms, full, halves, firsts, seconds, cube_sems)
     heads = [heads_ref.at[line.me, i] for i in range(lats)]
     h1s = [h1_ref.at[i] for i in range(lats)]
@@ -1145,48 +1146,44 @@
     )(da, heads, qkv, lse, wp, wq)
 
 
-def latents_kernel(dh1_ref, dx1_ref, lat_ref, mod_ref, *refs):
-    grad_ref, stats_ref = refs[-2:]
+def latents_kernel(*refs, lats):
+    lat_ref, mod_ref = refs[:2]
+    dh1_refs, dx1_refs, out_refs = [refs[2 + i * lats : 2 + (i + 1) * lats] for i in range(3)]
+    grad_ref, stats_ref, out_ref = refs[2 + 3 * lats :]
+    lat, step = pl.program_id(0), pl.program_id(1)
     n1, inv1 = norm_stats(lat_ref[0].astype(F32))
-    dh1 = dh1_ref[0].astype(F32)
-    grad = dx1_ref[0].astype(F32) + norm_back(n1, inv1, dh1 * (1.0 + mod_ref[0, 1:2]))
-    grad_ref[0] = grad.astype(BF)
-    stats = jnp.concatenate(
-        [
-            jnp.sum(dh1, 0, keepdims=True),
-            jnp.sum(dh1 * n1, 0, keepdims=True),
-            jnp.zeros((6, dh1.shape[1]), F32),
-        ],
-        0,
-    )
-
-    @pl.when(pl.program_id(0) == 0)
-    def _():
-        stats_ref[0] = stats
-
-    @pl.when(pl.program_id(0) > 0)
-    def _():
-        stats_ref[0] += stats
-
-
-def latents_back(dh1, dx1, latents, mod, index, rows, before):
+    for i in range(lats):
+
+        @pl.when(lat == i)
+        def _():
+            dh1 = dh1_refs[i][0].astype(F32)
+            back = norm_back(n1, inv1, dh1 * (1.0 + mod_ref[0, 1:2]))
+            grad_ref[0] = (dx1_refs[i][0].astype(F32) + back).astype(BF)
+            out_ref[0] = out_refs[i][0]
+            pad = jnp.zeros((6, dh1.shape[1]), F32)
+            sums = [jnp.sum(dh1, 0, keepdims=True), jnp.sum(dh1 * n1, 0, keepdims=True), pad]
+            stats_ref[0] = jnp.where(step == 0, 0.0, stats_ref[0]) + jnp.concatenate(sums, 0)
+
+
+def latents_back(dh1, dx1, outs, latents, mod, rows):
     lat, seq, dim = latents.shape
-    tok = pl.BlockSpec((1, rows, dim), lambda t: (index, t, 0))
-    new = pl.BlockSpec((1, rows, dim), lambda t: (0, t, 0))
+    steps = seq // rows
+    tok = pl.BlockSpec((1, rows, dim), lambda l, t: (l, t, 0))
+    at = lambda i: (lambda l, t: (0, jnp.where(l < i, 0, jnp.where(l == i, t, steps - 1)), 0))
+    each = [pl.BlockSpec((1, rows, dim), at(i)) for i in range(lat)]
     return pl.pallas_call(
-        latents_kernel,
-        grid=(seq // rows,),
-        in_specs=[new, new, tok, pl.BlockSpec((1, 6, dim), lambda t: (index, 0, 0))]
-        + [pl.BlockSpec(memory_space=pl.ANY)] * len(before),
-        out_specs=[tok, pl.BlockSpec((1, 8, dim), lambda t: (0, 0, 0))],
+        functools.partial(latents_kernel, lats=lat),
+        grid=(lat, steps),
+        in_specs=[tok, pl.BlockSpec((1, 6, dim), lambda l, t: (l, 0, 0))] + each * 3,
+        out_specs=[tok, pl.BlockSpec((1, 8, dim), lambda l, t: (l, 0, 0)), tok],
         out_shape=[
             jax.ShapeDtypeStruct((lat, seq, dim), BF),
-            jax.ShapeDtypeStruct((1, 8, dim), F32),
+            jax.ShapeDtypeStruct((lat, 8, dim), F32),
+            jax.ShapeDtypeStruct((lat, seq, dim), BF),
         ],
-        input_output_aliases={4: 0} if before else {},
         compiler_params=pltpu.CompilerParams(vmem_limit_bytes=63 * MIB),
         name="latents_back",
-    )(dh1, dx1, latents, mod, *before)
+    )(latents, mod, *dh1, *dx1, *outs)
 
 
 def per_device(
@@ -1218,27 +1215,26 @@
     direct = n_mp == 4 and n_dp == 8
     bias_row = jnp.concatenate([qv_bias.reshape(-1), fc1_bias]).astype(F32)[None]
     ada_row = ada_bias.astype(F32)[None]
+    wq_own = (
+        qkv_weight.reshape(dim, 3, n_heads, HEAD_DIM).transpose(1, 2, 3, 0).reshape(3 * local, dim)
+    )
     if direct:
-        small, cond_low = modulation_all(condition, ada_weight.T, ada_row, bias_row, n_mp)
+        own = (wq_own, proj_weight, fc1_weight, fc2_weight)
+        small_rows = jnp.concatenate([ada_row, bias_row], 0)
+        heads, qkv, lse, h1, small, cond_low, gathered = attn_gather(
+            latents, condition, small_rows, ada_weight.T, own, n_mp
+        )
+        gathered = (gathered,) * 3
     else:
         cond_low = jax.nn.silu(condition).astype(BF)
         mod_part = mm(cond_low, ada_weight) + ada_row
         small = lax.all_gather(jnp.concatenate([mod_part, bias_row], 0), "mp", axis=0)
     mod = small[:, :lat].transpose(1, 0, 2).reshape(lat, 6, dim)
-    qv_all = small[:, lat, : 2 * local].reshape(n_mp, 2, local)
-    b_qkv = jnp.stack([qv_all[:, 0], jnp.zeros((n_mp, local), F32), qv_all[:, 1]], 1).reshape(
-        n_mp, 1, 3 * local
-    )
     b_fc1 = small[:, lat, 2 * local :].reshape(n_mp, 1, hid)
-
-    wq_own = (
-        qkv_weight.reshape(dim, 3, n_heads, HEAD_DIM).transpose(1, 2, 3, 0).reshape(3 * local, dim)
-    )
-    if direct:
-        own = (wq_own, proj_weight, fc1_weight, fc2_weight)
-        heads, qkv, lse, h1, gathered = attn_gather(latents, mod, b_qkv, own, n_mp)
-        gathered = (gathered,) * 3
-    else:
+    if not direct:
+        qv_all = small[:, lat, : 2 * local].reshape(n_mp, 2, local)
+        b_qkv = jnp.stack([qv_all[:, 0], jnp.zeros((n_mp, local), F32), qv_all[:, 1]], 1)
+        b_qkv = b_qkv.reshape(n_mp, 1, 3 * local)
 
         def gather(weight):
             share = weight.shape[0] // n_dp
@@ -1283,7 +1279,6 @@
     outs_by_kind = list(zip(*results))
     h2, dm, z, du = outs_by_kind[3:7]
     da = outs_by_kind[2]
-    block_out = jnp.concatenate(outs_by_kind[0], 0)
     stats_two = jnp.concatenate(outs_by_kind[7], 0)
     grad_fc1_bias = sum(outs_by_kind[8])[0, 0]
     gate_one, gate_two = mod[:, 2], mod[:, 5]
@@ -1320,12 +1315,9 @@
         biases = lax.psum((grad_fc1_bias, grad_fc2_bias, grad_proj_bias, grad_qv_bias), "dp")
         grad_fc1_bias, grad_fc2_bias, grad_proj_bias, grad_qv_bias = biases
 
-    before, stats_one = [], []
-    for i in range(lat):
-        latents_grad, stats = latents_back(dh1[i], results[i][1], latents, mod, i, rows, before)
-        before = [latents_grad]
-        stats_one.append(stats)
-    stats_one = jnp.concatenate(stats_one, 0)
+    latents_grad, stats_one, block_out = latents_back(
+        dh1, outs_by_kind[1], outs_by_kind[0], latents, mod, rows
+    )
 
     dmod = jnp.stack(
         [

time: 665 us -> 654 us (0.983)
    pallas_call x1, Pallas kernels: 150 us -> 165 us  [attn_gather(): pl.pallas_call(attn_gather_kernel, grid=(n_mp, lat), in_specs=[pl.BlockSp...]
    pallas_call x1, Pallas kernels: 114 us -> 101 us  [tail_sums(): pl.pallas_call(functools.partial(tail_kernel, lats=lats), in_specs=[vmem,...]
    pallas_call x4 -> x1, Pallas kernels: 31.8 us -> 21.9 us  [latents_back(): pl.pallas_call(functools.partial(latents_kernel, lats=lat), grid=(lat, st...]
    pallas_call x1, Pallas kernels: 12.6 us -> 20 us  [rows_exchange(): pl.pallas_call(rows_kernel, in_specs=[vmem, vmem], out_specs=[vmem, vmem]...]
where the time goes in v6:
time: 654 us; the launch traced here: 645 us
  Pallas kernels  605 us (93%)
  local copies, waits for them, and re-layouts  16 us (2%)
  other arithmetic  15 us (2%)
  matrix products  7.25 us (1%)
    pallas_call x3, Pallas kernels, mlp_both(): pl.pallas_call(functools.partial(mlp_kernel, summing=summing), grid=(seq...  238 us
    pallas_call x1, Pallas kernels, attn_gather(): pl.pallas_call(attn_gather_kernel, grid=(n_mp, lat), in_specs=[pl.BlockSp...  165 us
    pallas_call x1, Pallas kernels, tail_sums(): pl.pallas_call(functools.partial(tail_kernel, lats=lats), in_specs=[vmem,...  101 us
    pallas_call x3, Pallas kernels, attn_bwd(): pl.pallas_call(functools.partial(attn_bwd_kernel, rows=rows), grid=(1,),...  59.6 us
    pallas_call x1, Pallas kernels, latents_back(): pl.pallas_call(functools.partial(latents_kernel, lats=lat), grid=(lat, st...  21.9 us
    pallas_call x1, Pallas kernels, rows_exchange(): pl.pallas_call(rows_kernel, in_specs=[vmem, vmem], out_specs=[vmem, vmem]...  20 us

profile of v6, /device:TPU:0, one launch (start us, length us, event | category | flops | bytes accessed | tf_op | source)
XLA Modules:
  0.0 644.6 jit_solution(3316617814529317526)
XLA Ops:
  0.6 0.7 broadcast_in_dim.19
  1.3 0.7 concatenate.26
  2.0 0.8 concatenate.25
  2.8 0.7 fusion.18.rows_ref
  3.5 165.1 %attn_gather.1 = (bf16[4,3,288,1024]{3,2,1,0:T(8,128)(2,1)}, bf16[3,12,72,1024]{3,2,1,0:T(8,128)(2,1)}, f32[3,4,1024]{2,1,0:T(4,128)}, bf16[3,1024,1152]{2,1,0:T...) custom-call(bf16[3,1024,1152]{2,1,0:T(8,128)(2,1)} %refs_0_.1, ...), custom_call_target="tpu_custom_call" | custom-call | tf_op jit(solution)/shard_map/attn_gather/pallas_call | solution.py:397
  168.6 1.0 slice_bitcast_fusion
  169.6 0.8 reshape.107.refs_3_.refs_1_
  170.4 1.6 slice.83.refs_5_
  173.2 73.8 %mlp_both.1 = (bf16[1,1024,1152]{2,1,0:T(8,128)(2,1)}, bf16[1,1024,1152]{2,1,0:T(8,128)(2,1)}, bf16[1,1024,1152]{2,1,0:T(8,128)(2,1)}, bf16[1,1024,1152]{2,1,0:T...) custom-call(bf16[4,3,288,1024]{3,2,1,0:T(8,128)(2,1)} %get-tuple-ele, ...), custom_call_target="tpu_custom_call" | custom-call | tf_op jit(solution)/shard_map/mlp_both/pallas_call | solution.py:717
  247.0 19.7 %attn_bwd.3 = (bf16[1,864,1024]{2,1,0:T(8,128)(2,1)}, bf16[1,1024,1152]{2,1,0:T(8,128)(2,1)}, f32[1,864,1]{2,1,0:T(8,128)}) custom-call(bf16[1,1024,1152]{2,1,0:T(8,128)(2,1)} %get-tuple-element.68.da_ref.refs_19_, bf16[4,3,288,1024]{3,2,1,0:T(8,128)(2,1)} %get-tuple-element.66.refs_0_.heads_ref.refs_2_, ...), custom_call_target="tpu_custom_call" | custom-call | tf_op jit(solution)/shard_map/attn_bwd/pallas_call | solution.py:1127
  266.7 83.1 %mlp_sum.2 = (bf16[1,1024,1152]{2,1,0:T(8,128)(2,1)}, bf16[1,1024,1152]{2,1,0:T(8,128)(2,1)}, bf16[1,1024,1152]{2,1,0:T(8,128)(2,1)}, bf16[1,1024,1152]{2,1,0:T(...) custom-call(bf16[4,3,288,1024]{3,2,1,0:T(8,128)(2,1)} %get-tuple-ele, ...), custom_call_target="tpu_custom_call" | custom-call | tf_op jit(solution)/shard_map/mlp_sum/pallas_call | solution.py:717
  349.9 19.8 %attn_bwd.4 = (bf16[1,864,1024]{2,1,0:T(8,128)(2,1)}, bf16[1,1024,1152]{2,1,0:T(8,128)(2,1)}, f32[1,864,1]{2,1,0:T(8,128)}) custom-call(bf16[1,1024,1152]{2,1,0:T(8,128)(2,1)} %get-tuple-element.73.da_ref.refs_20_, bf16[4,3,288,1024]{3,2,1,0:T(8,128)(2,1)} %get-tuple-element.66.refs_0_.heads_ref.refs_2_, ...), custom_call_target="tpu_custom_call" | custom-call | tf_op jit(solution)/shard_map/attn_bwd/pallas_call | solution.py:1127
  369.7 81.3 %mlp_sum.3 = (bf16[1,1024,1152]{2,1,0:T(8,128)(2,1)}, bf16[1,1024,1152]{2,1,0:T(8,128)(2,1)}, bf16[1,1024,1152]{2,1,0:T(8,128)(2,1)}, bf16[1,1024,1152]{2,1,0:T(...) custom-call(bf16[4,3,288,1024]{3,2,1,0:T(8,128)(2,1)} %get-tuple-ele, ...), custom_call_target="tpu_custom_call" | custom-call | tf_op jit(solution)/shard_map/mlp_sum/pallas_call | solution.py:717
  451.0 0.7 convert_bitcast_fusion.1
  451.7 0.8 constant_dynamic-update-slice_fusion
  452.5 1.0 fusion.15
  453.6 20.1 %attn_bwd.5 = (bf16[1,864,1024]{2,1,0:T(8,128)(2,1)}, bf16[1,1024,1152]{2,1,0:T(8,128)(2,1)}, f32[1,864,1]{2,1,0:T(8,128)}) custom-call(bf16[1,1024,1152]{2,1,0:T(8,128)(2,1)} %get-tuple-element.76.da_ref.refs_21_, bf16[4,3,288,1024]{3,2,1,0:T(8,128)(2,1)} %get-tuple-element.66.refs_0_.heads_ref.refs_2_, ...), custom_call_target="tpu_custom_call" | custom-call | tf_op jit(solution)/shard_map/attn_bwd/pallas_call | solution.py:1127
  473.6 1.1 add_convert_fusion
  475.0 0.8 fusion.8
  475.8 100.5 %tail_sums.1 = (bf16[1,1024,1152]{2,1,0:T(8,128)(2,1)}, bf16[112,32,1152]{2,1,0:T(8,128)(2,1)}) custom-call(bf16[1,1024,1152]{2,1,0:T(8,128)(2,1)} %get-tuple-element.77.refs_0_, bf16[4,32,1152]{2,1,0:T(8,128)(2,1)} %bitcast.52, bf16[4,3,288,1024]{3,2,1,0:T(8,128)(2,1)} %get-tuple-element.66.refs_0_.heads_ref.refs_2_, ...), custom_call_target="tpu_custom_call" | custom-call | tf_op jit(solution)/shard_map/tail_sums/pallas_call | solution.py:992
  576.3 3.0 fusion.19
  579.3 5.2 bitcast_convert_fusion
  584.5 21.9 %latents_back.1 = (bf16[3,1024,1152]{2,1,0:T(8,128)(2,1)}, f32[3,8,1152]{2,1,0:T(8,128)}, bf16[3,1024,1152]{2,1,0:T(8,128)(2,1)}) custom-call(bf16[3,1024,1152]{2,1,0:T(8,128)(2,1)} %refs_0_.1, f32[3,6,1152]{2,1,0:T(8,128)} %reshape.107.refs_3_.refs_1_, bf16[1,1024,1152]{2,1,0:T(8,128)(2,1)} %get-tuple-element.72.refs_2_, ...), custom_call_target="tpu_custom_call" | custom-call | tf_op jit(solution)/shard_map/latents_back/pallas_call | solution.py:1174
  606.4 0.9 slice.141
  607.5 2.8 fusion.20
  610.3 20.0 %rows_exchange.1 = (bf16[8,16,2880]{2,1,0:T(8,128)(2,1)S(1)}, f32[8,1152]{1,0:T(8,128)S(1)}) custom-call(bf16[16,2880]{1,0:T(8,128)(2,1)S(1)} %fusion.12.rows_ref, f32[8,1152]{1,0:T(8,128)S(1)} %pad.20.act_ref), custom_call_target="tpu_custom_call" | custom-call | tf_op jit(solution)/shard_map/rows_exchange/pallas_call | solution.py:1062
  630.3 4.5 fusion.4
  636.1 1.7 slice.95
  637.8 2.2 convert_bitcast_fusion
  640.0 1.1 slice.98
  641.2 1.2 bitcast_convert_fusion.2
  642.4 0.7 slice_convert_fusion.2
  (45 shorter events, 4.4 us)
Async XLA Ops:
  3.5 168.5 %copy-start.8 = (bf16[1152]{0:T(1024)(128)(2,1)S(1)}, bf16[1152]{0:T(1024)(128)(2,1)}, u32[]{:S(2)}) copy-start(bf16[1152]{0:T(1024)(128)(2,1)} %param.19) | copy-start | bytes 6916
  3.5 169.1 %copy-start.9 = (bf16[1152]{0:T(1024)(128)(2,1)S(1)}, bf16[1152]{0:T(1024)(128)(2,1)}, u32[]{:S(2)}) copy-start(bf16[1152]{0:T(1024)(128)(2,1)} %param.23) | copy-start | bytes 6916
  369.7 81.3 %copy-start.6 = (f32[1,1,1152]{2,1,0:T(1,128)S(1)}, f32[1,1,1152]{2,1,0:T(1,128)}, u32[]{:S(2)}) copy-start(f32[1,1,1152]{2,1,0:T(1,128)} %get-tuple-element.78) | copy-start | bytes 13828
  369.7 81.3 %copy-start.7 = (f32[1,1,1152]{2,1,0:T(1,128)S(1)}, f32[1,1,1152]{2,1,0:T(1,128)}, u32[]{:S(2)}) copy-start(f32[1,1,1152]{2,1,0:T(1,128)} %get-tuple-element.79) | copy-start | bytes 13828
  369.7 82.0 %copy-start.3 = (f32[1,8,1152]{2,1,0:T(8,128)S(1)}, f32[1,8,1152]{2,1,0:T(8,128)}, u32[]{:S(2)}) copy-start(f32[1,8,1152]{2,1,0:T(8,128)} %get-tuple-element.81) | copy-start | bytes 110596
  369.7 82.0 %copy-start.4 = (f32[1,8,1152]{2,1,0:T(8,128)S(1)}, f32[1,8,1152]{2,1,0:T(8,128)}, u32[]{:S(2)}) copy-start(f32[1,8,1152]{2,1,0:T(8,128)} %get-tuple-element.82) | copy-start | bytes 110596
  453.6 20.1 %copy-start = (f32[1,864,1]{2,1,0:T(8,128)S(1)}, f32[1,864,1]{2,1,0:T(8,128)}, u32[]{:S(2)}) copy-start(f32[1,864,1]{2,1,0:T(8,128)} %get-tuple-element.84) | copy-start | bytes 10372
  453.6 20.1 %copy-start.1 = (f32[1,864,1]{2,1,0:T(8,128)S(1)}, f32[1,864,1]{2,1,0:T(8,128)}, u32[]{:S(2)}) copy-start(f32[1,864,1]{2,1,0:T(8,128)} %get-tuple-element.85) | copy-start | bytes 10372
  584.5 23.0 %copy-start.5 = (bf16[3,1152]{1,0:T(4,128)(2,1)S(1)}, bf16[3,1152]{1,0:T(4,128)(2,1)}, u32[]{:S(2)}) copy-start(bf16[3,1152]{1,0:T(4,128)(2,1)} %get-tuple-element.112) | copy-start | bytes 20740
  630.3 4.5 copy-start.2

commit v7 on v6

--- a/solution.py
+++ b/solution.py
@@ -153,7 +153,7 @@
 ):
     n_mp = all_ref.shape[0]
     lats = h1_all.shape[0]
-    units, pace = 3 * (n_mp - 1), 4
+    units, pace = 3 * (n_mp - 1), 5
     slot, lat = pl.program_id(0), pl.program_id(1)
     step = slot * lats + lat
     dp_at, me = lax.axis_index("dp"), lax.axis_index("mp")
@@ -298,13 +298,13 @@
         def due(at, every):
             return jnp.where((t - at) % every == 0, (t - at) // every, -1)
 
-        for k, at in ((0, 3), (1, 4), (2, 7)):
+        for k, at in ((0, 0), (1, 0), (2, 4)):
             nth = due(at, 3 * pace)
             event(0, jnp.where(nth < 0, -1, nth * 3 + k))
-        for stage, at in ((1, 3), (3, 8), (2, 5), (4, 11)):
+        for stage, at in ((3, 8), (2, 3), (1, 0), (4, 11)):
             event(stage, due(at, pace))
         for c in (1, 2):
-            pl.when(t == 3 * pace * c - 3)(lambda: send_own(c))
+            pl.when(t == 3 * pace * c - 6)(lambda: send_own(c))
 
     @pl.when((lat == 0) & (slot == 0))
     def _():
@@ -926,8 +926,8 @@
     part_ref, bias_ref, heads_ref, h1_ref = refs[:4]
     lists = [refs[4 + i * lats : 4 + (i + 1) * lats] for i in range(6)]
     h2s, dus, zs, dms, dqkvs, das = [[ref.at[0] for ref in group] for group in lists]
-    sum_ref, full_ref = refs[4 + 6 * lats : 6 + 6 * lats]
-    refs = refs[6 + 6 * lats :]
+    sum_ref, *total_refs = refs[4 + 6 * lats : 10 + 6 * lats]
+    refs = refs[10 + 6 * lats :]
     up, down, line_sems, terms, full, halves, firsts, seconds, cube_sems = refs[:9]
     right, left_cols, left_rows, right_sems, left_sems, local_sem = refs[9:]
     line = LineSum(part_ref, up, down, line_sems, sum_ref, 3)
@@ -971,11 +971,17 @@
         return carry
 
     lax.fori_loop(cube.units, cube.units + 6, advance, 0)
-    store = pltpu.make_async_copy(full, full_ref, local_sem.at[0])
-    store.start()
+    stores = []
+    first = 0
+    for i, ref in enumerate(total_refs):
+        source = full.at[pl.ds(first, ref.shape[0])]
+        stores.append(pltpu.make_async_copy(source, ref, local_sem.at[i]))
+        stores[-1].start()
+        first += ref.shape[0]
     line.finish(2 * (cube.units + 6) + 1)
     cube.finish()
-    store.wait()
+    for store in stores:
+        store.wait()
 
 
 def tail_sums(part, biases, heads, h1, lists):
@@ -989,11 +995,13 @@
     any_spec = pl.BlockSpec(memory_space=pl.ANY)
     shape = (units * 16, BLOCK, dim)
     flat = [array for group in lists for array in group]
-    total, full = pl.pallas_call(
+    counts = [dim // BLOCK, dim // BLOCK, 3 * local // BLOCK, local // BLOCK, spare]
+    total, *grads = pl.pallas_call(
         functools.partial(tail_kernel, lats=lats),
         in_specs=[vmem, vmem] + [any_spec] * (2 + len(flat)),
-        out_specs=[vmem, any_spec],
-        out_shape=[jax.ShapeDtypeStruct(part.shape, BF), jax.ShapeDtypeStruct(shape, BF)],
+        out_specs=[vmem] + [any_spec] * len(counts),
+        out_shape=[jax.ShapeDtypeStruct(part.shape, BF)]
+        + [jax.ShapeDtypeStruct((count, BLOCK, dim), BF) for count in counts],
         scratch_shapes=line_scratch(seq, dim)
         + [
             pltpu.VMEM(shape, BF),
@@ -1007,14 +1015,14 @@
             pltpu.VMEM((2, lats, (3 * local // BLOCK + 1) // 2 * BLOCK, seq), BF),
             pltpu.SemaphoreType.DMA((2, lats)),
             pltpu.SemaphoreType.DMA((2, lats)),
-            pltpu.SemaphoreType.DMA((1,)),
+            pltpu.SemaphoreType.DMA((len(counts),)),
         ],
         compiler_params=pltpu.CompilerParams(
             collective_id=2, has_side_effects=True, vmem_limit_bytes=63 * MIB
         ),
         name="tail_sums",
     )(part, biases.reshape(spare, BLOCK, dim), heads, h1, *flat)
-    return total, full.reshape(units * 16 * BLOCK, dim)
+    return total, [grad.reshape(-1, dim) for grad in grads]
 
 
 def rows_kernel(rows_ref, act_ref, every_ref, total_ref, acts, sems):
@@ -1297,10 +1305,8 @@
         ).astype(BF)
         dh1_i, sums = tail_sums(dh1_i, bias_rows, heads, h1, (h2, du, z, dm, dqkv, da))
         dh1.append(dh1_i)
-        grad_fc1, grad_fc2 = sums[:dim], sums[dim : 2 * dim]
-        grad_qkv = sums[2 * dim : 2 * dim + 3 * local]
-        grad_proj = sums[2 * dim + 3 * local : 3 * dim]
-        bias_rows = sums[3 * dim : 3 * dim + 4].astype(F32)
+        grad_fc1, grad_fc2, grad_qkv, grad_proj, bias_rows = sums
+        bias_rows = bias_rows[:4].astype(F32)
         grad_fc1_bias, grad_fc2_bias, grad_proj_bias = bias_rows[:3]
         grad_qv_bias = bias_rows[3, : 2 * local].reshape(2, local)
     else:

time: 654 us -> 650 us (level)
    pallas_call x3, Pallas kernels: 238 us -> 245 us  [mlp_both(): pl.pallas_call(functools.partial(mlp_kernel, summing=summing), grid=(seq...]
where the time goes in v7:
time: 650 us; the launch traced here: 641 us
  Pallas kernels  605 us (93%)
  other arithmetic  17.1 us (3%)
  local copies, waits for them, and re-layouts  10.2 us (2%)
  matrix products  7.25 us (1%)
    pallas_call x3, Pallas kernels, mlp_both(): pl.pallas_call(functools.partial(mlp_kernel, summing=summing), grid=(seq...  245 us
    pallas_call x1, Pallas kernels, attn_gather(): pl.pallas_call(attn_gather_kernel, grid=(n_mp, lat), in_specs=[pl.BlockSp...  161 us
    pallas_call x1, Pallas kernels, tail_sums(): pl.pallas_call(functools.partial(tail_kernel, lats=lats), in_specs=[vmem,...  99.4 us
    pallas_call x3, Pallas kernels, attn_bwd(): pl.pallas_call(functools.partial(attn_bwd_kernel, rows=rows), grid=(1,),...  59.6 us
    pallas_call x1, Pallas kernels, latents_back(): pl.pallas_call(functools.partial(latents_kernel, lats=lat), grid=(lat, st...  21.9 us
    pallas_call x1, Pallas kernels, rows_exchange(): pl.pallas_call(rows_kernel, in_specs=[vmem, vmem], out_specs=[vmem, vmem]...  18 us

profile of v7, /device:TPU:0, one launch (start us, length us, event | category | flops | bytes accessed | tf_op | source)
XLA Modules:
  0.0 640.7 jit_solution(4288082962355766860)
XLA Ops:
  0.6 0.7 broadcast_in_dim.19
  1.3 0.7 concatenate.26
  2.0 0.8 concatenate.25
  2.8 0.7 fusion.18.rows_ref
  3.5 160.7 %attn_gather.1 = (bf16[4,3,288,1024]{3,2,1,0:T(8,128)(2,1)}, bf16[3,12,72,1024]{3,2,1,0:T(8,128)(2,1)}, f32[3,4,1024]{2,1,0:T(4,128)}, bf16[3,1024,1152]{2,1,0:T...) custom-call(bf16[3,1024,1152]{2,1,0:T(8,128)(2,1)} %refs_0_.1, ...), custom_call_target="tpu_custom_call" | custom-call | tf_op jit(solution)/shard_map/attn_gather/pallas_call | solution.py:397
  164.2 1.0 slice_bitcast_fusion
  165.2 0.8 reshape.107.refs_3_.refs_1_
  166.0 1.6 slice.67.refs_5_
  168.8 73.8 %mlp_both.1 = (bf16[1,1024,1152]{2,1,0:T(8,128)(2,1)}, bf16[1,1024,1152]{2,1,0:T(8,128)(2,1)}, bf16[1,1024,1152]{2,1,0:T(8,128)(2,1)}, bf16[1,1024,1152]{2,1,0:T...) custom-call(bf16[4,3,288,1024]{3,2,1,0:T(8,128)(2,1)} %get-tuple-ele, ...), custom_call_target="tpu_custom_call" | custom-call | tf_op jit(solution)/shard_map/mlp_both/pallas_call | solution.py:717
  242.6 19.7 %attn_bwd.3 = (bf16[1,864,1024]{2,1,0:T(8,128)(2,1)}, bf16[1,1024,1152]{2,1,0:T(8,128)(2,1)}, f32[1,864,1]{2,1,0:T(8,128)}) custom-call(bf16[1,1024,1152]{2,1,0:T(8,128)(2,1)} %get-tuple-element.72.da_ref.refs_19_, bf16[4,3,288,1024]{3,2,1,0:T(8,128)(2,1)} %get-tuple-element.70.refs_0_.heads_ref.refs_2_, ...), custom_call_target="tpu_custom_call" | custom-call | tf_op jit(solution)/shard_map/attn_bwd/pallas_call | solution.py:1135
  262.4 89.6 %mlp_sum.2 = (bf16[1,1024,1152]{2,1,0:T(8,128)(2,1)}, bf16[1,1024,1152]{2,1,0:T(8,128)(2,1)}, bf16[1,1024,1152]{2,1,0:T(8,128)(2,1)}, bf16[1,1024,1152]{2,1,0:T(...) custom-call(bf16[4,3,288,1024]{3,2,1,0:T(8,128)(2,1)} %get-tuple-ele, ...), custom_call_target="tpu_custom_call" | custom-call | tf_op jit(solution)/shard_map/mlp_sum/pallas_call | solution.py:717
  352.0 19.8 %attn_bwd.4 = (bf16[1,864,1024]{2,1,0:T(8,128)(2,1)}, bf16[1,1024,1152]{2,1,0:T(8,128)(2,1)}, f32[1,864,1]{2,1,0:T(8,128)}) custom-call(bf16[1,1024,1152]{2,1,0:T(8,128)(2,1)} %get-tuple-element.77.da_ref.refs_20_, bf16[4,3,288,1024]{3,2,1,0:T(8,128)(2,1)} %get-tuple-element.70.refs_0_.heads_ref.refs_2_, ...), custom_call_target="tpu_custom_call" | custom-call | tf_op jit(solution)/shard_map/attn_bwd/pallas_call | solution.py:1135
  371.8 81.8 %mlp_sum.3 = (bf16[1,1024,1152]{2,1,0:T(8,128)(2,1)}, bf16[1,1024,1152]{2,1,0:T(8,128)(2,1)}, bf16[1,1024,1152]{2,1,0:T(8,128)(2,1)}, bf16[1,1024,1152]{2,1,0:T(...) custom-call(bf16[4,3,288,1024]{3,2,1,0:T(8,128)(2,1)} %get-tuple-ele, ...), custom_call_target="tpu_custom_call" | custom-call | tf_op jit(solution)/shard_map/mlp_sum/pallas_call | solution.py:717
  453.6 0.7 convert_bitcast_fusion.1
  454.4 0.8 constant_dynamic-update-slice_fusion
  455.1 1.0 fusion.15
  456.2 20.1 %attn_bwd.5 = (bf16[1,864,1024]{2,1,0:T(8,128)(2,1)}, bf16[1,1024,1152]{2,1,0:T(8,128)(2,1)}, f32[1,864,1]{2,1,0:T(8,128)}) custom-call(bf16[1,1024,1152]{2,1,0:T(8,128)(2,1)} %get-tuple-element.80.da_ref.refs_21_, bf16[4,3,288,1024]{3,2,1,0:T(8,128)(2,1)} %get-tuple-element.70.refs_0_.heads_ref.refs_2_, ...), custom_call_target="tpu_custom_call" | custom-call | tf_op jit(solution)/shard_map/attn_bwd/pallas_call | solution.py:1135
  476.4 1.1 add_convert_fusion
  477.7 0.8 fusion.8
  478.5 99.4 %tail_sums.1 = (bf16[1,1024,1152]{2,1,0:T(8,128)(2,1)}, bf16[36,32,1152]{2,1,0:T(8,128)(2,1)}, bf16[36,32,1152]{2,1,0:T(8,128)(2,1)}, bf16[27,32,1152]{2,1,0:T(8...) custom-call(bf16[1,1024,1152]{2,1,0:T(8,128)(2,1)} %get-tuple-element.81.refs_0_, ...), custom_call_target="tpu_custom_call" | custom-call | tf_op jit(solution)/shard_map/tail_sums/pallas_call | solution.py:999
  577.9 7.4 %bitcast_convert_fusion = (f32[1152,1152]{1,0:T(8,128)}, f32[1152,1152]{1,0:T(8,128)}) fusion(bf16[36,32,1152]{2,1,0:T(8,128)(2,1)} %get-tuple-element.123, bf16[36,32,1152]{2,1,0:T(8,128)(2,1)} %get-tuple-element.122), kind=kLoop, calls=%fused_computation.1 | loop fusion | flops 2654208 | bytes 15925248 | tf_op jit(solution)/shard_map/convert_element_type | solution.py:1355
  585.3 21.9 %latents_back.1 = (bf16[3,1024,1152]{2,1,0:T(8,128)(2,1)}, f32[3,8,1152]{2,1,0:T(8,128)}, bf16[3,1024,1152]{2,1,0:T(8,128)(2,1)}) custom-call(bf16[3,1024,1152]{2,1,0:T(8,128)(2,1)} %refs_0_.1, f32[3,6,1152]{2,1,0:T(8,128)} %reshape.107.refs_3_.refs_1_, bf16[1,1024,1152]{2,1,0:T(8,128)(2,1)} %get-tuple-element.76.refs_2_, ...), custom_call_target="tpu_custom_call" | custom-call | tf_op jit(solution)/shard_map/latents_back/pallas_call | solution.py:1182
  607.2 0.9 slice.121
  608.3 2.8 fusion.19
  611.1 18.0 %rows_exchange.1 = (bf16[8,16,2880]{2,1,0:T(8,128)(2,1)S(1)}, f32[8,1152]{1,0:T(8,128)S(1)}) custom-call(bf16[16,2880]{1,0:T(8,128)(2,1)S(1)} %fusion.12.rows_ref, f32[8,1152]{1,0:T(8,128)S(1)} %pad.20.act_ref), custom_call_target="tpu_custom_call" | custom-call | tf_op jit(solution)/shard_map/rows_exchange/pallas_call | solution.py:1070
  629.2 4.5 fusion.4
  634.3 0.7 convert_reduce_fusion
  635.0 2.2 convert_bitcast_fusion
  637.2 1.2 bitcast_convert_fusion.2
  638.4 0.7 slice_convert_fusion.2
  639.1 0.6 slice_reduce_fusion.2
  639.8 0.7 reshape_squeeze.3
  (46 shorter events, 2.4 us)
Async XLA Ops:
  3.5 164.1 %copy-start.10 = (bf16[1152]{0:T(1024)(128)(2,1)S(1)}, bf16[1152]{0:T(1024)(128)(2,1)}, u32[]{:S(2)}) copy-start(bf16[1152]{0:T(1024)(128)(2,1)} %param.19) | copy-start | bytes 6916
  3.5 164.7 %copy-start.11 = (bf16[1152]{0:T(1024)(128)(2,1)S(1)}, bf16[1152]{0:T(1024)(128)(2,1)}, u32[]{:S(2)}) copy-start(bf16[1152]{0:T(1024)(128)(2,1)} %param.23) | copy-start | bytes 6916
  371.8 81.8 %copy-start.8 = (f32[1,1,1152]{2,1,0:T(1,128)S(1)}, f32[1,1,1152]{2,1,0:T(1,128)}, u32[]{:S(2)}) copy-start(f32[1,1,1152]{2,1,0:T(1,128)} %get-tuple-element.82) | copy-start | bytes 13828
  371.8 81.8 %copy-start.9 = (f32[1,1,1152]{2,1,0:T(1,128)S(1)}, f32[1,1,1152]{2,1,0:T(1,128)}, u32[]{:S(2)}) copy-start(f32[1,1,1152]{2,1,0:T(1,128)} %get-tuple-element.83) | copy-start | bytes 13828
  371.8 82.6 %copy-start.5 = (f32[1,8,1152]{2,1,0:T(8,128)S(1)}, f32[1,8,1152]{2,1,0:T(8,128)}, u32[]{:S(2)}) copy-start(f32[1,8,1152]{2,1,0:T(8,128)} %get-tuple-element.85) | copy-start | bytes 110596
  371.8 82.6 %copy-start.6 = (f32[1,8,1152]{2,1,0:T(8,128)S(1)}, f32[1,8,1152]{2,1,0:T(8,128)}, u32[]{:S(2)}) copy-start(f32[1,8,1152]{2,1,0:T(8,128)} %get-tuple-element.86) | copy-start | bytes 110596
  456.2 20.2 %copy-start.2 = (f32[1,864,1]{2,1,0:T(8,128)S(1)}, f32[1,864,1]{2,1,0:T(8,128)}, u32[]{:S(2)}) copy-start(f32[1,864,1]{2,1,0:T(8,128)} %get-tuple-element.88) | copy-start | bytes 10372
  456.2 20.1 %copy-start.3 = (f32[1,864,1]{2,1,0:T(8,128)S(1)}, f32[1,864,1]{2,1,0:T(8,128)}, u32[]{:S(2)}) copy-start(f32[1,864,1]{2,1,0:T(8,128)} %get-tuple-element.89) | copy-start | bytes 10372
  585.3 23.0 %copy-start.7 = (bf16[3,1152]{1,0:T(4,128)(2,1)S(1)}, bf16[3,1152]{1,0:T(4,128)(2,1)}, u32[]{:S(2)}) copy-start(bf16[3,1152]{1,0:T(4,128)(2,1)} %get-tuple-element.116) | copy-start | bytes 20740
  629.1 4.5 copy-start.4
  629.2 5.8 copy-start
  635.0 2.2 copy-start.1

commit v8 on v7

--- a/solution.py
+++ b/solution.py
@@ -136,7 +136,8 @@
     qkv_ref,
     lse_ref,
     h1_ref,
-    small_ref,
+    mod_ref,
+    b1_ref,
     low_ref,
     all_ref,
     h1_all,
@@ -289,7 +290,17 @@
             small_copy(k).start()
         for k in range(1, n_mp):
             small_copy(k, True).wait_recv()
-        small_ref[...] = small[...]
+        dim, cols = h1_all.shape[2], small.shape[2]
+        for j in range(6):
+            at, off = j * dim // cols, j * dim % cols
+            kept = small[at, :lats, :][:, off : off + dim]
+            if kept.shape[1] < dim:
+                more = small[at + 1, :lats, : dim - kept.shape[1]]
+                kept = jnp.concatenate([kept, more], 1)
+            for i in range(lats):
+                mod_ref[i, j : j + 1] = kept[i : i + 1]
+        for at in range(n_mp):
+            b1_ref[at] = small[at, lats : lats + 1, :][:, cols - b1_ref.shape[2] :]
 
     def next_weights(k):
         return pltpu.make_async_copy(all_ref.at[near_part(me, k), 0], w_buf, local_sem.at[0])
@@ -394,7 +405,7 @@
     part = lambda s: near_part(lax.axis_index("mp"), s)
     whole = lambda shape: pl.BlockSpec(shape, lambda s, l: (0,) * len(shape))
     any_spec = pl.BlockSpec(memory_space=pl.ANY)
-    heads, qkv, lse, h1, small, cond_low, gathered = pl.pallas_call(
+    heads, qkv, lse, h1, mod, b_fc1, cond_low, gathered = pl.pallas_call(
         attn_gather_kernel,
         grid=(n_mp, lat),
         in_specs=[
@@ -408,7 +419,8 @@
             pl.BlockSpec((1, 3 * n_heads, HEAD_DIM, seq), lambda s, l: (first(s, l), 0, 0, 0)),
             pl.BlockSpec((1, n_heads, seq), lambda s, l: (first(s, l), 0, 0)),
             pl.BlockSpec((1, seq, dim), lambda s, l: (first(s, l), 0, 0)),
-            whole((n_mp, 8, cols)),
+            whole((lat, 6, dim)),
+            whole((n_mp, 1, own[2].shape[1])),
             whole(condition.shape),
             any_spec,
         ],
@@ -417,7 +429,8 @@
             jax.ShapeDtypeStruct((lat, 3 * n_heads, HEAD_DIM, seq), BF),
             jax.ShapeDtypeStruct((lat, n_heads, seq), F32),
             jax.ShapeDtypeStruct((lat, seq, dim), BF),
-            jax.ShapeDtypeStruct((n_mp, 8, cols), F32),
+            jax.ShapeDtypeStruct((lat, 6, dim), F32),
+            jax.ShapeDtypeStruct((n_mp, 1, own[2].shape[1]), F32),
             jax.ShapeDtypeStruct(condition.shape, BF),
             jax.ShapeDtypeStruct((n_mp, 3, 2, 2, 2, rows, dim), BF),
         ],
@@ -439,7 +452,7 @@
         ),
         name="attn_gather",
     )(latents, condition, small_rows, ada_rows, *own)
-    return heads, qkv, lse, h1, small, cond_low, gathered.reshape(n_mp, 3, dim, dim)
+    return heads, qkv, lse, h1, mod, b_fc1, cond_low, gathered.reshape(n_mp, 3, dim, dim)
 
 
 def attn_fwd(me, latents, mod, gathered, bias, n_mp):
@@ -1229,7 +1242,7 @@
     if direct:
         own = (wq_own, proj_weight, fc1_weight, fc2_weight)
         small_rows = jnp.concatenate([ada_row, bias_row], 0)
-        heads, qkv, lse, h1, small, cond_low, gathered = attn_gather(
+        heads, qkv, lse, h1, mod, b_fc1, cond_low, gathered = attn_gather(
             latents, condition, small_rows, ada_weight.T, own, n_mp
         )
         gathered = (gathered,) * 3
@@ -1237,9 +1250,8 @@
         cond_low = jax.nn.silu(condition).astype(BF)
         mod_part = mm(cond_low, ada_weight) + ada_row
         small = lax.all_gather(jnp.concatenate([mod_part, bias_row], 0), "mp", axis=0)
-    mod = small[:, :lat].transpose(1, 0, 2).reshape(lat, 6, dim)
-    b_fc1 = small[:, lat, 2 * local :].reshape(n_mp, 1, hid)
-    if not direct:
+        mod = small[:, :lat].transpose(1, 0, 2).reshape(lat, 6, dim)
+        b_fc1 = small[:, lat, 2 * local :].reshape(n_mp, 1, hid)
         qv_all = small[:, lat, : 2 * local].reshape(n_mp, 2, local)
         b_qkv = jnp.stack([qv_all[:, 0], jnp.zeros((n_mp, local), F32), qv_all[:, 1]], 1)
         b_qkv = b_qkv.reshape(n_mp, 1, 3 * local)
@@ -1341,10 +1353,11 @@
     both = jnp.concatenate([cond_low, dmod_own], 1)
     grad_act = nt(dmod_own, ada_weight)
     if direct:
-        both = jnp.pad(both, ((0, 16 - lat), (0, 0)))
+        both = jnp.pad(both.reshape(5 * lat, -1), ((0, -5 * lat % 16), (0, 0)))
         grad_act = jnp.pad(grad_act, ((0, 8 - lat), (0, 0)))
         every, grad_act = rows_exchange(both, grad_act, n_dp, n_mp)
-        every, grad_act = every.reshape(n_dp * 16, dim + cols), grad_act[:lat]
+        every = every[:, : 5 * lat].reshape(n_dp * lat, dim + cols)
+        grad_act = grad_act[:lat]
     else:
         every = lax.all_gather(both, "dp", axis=0, tiled=True)
         grad_act = lax.psum(grad_act, "mp")

time: 650 us -> 643 us (0.989)
  no operation moved by 1% of the time
where the time goes in v8:
time: 643 us; the launch traced here: 634 us
  Pallas kernels  601 us (93%)
  other arithmetic  17.1 us (3%)
  matrix products  7.25 us (1%)
  local copies, waits for them, and re-layouts  7.13 us (1%)
    pallas_call x3, Pallas kernels, mlp_both(): pl.pallas_call(functools.partial(mlp_kernel, summing=summing), grid=(seq...  245 us
    pallas_call x1, Pallas kernels, attn_gather(): pl.pallas_call(attn_gather_kernel, grid=(n_mp, lat), in_specs=[pl.BlockSp...  161 us
    pallas_call x1, Pallas kernels, tail_sums(): pl.pallas_call(functools.partial(tail_kernel, lats=lats), in_specs=[vmem,...  99.4 us
    pallas_call x3, Pallas kernels, attn_bwd(): pl.pallas_call(functools.partial(attn_bwd_kernel, rows=rows), grid=(1,),...  59.6 us
    pallas_call x1, Pallas kernels, latents_back(): pl.pallas_call(functools.partial(latents_kernel, lats=lat), grid=(lat, st...  21.9 us
    pallas_call x1, Pallas kernels, rows_exchange(): pl.pallas_call(rows_kernel, in_specs=[vmem, vmem], out_specs=[vmem, vmem]...  14.1 us

profile of v8, /device:TPU:0, one launch (start us, length us, event | category | flops | bytes accessed | tf_op | source)
XLA Modules:
  0.0 633.7 jit_solution(15900932190518739665)
XLA Ops:
  0.6 0.7 broadcast_in_dim.19
  1.3 0.7 concatenate.26
  2.0 0.8 concatenate.25
  2.8 0.7 fusion.15.rows_ref
  3.5 160.8 %attn_gather.1 = (bf16[4,3,288,1024]{3,2,1,0:T(8,128)(2,1)}, bf16[3,12,72,1024]{3,2,1,0:T(8,128)(2,1)}, f32[3,4,1024]{2,1,0:T(4,128)}, bf16[3,1024,1152]{2,1,0:T...) custom-call(bf16[3,1024,1152]{2,1,0:T(8,128)(2,1)} %refs_0_.1, ...), custom_call_target="tpu_custom_call" | custom-call | tf_op jit(solution)/shard_map/attn_gather/pallas_call | solution.py:408
  164.3 0.6 reshape.113.refs_4_
  164.9 0.6 reshape.114.refs_6_
  165.5 73.8 %mlp_both.1 = (bf16[1,1024,1152]{2,1,0:T(8,128)(2,1)}, bf16[1,1024,1152]{2,1,0:T(8,128)(2,1)}, bf16[1,1024,1152]{2,1,0:T(8,128)(2,1)}, bf16[1,1024,1152]{2,1,0:T...) custom-call(bf16[4,3,288,1024]{3,2,1,0:T(8,128)(2,1)} %get-tuple-ele, ...), custom_call_target="tpu_custom_call" | custom-call | tf_op jit(solution)/shard_map/mlp_both/pallas_call | solution.py:730
  239.3 19.7 %attn_bwd.3 = (bf16[1,864,1024]{2,1,0:T(8,128)(2,1)}, bf16[1,1024,1152]{2,1,0:T(8,128)(2,1)}, f32[1,864,1]{2,1,0:T(8,128)}) custom-call(bf16[1,1024,1152]{2,1,0:T(8,128)(2,1)} %get-tuple-element.74.da_ref.refs_19_, bf16[4,3,288,1024]{3,2,1,0:T(8,128)(2,1)} %get-tuple-element.71.refs_0_.heads_ref.refs_2_, ...), custom_call_target="tpu_custom_call" | custom-call | tf_op jit(solution)/shard_map/attn_bwd/pallas_call | solution.py:1148
  259.1 89.5 %mlp_sum.2 = (bf16[1,1024,1152]{2,1,0:T(8,128)(2,1)}, bf16[1,1024,1152]{2,1,0:T(8,128)(2,1)}, bf16[1,1024,1152]{2,1,0:T(8,128)(2,1)}, bf16[1,1024,1152]{2,1,0:T(...) custom-call(bf16[4,3,288,1024]{3,2,1,0:T(8,128)(2,1)} %get-tuple-ele, ...), custom_call_target="tpu_custom_call" | custom-call | tf_op jit(solution)/shard_map/mlp_sum/pallas_call | solution.py:730
  348.6 19.8 %attn_bwd.4 = (bf16[1,864,1024]{2,1,0:T(8,128)(2,1)}, bf16[1,1024,1152]{2,1,0:T(8,128)(2,1)}, f32[1,864,1]{2,1,0:T(8,128)}) custom-call(bf16[1,1024,1152]{2,1,0:T(8,128)(2,1)} %get-tuple-element.79.da_ref.refs_20_, bf16[4,3,288,1024]{3,2,1,0:T(8,128)(2,1)} %get-tuple-element.71.refs_0_.heads_ref.refs_2_, ...), custom_call_target="tpu_custom_call" | custom-call | tf_op jit(solution)/shard_map/attn_bwd/pallas_call | solution.py:1148
  368.4 81.9 %mlp_sum.3 = (bf16[1,1024,1152]{2,1,0:T(8,128)(2,1)}, bf16[1,1024,1152]{2,1,0:T(8,128)(2,1)}, bf16[1,1024,1152]{2,1,0:T(8,128)(2,1)}, bf16[1,1024,1152]{2,1,0:T(...) custom-call(bf16[4,3,288,1024]{3,2,1,0:T(8,128)(2,1)} %get-tuple-ele, ...), custom_call_target="tpu_custom_call" | custom-call | tf_op jit(solution)/shard_map/mlp_sum/pallas_call | solution.py:730
  450.3 0.7 convert_bitcast_fusion.1
  451.1 0.8 constant_dynamic-update-slice_fusion
  451.8 1.0 fusion.12
  452.9 20.1 %attn_bwd.5 = (bf16[1,864,1024]{2,1,0:T(8,128)(2,1)}, bf16[1,1024,1152]{2,1,0:T(8,128)(2,1)}, f32[1,864,1]{2,1,0:T(8,128)}) custom-call(bf16[1,1024,1152]{2,1,0:T(8,128)(2,1)} %get-tuple-element.82.da_ref.refs_21_, bf16[4,3,288,1024]{3,2,1,0:T(8,128)(2,1)} %get-tuple-element.71.refs_0_.heads_ref.refs_2_, ...), custom_call_target="tpu_custom_call" | custom-call | tf_op jit(solution)/shard_map/attn_bwd/pallas_call | solution.py:1148
  473.1 1.1 add_convert_fusion
  474.4 0.8 fusion.6
  475.2 99.4 %tail_sums.1 = (bf16[1,1024,1152]{2,1,0:T(8,128)(2,1)}, bf16[36,32,1152]{2,1,0:T(8,128)(2,1)}, bf16[36,32,1152]{2,1,0:T(8,128)(2,1)}, bf16[27,32,1152]{2,1,0:T(8...) custom-call(bf16[1,1024,1152]{2,1,0:T(8,128)(2,1)} %get-tuple-element.83.refs_0_, ...), custom_call_target="tpu_custom_call" | custom-call | tf_op jit(solution)/shard_map/tail_sums/pallas_call | solution.py:1012
  574.6 7.4 %bitcast_convert_fusion = (f32[1152,1152]{1,0:T(8,128)}, f32[1152,1152]{1,0:T(8,128)}) fusion(bf16[36,32,1152]{2,1,0:T(8,128)(2,1)} %get-tuple-element.125, bf16[36,32,1152]{2,1,0:T(8,128)(2,1)} %get-tuple-element.124), kind=kLoop, calls=%fused_computation.1 | loop fusion | flops 2654208 | bytes 15925248 | tf_op jit(solution)/shard_map/convert_element_type | solution.py:1368
  582.0 21.9 %latents_back.1 = (bf16[3,1024,1152]{2,1,0:T(8,128)(2,1)}, f32[3,8,1152]{2,1,0:T(8,128)}, bf16[3,1024,1152]{2,1,0:T(8,128)(2,1)}) custom-call(bf16[3,1024,1152]{2,1,0:T(8,128)(2,1)} %refs_0_.1, f32[3,6,1152]{2,1,0:T(8,128)} %get-tuple-element.70.refs_3_.refs_1_, bf16[1,1024,1152]{2,1,0:T(8,128)(2,1)} %get-tuple-element.78.refs_2_, ...), custom_call_target="tpu_custom_call" | custom-call | tf_op jit(solution)/shard_map/latents_back/pallas_call | solution.py:1195
  603.9 0.9 slice.114
  605.1 2.8 fusion.16
  607.9 14.1 %rows_exchange.1 = (bf16[8,16,576]{2,1,0:T(8,128)(2,1)S(1)}, f32[8,1152]{1,0:T(8,128)S(1)}) custom-call(bf16[16,576]{1,0:T(8,128)(2,1)S(1)} %pad.19.rows_ref, f32[8,1152]{1,0:T(8,128)S(1)} %pad.20.act_ref), custom_call_target="tpu_custom_call" | custom-call | tf_op jit(solution)/shard_map/rows_exchange/pallas_call | solution.py:1083
  622.3 4.5 fusion.7
  626.8 0.6 convert_reduce_fusion
  627.4 0.6 fusion.11
  628.1 2.2 convert_bitcast_fusion
  630.3 1.2 bitcast_convert_fusion.2
  631.5 0.7 slice_convert_fusion.2
  632.2 0.6 slice_reduce_fusion.2
  632.8 0.7 reshape_squeeze.3
  (45 shorter events, 0.9 us)
Async XLA Ops:
  3.5 160.8 %copy-start.10 = (bf16[1152]{0:T(1024)(128)(2,1)S(1)}, bf16[1152]{0:T(1024)(128)(2,1)}, u32[]{:S(2)}) copy-start(bf16[1152]{0:T(1024)(128)(2,1)} %param.19) | copy-start | bytes 6916
  3.5 161.4 %copy-start.11 = (bf16[1152]{0:T(1024)(128)(2,1)S(1)}, bf16[1152]{0:T(1024)(128)(2,1)}, u32[]{:S(2)}) copy-start(bf16[1152]{0:T(1024)(128)(2,1)} %param.23) | copy-start | bytes 6916
  368.4 81.9 %copy-start.8 = (f32[1,1,1152]{2,1,0:T(1,128)S(1)}, f32[1,1,1152]{2,1,0:T(1,128)}, u32[]{:S(2)}) copy-start(f32[1,1,1152]{2,1,0:T(1,128)} %get-tuple-element.84) | copy-start | bytes 13828
  368.4 81.9 %copy-start.9 = (f32[1,1,1152]{2,1,0:T(1,128)S(1)}, f32[1,1,1152]{2,1,0:T(1,128)}, u32[]{:S(2)}) copy-start(f32[1,1,1152]{2,1,0:T(1,128)} %get-tuple-element.85) | copy-start | bytes 13828
  368.4 82.6 %copy-start.5 = (f32[1,8,1152]{2,1,0:T(8,128)S(1)}, f32[1,8,1152]{2,1,0:T(8,128)}, u32[]{:S(2)}) copy-start(f32[1,8,1152]{2,1,0:T(8,128)} %get-tuple-element.87) | copy-start | bytes 110596
  368.4 82.6 %copy-start.6 = (f32[1,8,1152]{2,1,0:T(8,128)S(1)}, f32[1,8,1152]{2,1,0:T(8,128)}, u32[]{:S(2)}) copy-start(f32[1,8,1152]{2,1,0:T(8,128)} %get-tuple-element.88) | copy-start | bytes 110596
  452.9 20.1 %copy-start.2 = (f32[1,864,1]{2,1,0:T(8,128)S(1)}, f32[1,864,1]{2,1,0:T(8,128)}, u32[]{:S(2)}) copy-start(f32[1,864,1]{2,1,0:T(8,128)} %get-tuple-element.90) | copy-start | bytes 10372
  452.9 20.1 %copy-start.3 = (f32[1,864,1]{2,1,0:T(8,128)S(1)}, f32[1,864,1]{2,1,0:T(8,128)}, u32[]{:S(2)}) copy-start(f32[1,864,1]{2,1,0:T(8,128)} %get-tuple-element.91) | copy-start | bytes 10372
  582.0 23.0 %copy-start.7 = (bf16[3,1152]{1,0:T(4,128)(2,1)S(1)}, bf16[3,1152]{1,0:T(4,128)(2,1)}, u32[]{:S(2)}) copy-start(bf16[3,1152]{1,0:T(4,128)(2,1)} %get-tuple-element.118) | copy-start | bytes 20740
  622.3 5.2 copy-start.4
  622.3 5.8 copy-start
  628.0 2.2 copy-start.1
